TPU v7x, 32 devices: a whole 2x2x4 slice. The times are simulated.
32 devices in a mesh: rows: 2 (over y), seq: 16 (over z, x, core).
Axes of the slice: x: 2, y: 2, z: 4, core: 2. Of those that a mesh axis runs over, the one named last changes fastest.
Arguments:
- hidden_in: bfloat16 [2, 2048, 768], P('rows', 'seq'), may hold values from -6 to 6
- segments: int32 [2, 2048], P('rows', 'seq'), may hold values from -1 to 6, as said below
- cotangent: bfloat16 [2, 2048, 768], P('rows', 'seq'), may hold values from -6 to 6
- w_query: bfloat16 [768, 768], replicated, may hold values from -0.0546875 to 0.0546875
- w_key: bfloat16 [768, 768], replicated, may hold values from -0.21875 to 0.21875
- w_value: bfloat16 [768, 768], replicated, may hold values from -0.21875 to 0.21875
- w_out: bfloat16 [768, 768], replicated, may hold values from -0.875 to 0.875
- w_gate: bfloat16 [768, 2048], replicated, may hold values from -0.21875 to 0.21875
- w_up: bfloat16 [768, 2048], replicated, may hold values from -0.21875 to 0.21875
- w_down: bfloat16 [2048, 768], replicated, may hold values from -0.125 to 0.125
- bias_table: bfloat16 [32, 12], replicated, may hold values from -4 to 4
- gain_attn: bfloat16 [768], replicated, may hold values from 0.5 to 1.5
- gain_ffn: bfloat16 [768], replicated, may hold values from 0.5 to 1.5
Outputs:
- output: bfloat16 [2, 2048, 768], P('rows', 'seq')
- grad_input: bfloat16 [2, 2048, 768], P('rows', 'seq')
- grad_w_query: float32 [768, 768], P(('rows', 'seq'))
- grad_w_key: float32 [768, 768], P(('rows', 'seq'))
- grad_w_value: float32 [768, 768], P(('rows', 'seq'))
- grad_w_out: float32 [768, 768], P(('rows', 'seq'))
- grad_w_gate: float32 [768, 2048], P(('rows', 'seq'))
- grad_w_up: float32 [768, 2048], P(('rows', 'seq'))
- grad_w_down: float32 [2048, 768], P(('rows', 'seq'))
- grad_table: float32 [32, 12], replicated
- grad_gain_attn: float32 [768], replicated
- grad_gain_ffn: float32 [768], replicated
Inputs may be any that keep to these rules, and one draw needn't show every extreme that they name: `segments`: each row is a pack of documents laid end to end: documents 0, 1 and 2 within the row's first 128 tokens (some may be empty), document 3 starting there and ending within the row's last 128 tokens, documents 4, 5 and 6 after it (some may be empty), then 1 to 32 padding tokens (-1) at the row's end. Document numbers never fall along a row except to padding.
All inputs are finite; a program needn't handle non-finite values.
Results may differ from a plain program's by a relative error of at most 0.018.
Values may be sent and summed in bfloat16 or wider, within the bound.
A program may use at most 320 MiB of HBM per device.

v0:
```python
import math

import jax
import jax.numpy as jnp
from jax import lax
from jax.sharding import PartitionSpec as P

D = 768
H = 12
DH = 64
NB = 32


BORDERS = (12, 16, 23, 32, 46, 64, 91)
EPSILON = 1e-06
MASKED = -1e30
BLOCK_LIMIT = 2048


def bucket_of(offset):
    distance = jnp.abs(offset)
    far_bucket = 8 + sum(((distance >= border).astype(jnp.int32) for border in BORDERS))
    return jnp.where(offset > 0, 16, 0) + jnp.where(distance < 8, distance, far_bucket)


def rms_scale(values, gain_vec):
    return (
        values * lax.rsqrt(jnp.mean(values * values, axis=-1, keepdims=True) + EPSILON) * gain_vec
    )


def gelu_tanh(values):
    return jax.nn.gelu(values, approximate=True)


def block_rows(row_count, row_unit):
    if row_count <= BLOCK_LIMIT:
        return row_count
    grain_rows = math.gcd(row_count, row_unit)
    pieces = row_count // grain_rows
    chosen = max(
        (
            factor
            for factor in range(1, pieces + 1)
            if pieces % factor == 0 and factor * grain_rows <= max(BLOCK_LIMIT, grain_rows)
        )
    )
    return chosen * grain_rows


def over_blocks(update, carried, arrays, block_len):
    step_count = arrays[0].shape[0] // block_len
    if step_count == 1:
        return update(carried, arrays, 0)

    def one_step(block_index, current):
        offset_rows = block_index * block_len
        sliced = tuple(
            (lax.dynamic_slice_in_dim(member, offset_rows, block_len, 0) for member in arrays)
        )
        return update(current, sliced, offset_rows)

    return lax.fori_loop(0, step_count, one_step, carried)


def offset_hot(base_offset, direction, row_count, col_count):
    span_len = row_count + col_count - 1
    offsets = base_offset + direction * (jnp.arange(span_len, dtype=jnp.int32) - (row_count - 1))
    return bucket_of(offsets)[:, None] == jnp.arange(NB, dtype=jnp.int32)[None, :]


def toeplitz_bias(one_hot, bias_table, row_count, col_count):
    per_offset = jnp.dot(
        jnp.transpose(bias_table),
        jnp.transpose(one_hot).astype(jnp.bfloat16),
        preferred_element_type=jnp.float32,
    )
    span_len = per_offset.shape[1]
    tiled_vec = jnp.tile(per_offset, (1, row_count + 1))
    window = tiled_vec[:, row_count - 1 : row_count - 1 + row_count * (span_len - 1)]
    return window.reshape(per_offset.shape[0], row_count, span_len - 1)[:, :, :col_count]


def bias_grad(grad_score, one_hot, row_count, col_count):
    head_count = grad_score.shape[0]
    span_len = row_count + col_count - 1
    padded = jnp.pad(grad_score, ((0, 0), (0, 0), (0, span_len - 1 - col_count)))
    flattened = padded.reshape(head_count, row_count * (span_len - 1))
    flattened = jnp.pad(flattened, ((0, 0), (row_count - 1, span_len + 1)))
    per_offset = jnp.sum(flattened.reshape(head_count, row_count + 1, span_len), axis=1)
    return jnp.transpose(
        jnp.dot(per_offset, one_hot.astype(jnp.float32), precision=lax.Precision.HIGHEST)
    )


def per_device(
    hidden_in,
    segments,
    cotangent,
    w_query,
    w_key,
    w_value,
    w_out,
    w_gate,
    w_up,
    w_down,
    bias_table,
    gain_attn,
    gain_ffn,
):
    row_in = hidden_in[0].astype(jnp.float32)
    seg_own = segments[0]
    tok_count = row_in.shape[0]
    own_first = lax.axis_index("seq") * tok_count
    seg_all = lax.all_gather(seg_own, "seq", axis=0, tiled=True)
    is_valid = (seg_own >= 0)[:, None]
    gain_first = gain_attn.astype(jnp.float32)
    gain_second = gain_ffn.astype(jnp.float32)
    norm_first, norm_back_first = jax.vjp(rms_scale, row_in, gain_first)
    normed_attn = norm_first.astype(jnp.bfloat16)
    queries = jnp.dot(normed_attn, w_query, preferred_element_type=jnp.float32).astype(jnp.bfloat16)
    keys_own = jnp.dot(normed_attn, w_key, preferred_element_type=jnp.float32).astype(jnp.bfloat16)
    values_own = jnp.dot(normed_attn, w_value, preferred_element_type=jnp.float32).astype(
        jnp.bfloat16
    )
    query_heads = queries.reshape(tok_count, H, DH)
    key_heads = keys_own.reshape(tok_count, H, DH)
    value_heads = values_own.reshape(tok_count, H, DH)

    def block_scores(row_heads, col_heads, seg_rows, seg_cols, base_offset, direction):
        row_count, col_count = (row_heads.shape[0], col_heads.shape[0])
        one_hot = offset_hot(base_offset, direction, row_count, col_count)
        product = jnp.einsum(
            "rhd,chd->hrc", row_heads, col_heads, preferred_element_type=jnp.float32
        )
        allowed = (seg_rows[:, None] == seg_cols[None, :])[None]
        scores = jnp.where(
            allowed, product + toeplitz_bias(one_hot, bias_table, row_count, col_count), MASKED
        )
        return (scores, allowed, one_hot)

    start_state = (
        jnp.full((H, tok_count), MASKED, jnp.float32),
        jnp.zeros((H, tok_count), jnp.float32),
        jnp.zeros((tok_count, H, DH), jnp.float32),
    )
    incoming = (
        lax.all_gather(keys_own, "seq", axis=0, tiled=True),
        lax.all_gather(values_own, "seq", axis=0, tiled=True),
    )
    begin_at = jnp.int32(0)

    def update(current, sliced, offset_rows):
        keys_part, values_part = sliced
        count_part = keys_part.shape[0]
        first_key = begin_at + offset_rows
        seg_part = lax.dynamic_slice_in_dim(seg_all, first_key, count_part, 0)
        scores, allowed, one_hot = block_scores(
            query_heads,
            keys_part.reshape(count_part, H, DH),
            seg_own,
            seg_part,
            first_key - own_first,
            1,
        )
        running, totals, summed = current
        newest = jnp.maximum(running, jnp.max(scores, axis=-1))
        rescale = jnp.exp(running - newest)
        weights = jnp.where(allowed, jnp.exp(scores - newest[:, :, None]), 0.0)
        totals = totals * rescale + jnp.sum(weights, axis=-1)
        summed = summed * jnp.transpose(rescale)[:, :, None] + jnp.einsum(
            "hqk,khd->qhd",
            weights.astype(jnp.bfloat16),
            values_part.reshape(count_part, H, DH),
            preferred_element_type=jnp.float32,
        )
        return (newest, totals, summed)

    running, totals, summed = over_blocks(
        update, start_state, incoming, block_rows(incoming[0].shape[0], tok_count)
    )
    context = summed / jnp.transpose(totals)[:, :, None]
    log_total = running + jnp.log(totals)
    context_low = context.reshape(tok_count, D).astype(jnp.bfloat16)
    middle = row_in + jnp.dot(context_low, w_out, preferred_element_type=jnp.float32)
    norm_second, norm_back_second = jax.vjp(rms_scale, middle, gain_second)
    normed_ffn = norm_second.astype(jnp.bfloat16)
    gate_pre = jnp.dot(normed_ffn, w_gate, preferred_element_type=jnp.float32)
    upward = jnp.dot(normed_ffn, w_up, preferred_element_type=jnp.float32)
    gelu_out, gelu_back = jax.vjp(gelu_tanh, gate_pre)
    hidden_act = (gelu_out * upward).astype(jnp.bfloat16)
    result = middle + jnp.dot(hidden_act, w_down, preferred_element_type=jnp.float32)
    output = jnp.where(is_valid, result, 0.0).astype(jnp.bfloat16)[None]
    grad_result = jnp.where(is_valid, cotangent[0].astype(jnp.float32), 0.0)
    grad_branch = grad_result.astype(jnp.bfloat16)
    grad_w_down = jnp.einsum(
        "tf,td->fd", hidden_act, grad_branch, preferred_element_type=jnp.float32
    )
    grad_hidden = jnp.einsum("td,fd->tf", grad_branch, w_down, preferred_element_type=jnp.float32)
    grad_gate = gelu_back(grad_hidden * upward)[0].astype(jnp.bfloat16)
    grad_upward = (grad_hidden * gelu_out).astype(jnp.bfloat16)
    grad_w_gate = jnp.einsum("td,tf->df", normed_ffn, grad_gate, preferred_element_type=jnp.float32)
    grad_w_up = jnp.einsum("td,tf->df", normed_ffn, grad_upward, preferred_element_type=jnp.float32)
    grad_normed_ffn = jnp.einsum(
        "tf,df->td", grad_gate, w_gate, preferred_element_type=jnp.float32
    ) + jnp.einsum("tf,df->td", grad_upward, w_up, preferred_element_type=jnp.float32)
    grad_mid_part, grad_gain_ffn = norm_back_second(grad_normed_ffn)
    grad_middle = grad_result + grad_mid_part
    grad_attn = grad_middle.astype(jnp.bfloat16)
    grad_w_out = jnp.einsum("td,te->de", context_low, grad_attn, preferred_element_type=jnp.float32)
    grad_context = jnp.einsum(
        "te,de->td", grad_attn, w_out, preferred_element_type=jnp.float32
    ).astype(jnp.bfloat16)
    grad_heads = grad_context.reshape(tok_count, H, DH)
    delta_own = jnp.sum(grad_heads.astype(jnp.float32) * context, axis=-1)
    delta_rows = jnp.transpose(delta_own)
    lse_all, delta_all = (
        lax.all_gather(jnp.transpose(log_total), "seq", axis=0, tiled=True),
        lax.all_gather(delta_own, "seq", axis=0, tiled=True),
    )

    def query_update(current, keys_part, values_part, first_key):
        count_part = keys_part.shape[0]
        key_part_heads = keys_part.reshape(count_part, H, DH)
        seg_part = lax.dynamic_slice_in_dim(seg_all, first_key, count_part, 0)
        scores, allowed, one_hot = block_scores(
            query_heads, key_part_heads, seg_own, seg_part, first_key - own_first, 1
        )
        attn_prob = jnp.where(allowed, jnp.exp(scores - log_total[:, :, None]), 0.0)
        grad_prob = jnp.einsum(
            "qhd,khd->hqk",
            grad_heads,
            values_part.reshape(count_part, H, DH),
            preferred_element_type=jnp.float32,
        )
        grad_score = attn_prob * (grad_prob - delta_rows[:, :, None])
        grad_q, grad_tab = current
        grad_q = grad_q + jnp.einsum(
            "hqk,khd->qhd",
            grad_score.astype(jnp.bfloat16),
            key_part_heads,
            preferred_element_type=jnp.float32,
        )
        grad_tab = grad_tab + bias_grad(grad_score, one_hot, tok_count, count_part)
        return (grad_q, grad_tab)

    def key_update(current, queries_part, grad_ctx_part, first_query):
        count_part = queries_part.shape[0]
        query_part_heads = queries_part.reshape(count_part, H, DH)
        grad_part_heads = grad_ctx_part.reshape(count_part, H, DH)
        seg_part = lax.dynamic_slice_in_dim(seg_all, first_query, count_part, 0)
        lse_part = jnp.transpose(lax.dynamic_slice_in_dim(lse_all, first_query, count_part, 0))
        delta_part = jnp.transpose(lax.dynamic_slice_in_dim(delta_all, first_query, count_part, 0))
        scores, allowed, one_hot = block_scores(
            key_heads, query_part_heads, seg_own, seg_part, own_first - first_query, -1
        )
        attn_prob = jnp.where(allowed, jnp.exp(scores - lse_part[:, None, :]), 0.0)
        grad_prob = jnp.einsum(
            "khd,qhd->hkq", value_heads, grad_part_heads, preferred_element_type=jnp.float32
        )
        grad_score = attn_prob * (grad_prob - delta_part[:, None, :])
        grad_k, grad_v = current
        grad_k = grad_k + jnp.einsum(
            "hkq,qhd->khd",
            grad_score.astype(jnp.bfloat16),
            query_part_heads,
            preferred_element_type=jnp.float32,
        )
        grad_v = grad_v + jnp.einsum(
            "hkq,qhd->khd",
            attn_prob.astype(jnp.bfloat16),
            grad_part_heads,
            preferred_element_type=jnp.float32,
        )
        return (grad_k, grad_v)

    zero_heads = jnp.zeros((tok_count, H, DH), jnp.float32)
    zero_table = jnp.zeros((NB, H), jnp.float32)
    incoming = (
        lax.all_gather(keys_own, "seq", axis=0, tiled=True),
        lax.all_gather(values_own, "seq", axis=0, tiled=True),
    )
    keys_begin_at = jnp.int32(0)

    def update(current, sliced, offset_rows):
        return query_update(current, sliced[0], sliced[1], keys_begin_at + offset_rows)

    grad_q, grad_tab = over_blocks(
        update, (zero_heads, zero_table), incoming, block_rows(incoming[0].shape[0], tok_count)
    )
    incoming = (
        lax.all_gather(queries, "seq", axis=0, tiled=True),
        lax.all_gather(grad_context, "seq", axis=0, tiled=True),
    )
    queries_begin_at = jnp.int32(0)

    def update(current, sliced, offset_rows):
        return key_update(current, sliced[0], sliced[1], queries_begin_at + offset_rows)

    grad_k, grad_v = over_blocks(
        update, (zero_heads, zero_heads), incoming, block_rows(incoming[0].shape[0], tok_count)
    )
    grad_q_low = grad_q.reshape(tok_count, D).astype(jnp.bfloat16)
    grad_k_low = grad_k.reshape(tok_count, D).astype(jnp.bfloat16)
    grad_v_low = grad_v.reshape(tok_count, D).astype(jnp.bfloat16)
    grad_w_query = jnp.einsum(
        "td,te->de", normed_attn, grad_q_low, preferred_element_type=jnp.float32
    )
    grad_w_key = jnp.einsum(
        "td,te->de", normed_attn, grad_k_low, preferred_element_type=jnp.float32
    )
    grad_w_value = jnp.einsum(
        "td,te->de", normed_attn, grad_v_low, preferred_element_type=jnp.float32
    )
    grad_normed_attn = jnp.einsum(
        "te,de->td", grad_q_low, w_query, preferred_element_type=jnp.float32
    )
    grad_normed_attn = grad_normed_attn + jnp.einsum(
        "te,de->td", grad_k_low, w_key, preferred_element_type=jnp.float32
    )
    grad_normed_attn = grad_normed_attn + jnp.einsum(
        "te,de->td", grad_v_low, w_value, preferred_element_type=jnp.float32
    )
    grad_in_part, grad_gain_attn = norm_back_first(grad_normed_attn)
    grad_input = (grad_middle + grad_in_part).astype(jnp.bfloat16)[None]
    summed_weights = tuple(
        (
            lax.psum_scatter(grad_w_query, ("rows", "seq"), scatter_dimension=0, tiled=True),
            lax.psum_scatter(grad_w_key, ("rows", "seq"), scatter_dimension=0, tiled=True),
            lax.psum_scatter(grad_w_value, ("rows", "seq"), scatter_dimension=0, tiled=True),
            lax.psum_scatter(grad_w_out, ("rows", "seq"), scatter_dimension=0, tiled=True),
            lax.psum_scatter(grad_w_gate, ("rows", "seq"), scatter_dimension=0, tiled=True),
            lax.psum_scatter(grad_w_up, ("rows", "seq"), scatter_dimension=0, tiled=True),
            lax.psum_scatter(grad_w_down, ("rows", "seq"), scatter_dimension=0, tiled=True),
        )
    )
    table_sum, gain_attn_sum, gain_ffn_sum = lax.psum(
        (grad_tab, grad_gain_attn, grad_gain_ffn), ("rows", "seq")
    )
    return (
        output,
        grad_input,
        summed_weights[0],
        summed_weights[1],
        summed_weights[2],
        summed_weights[3],
        summed_weights[4],
        summed_weights[5],
        summed_weights[6],
        table_sum,
        gain_attn_sum,
        gain_ffn_sum,
    )


def solution(mesh):
    in_specs = (
        P("rows", "seq", None),
        P("rows", "seq"),
        P("rows", "seq", None),
        P(),
        P(),
        P(),
        P(),
        P(),
        P(),
        P(),
        P(),
        P(),
        P(),
    )
    out_specs = (
        P("rows", "seq", None),
        P("rows", "seq", None),
        P(("rows", "seq"), None),
        P(("rows", "seq"), None),
        P(("rows", "seq"), None),
        P(("rows", "seq"), None),
        P(("rows", "seq"), None),
        P(("rows", "seq"), None),
        P(("rows", "seq"), None),
        P(),
        P(),
        P(),
    )
    return jax.shard_map(
        per_device, mesh=mesh, in_specs=in_specs, out_specs=out_specs, check_vma=False
    )
```

profile of v0, /device:TPU:0, one launch (start us, length us, event | category | flops | bytes accessed | tf_op | source)
XLA Modules:
  0.0 984.8 jit_solution(5866930044203306004)
XLA Ops:
  17.7 23.0 %all-gather = s32[1,2048]{1,0:T(1,128)S(1)} all-gather(s32[1,128]{1,0:T(1,128)S(1)} %copy-done.39), channel_id=2, replica_groups=mesh['rows'=2,'seq'=16] {'seq'}, dimensions={1}, use_global_device_ids=true | all-gather | bytes 8704 | tf_op jit(solution)/shard_map/all_gather | solution.py:115
  50.2 17.9 %tile.9 = f32[12,280575]{1,0:T(8,128)} reshape(f32[12,129,2175]{2,1,0:T(8,128)} %tile.8) | data formatting | bytes 26935200 | tf_op jit(solution)/shard_map/tile | solution.py:79
  68.1 13.7 %slice.18 = f32[12,278272]{1,0:T(8,128)} slice(f32[12,280575]{1,0:T(8,128)} %tile.9), slice={[0:12], [127:278399]} | slice | bytes 26714112 | tf_op jit(solution)/shard_map/slice | solution.py:80
  81.8 26.9 %reshape.282 = f32[12,128,2174]{2,1,0:T(8,128)} reshape(f32[12,278272]{1,0:T(8,128)} %slice.18) | data formatting | bytes 26714112 | tf_op jit(solution)/shard_map/reshape | solution.py:81
  115.0 12.5 %fusion.112 = (f32[12,128]{1,0:T(8,128)S(1)}, f32[12,128,2048]{2,1,0:T(8,128)}) fusion(f32[12,128,2174]{2,1,0:T(8,128)} %reshape.282, bf16[128,12,64]{0,2,1:T(8,128)(2,1)S(1)} %bitcast.164, bf16[2048,12,64]{0,2,1:T(8,128)(2,1)} %bitcast.152, pred[128,2048]{1,0:T(8,128)(4,1)} %broadcast_compare_fusion), kind=kOutput, calls=%fused_computation.140 | convolution fusion | flops 412088832 | bytes 28776448 | tf_op jit(solution)/shard_map/rhd,chd->hrc/dot_general | solution.py:133
  132.3 7.9 fusion.5
  161.1 9.9 %subtract_multiply_fusion = f32[12,128,2048]{2,1,0:T(8,128)S(1)} fusion(f32[12,128,2048]{2,1,0:T(8,128)} %get-tuple-element.26, f32[12,128]{1,0:T(8,128)S(1)} %bitcast.171, f32[12,128]{1,0:T(8,128)S(1)} %log_add_fusion, pred[128,2048]{1,0:T(8,128)(4,1)} %broadcast_compare_fusion, bf16[128,12,64]{0,2,1:T(8,128)(2,1)} %bitcast.163, ...), kind=kOutput, calls=%fused_computation.8 | convolution fusion | flops 415236096 | bytes 28782592 | tf_op jit(solution)/shard_map/qhd,khd->hqk/dot_general | solution.py:230
  203.9 17.8 %tile.11 = f32[12,280575]{1,0:T(8,128)} reshape(f32[12,129,2175]{2,1,0:T(8,128)} %tile.10) | data formatting | bytes 26935200 | tf_op jit(solution)/shard_map/tile | solution.py:79
  221.7 13.8 %slice.20 = f32[12,278272]{1,0:T(8,128)} slice(f32[12,280575]{1,0:T(8,128)} %tile.11), slice={[0:12], [127:278399]} | slice | bytes 26714112 | tf_op jit(solution)/shard_map/slice | solution.py:80
  235.5 27.1 %reshape.287 = f32[12,128,2174]{2,1,0:T(8,128)} reshape(f32[12,278272]{1,0:T(8,128)} %slice.20) | data formatting | bytes 26714112 | tf_op jit(solution)/shard_map/reshape | solution.py:81
  267.5 17.8 %all_gather.27 = f32[2048,12]{0,1:T(8,128)S(1)} all-gather(f32[128,12]{0,1:T(8,128)S(1)} %copy-done.32), channel_id=1, replica_groups=mesh['rows'=2,'seq'=16] {'seq'}, dimensions={0}, use_global_device_ids=true | all-gather | bytes 104448 | tf_op jit(solution)/shard_map/all_gather | solution.py:218
  285.3 14.3 %fusion.3 = f32[12,128,2048]{2,1,0:T(8,128)} fusion(f32[12,128,2174]{2,1,0:T(8,128)} %reshape.287, f32[12,2048]{1,0:T(8,128)S(1)} %bitcast.170, pred[128,2048]{1,0:T(8,128)(4,1)} %broadcast_compare_fusion, bf16[128,12,64]{0,2,1:T(8,128)(2,1)S(1)} %bitcast.165, bf16[2048,12,64]{0,2,1:T(8,128)(2,1)} %bitcast.148), kind=kOutput, calls=%fused_computation.4 | convolution fusion | flops 415236096 | bytes 28868608 | tf_op jit(solution)/shard_map/rhd,chd->hrc/dot_general | solution.py:133
  315.8 20.5 %all_gather.29 = f32[2048,12]{0,1:T(8,128)} all-gather(f32[128,12]{0,1:T(8,128)S(1)} %copy-done.28), channel_id=1, replica_groups=mesh['rows'=2,'seq'=16] {'seq'}, dimensions={0}, use_global_device_ids=true | all-gather | bytes 104448 | tf_op jit(solution)/shard_map/all_gather | solution.py:219
  336.3 10.7 %fusion.34 = bf16[12,64,128]{2,1,0:T(8,128)(2,1)S(1)} fusion(bf16[2048,12,64]{0,2,1:T(8,128)(2,1)} %bitcast.149, f32[12,128,2048]{2,1,0:T(8,128)} %fusion.3, f32[12,2048]{1,0:T(8,128)} %bitcast.169, bf16[128,12,64]{0,2,1:T(8,128)(2,1)} %bitcast.166, bf16[2048,12,64]{0,2,1:T(8,128)(2,1)} %bitcast.151), kind=kOutput, calls=%fused_computation.42 | convolution fusion | flops 814841856 | bytes 19365888 | tf_op jit(solution)/shard_map/hkq,qhd->khd/dot_general | solution.py:263
  349.1 10.7 %pad.8 = f32[12,128,2174]{2,1,0:T(8,128)} pad(f32[12,128,2048]{2,1,0:T(8,128)} %copy-done.1, f32[]{:T(128)} %constant.27.clone.1), padding=0_0x0_0x0_126 | pad | bytes 25939972 | tf_op jit(solution)/shard_map/jit(_pad)/pad | solution.py:87
  359.8 23.6 %reshape.290 = f32[12,278272]{1,0:T(8,128)} reshape(f32[12,128,2174]{2,1,0:T(8,128)} %pad.8) | data formatting | bytes 26714112 | tf_op jit(solution)/shard_map/reshape | solution.py:88
  383.4 13.6 %pad.9 = f32[12,280575]{1,0:T(8,128)} pad(f32[12,278272]{1,0:T(8,128)} %reshape.290, f32[]{:T(128)} %constant.27.clone.1), padding=0_0x127_2176 | pad | bytes 26824660 | tf_op jit(solution)/shard_map/jit(_pad)/pad | solution.py:89
  397.0 22.6 %reshape.291 = f32[12,129,2175]{2,1,0:T(8,128)} reshape(f32[12,280575]{1,0:T(8,128)} %pad.9) | data formatting | bytes 26935200 | tf_op jit(solution)/shard_map/reshape | solution.py:90
  435.2 37.2 %all-reduce.2 = (f32[32,12]{0,1:T(8,128)}, f32[768]{0:T(1024)}, f32[768]{0:T(1024)}) all-reduce(f32[32,12]{0,1:T(8,128)S(1)} %copy-done.35, f32[768]{0:T(1024)S(1)} %get-tuple-element.14, f32[768]{0:T(1024)S(1)} %copy-done.33), channel_id=1, replica_groups=mesh['rows'=2,'seq'=16] {'rows','seq'}, use_global_device_ids=true, to_apply=%region_15.16 | all-reduce | flops 1920 | bytes 15360 | tf_op jit(solution)/shard_map/psum | solution.py:337
  474.4 54.2 %reduce-scatter.20.cloned.1.call-done = f32[64,768]{1,0:T(8,128)} async-done(((f32[2048,768]{1,0:T(8,128)}), f32[64,768]{1,0:T(8,128)}) %reduce-scatter.20.cloned.1.call-update) | async-done | bytes 196624 | tf_op jit(solution)/shard_map/reduce_scatter | solution.py:334
  528.6 120.6 %reduce-scatter.18.cloned.1.call-done = f32[24,2048]{1,0:T(8,128)} async-done(((f32[768,2048]{1,0:T(8,128)}), f32[24,2048]{1,0:T(8,128)}) %reduce-scatter.18.cloned.1.call-update) | async-done | bytes 196624 | tf_op jit(solution)/shard_map/reduce_scatter | solution.py:333
  649.2 119.7 %reduce-scatter.16.cloned.1.call-done = f32[24,2048]{1,0:T(8,128)} async-done(((f32[768,2048]{1,0:T(8,128)}), f32[24,2048]{1,0:T(8,128)}) %reduce-scatter.16.cloned.1.call-update) | async-done | bytes 196624 | tf_op jit(solution)/shard_map/reduce_scatter | solution.py:332
  769.0 104.9 %reduce-scatter.12.cloned.1.call-done = f32[24,768]{1,0:T(8,128)} async-done(((f32[768,768]{1,0:T(8,128)}), f32[24,768]{1,0:T(8,128)}) %reduce-scatter.12.cloned.1.call-update) | async-done | bytes 73744 | tf_op jit(solution)/shard_map/reduce_scatter | solution.py:330
  873.8 103.9 %reduce-scatter.10.cloned.1.call-done = f32[24,768]{1,0:T(8,128)} async-done(((f32[768,768]{1,0:T(8,128)}), f32[24,768]{1,0:T(8,128)}) %reduce-scatter.10.cloned.1.call-update) | async-done | bytes 73744 | tf_op jit(solution)/shard_map/reduce_scatter | solution.py:329
  (170 shorter events, 124.9 us)
Async XLA Ops:
  7.2 142.2 %copy-start = (bf16[2048,768]{1,0:T(8,128)(2,1)S(1)}, bf16[2048,768]{1,0:T(8,128)(2,1)}, u32[]{:S(2)}) copy-start(bf16[2048,768]{1,0:T(8,128)(2,1)} %param.22) | copy-start | bytes 9437188
  7.2 7.6 copy-start.4
  7.2 9.9 %copy-start.39 = (s32[1,128]{1,0:T(1,128)S(1)}, s32[1,128]{1,0:T(1,128)}, u32[]{:S(2)}) copy-start(s32[1,128]{1,0:T(1,128)} %param.14) | copy-start | bytes 1540
  7.2 103.1 %all-gather.6.cloned.1.call-start = ((), (), s32[]{:S(2)}) async-start(), calls=%async_computation.7 | async-start | bytes 3342336 | tf_op jit(solution)/shard_map/all_gather | solution.py:148
  9.0 8.6 copy-start.30
  12.2 115.3 %all-gather.8.cloned.1.call-start = ((), (), s32[]{:S(2)}) async-start(), calls=%async_computation.8 | async-start | bytes 3342336 | tf_op jit(solution)/shard_map/all_gather | solution.py:149
  14.7 248.0 %all-gather.10.cloned.1.call-start = ((), (), s32[]{:S(2)}) async-start(), calls=%async_computation.9 | async-start | bytes 3342336 | tf_op jit(solution)/shard_map/all_gather | solution.py:292
  17.1 282.6 %all-gather.12.cloned.1.call-start = ((), (), s32[]{:S(2)}) async-start(), calls=%async_computation.10 | async-start | bytes 3342336 | tf_op jit(solution)/shard_map/all_gather | solution.py:293
  132.3 8.8 copy-start.2
  132.3 8.8 copy-start.8
  147.1 8.0 copy-start.7
  157.3 317.1 %reduce-scatter.8.cloned.1.call-start = ((), (), s32[]{:S(2)}) async-start(), calls=%async_computation.11 | async-start | bytes 2433024 | tf_op jit(solution)/shard_map/reduce_scatter | solution.py:328
  161.1 10.0 %copy-start.3 = (bf16[2048,768]{0,1:T(8,128)(2,1)S(1)}, bf16[2048,768]{0,1:T(8,128)(2,1)}, u32[]{:S(2)}) copy-start(bf16[2048,768]{0,1:T(8,128)(2,1)} %copy.36) | copy-start | bytes 9437188
  178.4 296.1 %reduce-scatter.14.cloned.1.call-start = ((), (), s32[]{:S(2)}) async-start(), calls=%async_computation.14 | async-start | bytes 2433024 | tf_op jit(solution)/shard_map/reduce_scatter | solution.py:331
  181.4 347.2 %reduce-scatter.20.cloned.1.call-start = ((), (), s32[]{:S(2)}) async-start(), calls=%async_computation.17 | async-start | bytes 6488064 | tf_op jit(solution)/shard_map/reduce_scatter | solution.py:334
  186.2 463.0 %reduce-scatter.18.cloned.1.call-start = ((), (), s32[]{:S(2)}) async-start(), calls=%async_computation.16 | async-start | bytes 6488064 | tf_op jit(solution)/shard_map/reduce_scatter | solution.py:333
  191.0 578.0 %reduce-scatter.16.cloned.1.call-start = ((), (), s32[]{:S(2)}) async-start(), calls=%async_computation.15 | async-start | bytes 6488064 | tf_op jit(solution)/shard_map/reduce_scatter | solution.py:332
  195.7 678.1 %reduce-scatter.12.cloned.1.call-start = ((), (), s32[]{:S(2)}) async-start(), calls=%async_computation.13 | async-start | bytes 2433024 | tf_op jit(solution)/shard_map/reduce_scatter | solution.py:330
  262.7 22.7 %copy-start.24 = (bf16[128,768]{0,1:T(8,128)(2,1)S(1)}, bf16[128,768]{0,1:T(8,128)(2,1)}, u32[]{:S(2)}) copy-start(bf16[128,768]{0,1:T(8,128)(2,1)} %copy.40) | copy-start | bytes 589828
  315.0 662.8 %reduce-scatter.10.cloned.1.call-start = ((), (), s32[]{:S(2)}) async-start(), calls=%async_computation.12 | async-start | bytes 2433024 | tf_op jit(solution)/shard_map/reduce_scatter | solution.py:329
  347.0 12.8 %copy-start.20 = (bf16[12,64,128]{2,1,0:T(8,128)(2,1)}, bf16[12,64,128]{2,1,0:T(8,128)(2,1)S(1)}, u32[]{:S(2)}) copy-start(bf16[12,64,128]{2,1,0:T(8,128)(2,1)S(1)} %fusion.34) | copy-start | bytes 589828
  419.6 9.4 copy-start.17
  419.6 11.2 %copy-start.38 = (pred[128]{0:T(512)(128)(4,1)S(1)}, pred[128]{0:T(512)(128)(4,1)}, u32[]{:S(2)}) copy-start(pred[128]{0:T(512)(128)(4,1)} %broadcast_compare_fusion.1) | copy-start | bytes 388
  433.4 39.1 %copy-start.41 = (f32[128]{0:T(128)S(1)}, f32[128]{0:T(128)}, u32[]{:S(2)}) copy-start(f32[128]{0:T(128)} %copy-done.40) | copy-start | bytes 1540
  (30 other events, 80.3 us)
Sparse Core Ops, SparseCore 0:
  12.3 47.8 all-gather.5
  62.5 43.9 all-gather.7
  109.4 43.9 all-gather.9
  157.4 42.7 all-gather.11
  205.9 97.8 reduce-scatter.7
  310.3 98.0 reduce-scatter.13
  414.6 113.9 reduce-scatter.19
  535.7 113.4 reduce-scatter.17
  655.5 113.4 reduce-scatter.15
  775.5 98.2 reduce-scatter.11
  879.7 98.0 reduce-scatter.9
where the time goes:
time: 992 us; the launch traced here: 985 us
  waiting for transfers between devices  504 us (51%)
  local copies, waits for them, and re-layouts  231 us (23%)
  matrix products  112 us (11%)
  blocking collectives  98.5 us (10%)
  other arithmetic  24.4 us (2%)
  between operations  14.9 us (2%)
    reduce_scatter x1, waiting for transfers between devices, per_device(): lax.psum_scatter(grad_w_up, ('rows', 'seq'), scatter_dimension=0, tiled=T...  121 us
    reduce_scatter x1, waiting for transfers between devices, per_device(): lax.psum_scatter(grad_w_gate, ('rows', 'seq'), scatter_dimension=0, tiled...  120 us
    reduce_scatter x1, waiting for transfers between devices, per_device(): lax.psum_scatter(grad_w_value, ('rows', 'seq'), scatter_dimension=0, tile...  105 us
    reduce_scatter x1, waiting for transfers between devices, per_device(): lax.psum_scatter(grad_w_key, ('rows', 'seq'), scatter_dimension=0, tiled=...  104 us
    reduce_scatter x1, waiting for transfers between devices, per_device(): lax.psum_scatter(grad_w_down, ('rows', 'seq'), scatter_dimension=0, tiled...  54.2 us
    reshape x2, local copies, waits for them, and re-layouts, toeplitz_bias(): window.reshape(per_offset.shape[0], row_count, span_len - 1)  54.1 us
    another operation x4, local copies, waits for them, and re-layouts, toeplitz_bias(): tiled_vec = jnp.tile(per_offset, (1, row_count + 1))  47.6 us
    psum x1, blocking collectives, per_device(): lax.psum((grad_tab, grad_gain_attn, grad_gain_ffn), ('rows', 'seq'))  37.2 us
  transfers between devices with their start and end apart: 11, of which 5 were waited for; matrix products, arithmetic and copies ran while one was open for 36% of the time, Pallas kernels for 0%

commit v1 on v0

--- a/solution.py
+++ b/solution.py
@@ -3,18 +3,282 @@
 import jax
 import jax.numpy as jnp
 from jax import lax
+from jax.experimental import pallas as pl
+from jax.experimental.pallas import tpu as pltpu
 from jax.sharding import PartitionSpec as P
 
 D = 768
 H = 12
 DH = 64
 NB = 32
+FF = 2048
 
 
 BORDERS = (12, 16, 23, 32, 46, 64, 91)
 EPSILON = 1e-06
 MASKED = -1e30
 BLOCK_LIMIT = 2048
+
+
+MESH = pl.DeviceIdType.MESH
+GATE_UNITS = 4
+GATE_COLS = FF // GATE_UNITS
+
+
+def place():
+    row = lax.axis_index("rows")
+    spot = lax.axis_index("seq")
+    return row, spot // 4, (spot // 2) % 2, spot % 2
+
+
+def device(row, zpos, xpos, core):
+    return (row, 4 * zpos + 2 * xpos + core)
+
+
+def flip(bit):
+    return 1 - bit
+
+
+def near_z(zpos):
+    return zpos + 1 - 2 * (zpos % 2)
+
+
+def far_z(zpos):
+    return (zpos + 2) % 4
+
+
+def greet(peers):
+    barrier = pltpu.get_barrier_semaphore()
+    for peer in peers:
+        pl.semaphore_signal(barrier, inc=1, device_id=peer, device_id_type=MESH)
+    pl.semaphore_wait(barrier, len(peers))
+
+
+def remote(src, dst, send_sem, recv_sem, peer):
+    return pltpu.make_async_remote_copy(
+        src_ref=src, dst_ref=dst, send_sem=send_sem, recv_sem=recv_sem, device_id=peer, device_id_type=MESH
+    )
+
+
+def weight_kernel(
+    lhs_down, lhs_gate, lhs_attn, rhs_down, rhs_gate, rhs_attn, small,
+    out_query, out_key, out_value, out_out, out_gate, out_up, out_down, out_small,
+    all_lhs_down, all_lhs_gate, all_lhs_attn, all_rhs_down, all_rhs_gate, all_rhs_attn,
+    total_down, total_gate, total_attn,
+    xs_down, xs_gate, xs_attn, xr_down, xr_gate, xr_attn,
+    ns_down, ns_gate, ns_attn, nr_down, nr_gate, nr_attn,
+    fs_down, fs_gate, fs_attn, fr_down, fr_gate, fr_attn,
+    small_send, small_recv,
+    swap_send_sem, swap_recv_sem, x_send_sem, x_recv_sem, near_send_sem, near_recv_sem, far_send_sem, far_recv_sem,
+    small_send_sem, small_recv_sem, local_sem,
+):
+    row, zpos, xpos, core = place()
+    mate = device(row, zpos, xpos, flip(core))
+    across = device(flip(row), zpos, xpos, core)
+    slant = device(flip(row), zpos, xpos, flip(core))
+    beside = device(row, zpos, flip(xpos), core)
+    near = device(row, near_z(zpos), xpos, core)
+    far = device(row, far_z(zpos), xpos, core)
+    greet((mate, across, slant, beside, near, far))
+    mine = 2 * row + core
+    mate_part = 2 * row + flip(core)
+    across_part = 2 * flip(row) + core
+    slant_part = 2 * flip(row) + flip(core)
+
+    pending = []
+    swaps = []
+    groups = ((lhs_down, rhs_down, all_lhs_down, all_rhs_down), (lhs_gate, rhs_gate, all_lhs_gate, all_rhs_gate),
+              (lhs_attn, rhs_attn, all_lhs_attn, all_rhs_attn))
+
+    def lanes(part):
+        return pl.ds(pl.multiple_of(part * 128, 128), 128)
+
+    for index, (lhs, rhs, all_lhs, all_rhs) in enumerate(groups):
+        copies = []
+        for slot, (peer, part) in enumerate(((across, across_part), (slant, slant_part), (mate, mate_part))):
+            copies.append(remote(lhs.at[part], all_lhs.at[:, lanes(mine)], swap_send_sem.at[index, slot],
+                                 swap_recv_sem.at[index, slot], peer))
+        for slot, peer in ((3, across), (4, mate)):
+            copies.append(remote(rhs, all_rhs.at[lanes(mine)], swap_send_sem.at[index, slot],
+                                 swap_recv_sem.at[index, slot], peer))
+        own_lhs = pltpu.make_async_copy(lhs.at[mine], all_lhs.at[:, lanes(mine)], local_sem.at[index, 0])
+        own_rhs = pltpu.make_async_copy(rhs, all_rhs.at[lanes(mine)], local_sem.at[index, 1])
+        for copy in copies:
+            copy.start()
+        own_lhs.start()
+        own_rhs.start()
+        onward = remote(all_rhs.at[lanes(across_part)], all_rhs.at[lanes(across_part)],
+                        swap_send_sem.at[index, 5], swap_recv_sem.at[index, 5], mate)
+        swaps.append((copies, (own_lhs, own_rhs), onward))
+
+    def finish_swap(index):
+        copies, locals_, onward = swaps[index]
+        copies[3].wait_recv()
+        onward.start()
+        for slot in (0, 1, 2, 4):
+            copies[slot].wait_recv()
+        for copy in locals_:
+            copy.wait()
+        onward.wait_recv()
+        pending.extend(copies)
+        pending.append(onward)
+
+    small_send[0] = small[...]
+    small_peers = (mate, across, beside, near, far)
+    small_step = 0
+
+    def advance_small(step):
+        copy = remote(small_send.at[step], small_recv.at[step], small_send_sem.at[step], small_recv_sem.at[step],
+                      small_peers[step])
+        copy.start()
+        copy.wait_recv()
+        summed = small_send[step] + small_recv[step]
+        if step < 4:
+            small_send[step + 1] = summed
+        else:
+            out_small[...] = summed
+        pending.append(copy)
+
+    def half_rows(x_half, height):
+        return pl.ds(pl.multiple_of(x_half * height, height), height)
+
+    def stacked(parts, height):
+        return [jnp.concatenate([part[height * block : height * (block + 1)] for part in parts], axis=0)
+                for block in range(4)]
+
+    def products(kind, unit, x_half):
+        if kind == "down":
+            lhs, rhs = all_lhs_down[half_rows(x_half, 256), :], (all_rhs_down[...],)
+            height = 64
+        elif kind == "gate":
+            lhs = all_lhs_gate[half_rows(x_half, 96), :]
+            first = unit * GATE_COLS
+            rhs = (all_rhs_gate[:, first : first + GATE_COLS], all_rhs_gate[:, FF + first : FF + first + GATE_COLS])
+            height = 24
+        else:
+            rhs = (all_rhs_attn[:, 2 * unit * D : (2 * unit + 1) * D],
+                   all_rhs_attn[:, (2 * unit + 1) * D : (2 * unit + 2) * D])
+            height = 24
+            lhs = None
+        parts = []
+        for place_in_pair, right in enumerate(rhs):
+            left = lhs
+            if left is None:
+                first = 192 if (unit == 1 and place_in_pair == 1) else 0
+                left = all_lhs_attn[pl.ds(pl.multiple_of(first + x_half * 96, 96), 96), :]
+            parts.append(jnp.dot(left, right, preferred_element_type=jnp.float32))
+        return stacked(parts, height)
+
+    units = [("down", 0)] + [("gate", unit) for unit in range(GATE_UNITS)] + [("attn", 0), ("attn", 1)]
+    buffers = {
+        "down": (total_down, xs_down, xr_down, ns_down, nr_down, fs_down, fr_down),
+        "gate": (total_gate, xs_gate, xr_gate, ns_gate, nr_gate, fs_gate, fr_gate),
+        "attn": (total_attn, xs_attn, xr_attn, ns_attn, nr_attn, fs_attn, fr_attn),
+    }
+    started = {}
+
+    def stage_x(number):
+        kind, unit = units[number]
+        total, xs, xr = buffers[kind][:3]
+        for block, value in enumerate(products(kind, unit, flip(xpos))):
+            xs[unit, block] = value.astype(jnp.bfloat16)
+        copy = remote(xs.at[unit], xr.at[unit], x_send_sem.at[number], x_recv_sem.at[number], beside)
+        copy.start()
+        started["x", number] = copy
+        for block, value in enumerate(products(kind, unit, xpos)):
+            total[unit, block] = value
+
+    def stage_near(number):
+        kind, unit = units[number]
+        total, _, xr, ns, nr = buffers[kind][:5]
+        started["x", number].wait_recv()
+        for block in range(4):
+            total[unit, block] = total[unit, block] + xr[unit, block].astype(jnp.float32)
+        ns[unit, 0] = total[unit, near_z(zpos)].astype(jnp.bfloat16)
+        ns[unit, 1] = total[unit, 3 - zpos].astype(jnp.bfloat16)
+        copy = remote(ns.at[unit], nr.at[unit], near_send_sem.at[number], near_recv_sem.at[number], near)
+        copy.start()
+        started["near", number] = copy
+
+    def stage_far(number):
+        kind, unit = units[number]
+        total, _, _, _, nr, fs, fr = buffers[kind]
+        started["near", number].wait_recv()
+        fs[unit] = (total[unit, far_z(zpos)] + nr[unit, 1].astype(jnp.float32)).astype(jnp.bfloat16)
+        copy = remote(fs.at[unit], fr.at[unit], far_send_sem.at[number], far_recv_sem.at[number], far)
+        copy.start()
+        started["far", number] = copy
+
+    def stage_last(number):
+        kind, unit = units[number]
+        total, _, _, _, nr, _, fr = buffers[kind]
+        started["far", number].wait_recv()
+        final = total[unit, zpos] + nr[unit, 0].astype(jnp.float32) + fr[unit].astype(jnp.float32)
+        if kind == "down":
+            out_down[...] = final
+        elif kind == "gate":
+            first = unit * GATE_COLS
+            out_gate[:, first : first + GATE_COLS] = final[:24]
+            out_up[:, first : first + GATE_COLS] = final[24:]
+        else:
+            outs = (out_query, out_key) if unit == 0 else (out_value, out_out)
+            outs[0][...] = final[:24]
+            outs[1][...] = final[24:]
+
+    count = len(units)
+    swap_before = {0: 0, 1: 1, 5: 2}
+    for tick in range(count + 3):
+        if tick in swap_before:
+            finish_swap(swap_before[tick])
+        if tick < count:
+            stage_x(tick)
+        if 0 <= tick - 1 < count:
+            stage_near(tick - 1)
+        if 0 <= tick - 2 < count:
+            stage_far(tick - 2)
+        if 0 <= tick - 3 < count:
+            stage_last(tick - 3)
+        if 1 <= tick <= 5:
+            advance_small(tick - 1)
+    pending.extend(started.values())
+    for copy in pending:
+        copy.wait_send()
+
+
+def weight_gradients(lhs_down, lhs_gate, lhs_attn, rhs_down, rhs_gate, rhs_attn, small):
+    own = D // 32
+    f32, low = jnp.float32, jnp.bfloat16
+    kinds = (("down", 1, 64, D), ("gate", GATE_UNITS, 48, GATE_COLS), ("attn", 2, 48, D))
+    vmem = lambda *shape: pltpu.VMEM(shape, low)
+    scratch = [vmem(512, 512), vmem(192, 512), vmem(384, 512), vmem(512, D), vmem(512, 2 * FF), vmem(512, 4 * D)]
+    scratch += [pltpu.VMEM((units, 4, high, wide), f32) for _, units, high, wide in kinds]
+    for blocks in (4, 4, 2, 2):
+        scratch += [vmem(units, blocks, high, wide) for _, units, high, wide in kinds]
+    for _ in range(2):
+        scratch += [vmem(units, high, wide) for _, units, high, wide in kinds]
+    scratch += [pltpu.VMEM((5, 8, D), f32)] * 2
+    count = 3 + GATE_UNITS
+    scratch += [pltpu.SemaphoreType.DMA((3, 6))] * 2
+    scratch += [pltpu.SemaphoreType.DMA((count,))] * 6
+    scratch += [pltpu.SemaphoreType.DMA((5,))] * 2
+    scratch += [pltpu.SemaphoreType.DMA((3, 2))]
+    outs = [jax.ShapeDtypeStruct((own, D), f32)] * 4 + [jax.ShapeDtypeStruct((own, FF), f32)] * 2
+    outs += [jax.ShapeDtypeStruct((FF // 32, D), f32), jax.ShapeDtypeStruct((8, D), f32)]
+    return pl.pallas_call(
+        weight_kernel,
+        out_shape=outs,
+        in_specs=[pl.BlockSpec(memory_space=pltpu.VMEM)] * 7,
+        out_specs=[pl.BlockSpec(memory_space=pltpu.VMEM)] * 8,
+        scratch_shapes=scratch,
+        compiler_params=pltpu.CompilerParams(collective_id=2, has_side_effects=True, vmem_limit_bytes=56 * 2**20),
+        name="weight_gradients",
+    )(lhs_down, lhs_gate, lhs_attn, rhs_down, rhs_gate, rhs_attn, small)
+
+
+def by_quarter(feature_major):
+    rows, count = feature_major.shape
+    parts = feature_major.reshape(2, 4, 2, 2, rows // 32, count)
+    return jnp.transpose(parts, (0, 3, 2, 1, 4, 5)).reshape(4, rows // 4, count)
 
 
 def bucket_of(offset):
@@ -323,20 +587,30 @@
     )
     grad_in_part, grad_gain_attn = norm_back_first(grad_normed_attn)
     grad_input = (grad_middle + grad_in_part).astype(jnp.bfloat16)[None]
-    summed_weights = tuple(
-        (
-            lax.psum_scatter(grad_w_query, ("rows", "seq"), scatter_dimension=0, tiled=True),
-            lax.psum_scatter(grad_w_key, ("rows", "seq"), scatter_dimension=0, tiled=True),
-            lax.psum_scatter(grad_w_value, ("rows", "seq"), scatter_dimension=0, tiled=True),
-            lax.psum_scatter(grad_w_out, ("rows", "seq"), scatter_dimension=0, tiled=True),
-            lax.psum_scatter(grad_w_gate, ("rows", "seq"), scatter_dimension=0, tiled=True),
-            lax.psum_scatter(grad_w_up, ("rows", "seq"), scatter_dimension=0, tiled=True),
-            lax.psum_scatter(grad_w_down, ("rows", "seq"), scatter_dimension=0, tiled=True),
-        )
-    )
-    table_sum, gain_attn_sum, gain_ffn_sum = lax.psum(
-        (grad_tab, grad_gain_attn, grad_gain_ffn), ("rows", "seq")
-    )
+    if lax.axis_size("rows") == 2 and lax.axis_size("seq") == 16 and tok_count == 128:
+        small = jnp.stack(
+            [grad_gain_attn, grad_gain_ffn, jnp.pad(grad_tab.reshape(-1), (0, D - NB * H))]
+            + [jnp.zeros((D,), jnp.float32)] * 5
+        )
+        *summed_weights, small_sum = weight_gradients(
+            by_quarter(hidden_act.T),
+            by_quarter(normed_ffn.T),
+            jnp.concatenate([by_quarter(normed_attn.T), by_quarter(context_low.T)], axis=1),
+            grad_branch,
+            jnp.concatenate([grad_gate, grad_upward], axis=1),
+            jnp.concatenate([grad_q_low, grad_k_low, grad_v_low, grad_attn], axis=1),
+            small,
+        )
+        gain_attn_sum, gain_ffn_sum = small_sum[0], small_sum[1]
+        table_sum = small_sum[2, : NB * H].reshape(NB, H)
+    else:
+        weight_parts = (grad_w_query, grad_w_key, grad_w_value, grad_w_out, grad_w_gate, grad_w_up, grad_w_down)
+        summed_weights = tuple(
+            lax.psum_scatter(part, ("rows", "seq"), scatter_dimension=0, tiled=True) for part in weight_parts
+        )
+        table_sum, gain_attn_sum, gain_ffn_sum = lax.psum(
+            (grad_tab, grad_gain_attn, grad_gain_ffn), ("rows", "seq")
+        )
     return (
         output,
         grad_input,

time: 992 us -> 546 us (0.55)
  waiting for transfers between devices: 504 us -> 0.09 us
  Pallas kernels: 0 us -> 102 us
  blocking collectives: 98.5 us -> 61.7 us
  matrix products: 112 us -> 81.5 us
  local copies, waits for them, and re-layouts: 231 us -> 259 us
    reduce_scatter x7 -> x0, waiting for transfers between devices: 503 us -> none  [the longest x1 121 us: per_device(): lax.psum_scatter(grad_w_up, ('rows', 'seq'), scatter_dimension=0, tiled=T...]
    pallas_call x0 -> x1, Pallas kernels: none -> 102 us  [weight_gradients(): pl.pallas_call(weight_kernel, out_shape=outs, in_specs=[pl.BlockSpec(memo...]
    psum x1 -> x0, blocking collectives: 37.2 us -> none  [per_device(): lax.psum((grad_tab, grad_gain_attn, grad_gain_ffn), ('rows', 'seq'))]
    dot_general x7 -> x0, matrix products: 23.1 us -> none  [the longest x1 4.74 us: per_device(): jnp.einsum('tf,td->fd', hidden_act, grad_branch, preferred_element_type=j...]
    reshape x2, local copies, waits for them, and re-layouts: 54.1 us -> 64.7 us  [toeplitz_bias(): window.reshape(per_offset.shape[0], row_count, span_len - 1)]
  transfers between devices with their start and end apart: 11 -> 4, of which waited for: 5 -> 0; matrix products, arithmetic and copies ran while one was open for 36% -> 56% of each run, Pallas kernels for 0% -> 0%
where the time goes in v1:
time: 546 us; the launch traced here: 539 us
  local copies, waits for them, and re-layouts  259 us (47%)
  Pallas kernels  102 us (19%)
  matrix products  81.5 us (15%)
  blocking collectives  61.7 us (11%)
  other arithmetic  19.6 us (4%)
  between operations  14.7 us (3%)
    pallas_call x1, Pallas kernels, weight_gradients(): pl.pallas_call(weight_kernel, out_shape=outs, in_specs=[pl.BlockSpec(memo...  102 us
    reshape x2, local copies, waits for them, and re-layouts, toeplitz_bias(): window.reshape(per_offset.shape[0], row_count, span_len - 1)  64.7 us
    another operation x4, local copies, waits for them, and re-layouts, toeplitz_bias(): tiled_vec = jnp.tile(per_offset, (1, row_count + 1))  47.7 us
    slice x2, local copies, waits for them, and re-layouts, toeplitz_bias(): tiled_vec[:, row_count - 1:row_count - 1 + row_count * (span_len - 1)]  27.3 us
    reshape x1, local copies, waits for them, and re-layouts, bias_grad(): flattened = padded.reshape(head_count, row_count * (span_len - 1))  23.4 us
    all_gather x1, blocking collectives, per_device(): seg_all = lax.all_gather(seg_own, 'seq', axis=0, tiled=True)  23 us
    reshape x1, local copies, waits for them, and re-layouts, bias_grad(): flattened.reshape(head_count, row_count + 1, span_len)  22.2 us
    all_gather x1, blocking collectives, per_device(): lax.all_gather(jnp.transpose(log_total), 'seq', axis=0, tiled=True)  19.6 us
  transfers between devices with their start and end apart: 4, of which 0 were waited for; matrix products, arithmetic and copies ran while one was open for 56% of the time, Pallas kernels for 0%

profile of v1, /device:TPU:0, one launch (start us, length us, event | category | flops | bytes accessed | tf_op | source)
XLA Modules:
  0.0 538.7 jit_solution(14296650357241645214)
XLA Ops:
  17.1 23.0 %all-gather = s32[1,2048]{1,0:T(1,128)S(1)} all-gather(s32[1,128]{1,0:T(1,128)S(1)} %copy-done.52), channel_id=2, replica_groups=mesh['rows'=2,'seq'=16] {'seq'}, dimensions={1}, use_global_device_ids=true | all-gather | bytes 8704 | tf_op jit(solution)/shard_map/all_gather | solution.py:379
  42.4 6.0 %tile.8 = f32[12,129,2175]{2,1,0:T(8,128)} broadcast(f32[12,2175]{1,0:T(8,128)S(1)} %convolution_bitcast_fusion.1), dimensions={0,2} | broadcast | bytes 13572000 | tf_op jit(solution)/shard_map/tile | solution.py:343
  48.3 18.0 %tile.9 = f32[12,280575]{1,0:T(8,128)} reshape(f32[12,129,2175]{2,1,0:T(8,128)} %tile.8) | data formatting | bytes 26935200 | tf_op jit(solution)/shard_map/tile | solution.py:343
  66.3 13.6 %slice.30 = f32[12,278272]{1,0:T(8,128)} slice(f32[12,280575]{1,0:T(8,128)} %tile.9), slice={[0:12], [127:278399]} | slice | bytes 26714112 | tf_op jit(solution)/shard_map/slice | solution.py:344
  79.9 38.1 %reshape.271 = f32[12,128,2174]{2,1,0:T(8,128)} reshape(f32[12,278272]{1,0:T(8,128)} %slice.30) | data formatting | bytes 26714112 | tf_op jit(solution)/shard_map/reshape | solution.py:345
  119.1 4.8 copy.44
  123.8 4.7 copy.43
  128.6 8.0 %fusion.108 = (f32[12,128]{1,0:T(8,128)S(1)}, f32[12,128,2048]{2,1,0:T(8,128)S(1)}) fusion(f32[12,128,2174]{2,1,0:T(8,128)} %reshape.271, bf16[128,12,64]{0,2,1:T(8,128)(2,1)} %bitcast.157, bf16[2048,12,64]{0,2,1:T(8,128)(2,1)} %bitcast.141, pred[128,2048]{1,0:T(8,128)(4,1)S(1)} %broadcast_compare_fusion), kind=kOutput, calls=%fused_computation.148 | convolution fusion | flops 412088832 | bytes 28776448 | tf_op jit(solution)/shard_map/rhd,chd->hrc/dot_general | solution.py:397
  160.9 5.9 %tile.10 = f32[12,129,2175]{2,1,0:T(8,128)} broadcast(f32[12,2175]{1,0:T(8,128)S(1)} %convolution_bitcast_fusion), dimensions={0,2} | broadcast | bytes 13572000 | tf_op jit(solution)/shard_map/tile | solution.py:343
  166.8 17.8 %tile.11 = f32[12,280575]{1,0:T(8,128)} reshape(f32[12,129,2175]{2,1,0:T(8,128)} %tile.10) | data formatting | bytes 26935200 | tf_op jit(solution)/shard_map/tile | solution.py:343
  184.7 13.6 %slice.32 = f32[12,278272]{1,0:T(8,128)} slice(f32[12,280575]{1,0:T(8,128)} %tile.11), slice={[0:12], [127:278399]} | slice | bytes 26714112 | tf_op jit(solution)/shard_map/slice | solution.py:344
  198.3 26.7 %reshape.276 = f32[12,128,2174]{2,1,0:T(8,128)} reshape(f32[12,278272]{1,0:T(8,128)} %slice.32) | data formatting | bytes 26714112 | tf_op jit(solution)/shard_map/reshape | solution.py:345
  228.8 9.8 %subtract_multiply_fusion = f32[12,128,2048]{2,1,0:T(8,128)S(1)} fusion(f32[12,128,2048]{2,1,0:T(8,128)} %copy-done.2, f32[12,128]{1,0:T(8,128)S(1)} %bitcast.167, f32[12,128]{1,0:T(8,128)S(1)} %log_add_fusion, pred[128,2048]{1,0:T(8,128)(4,1)} %copy-done.11, bf16[128,12,64]{0,2,1:T(8,128)(2,1)} %bitcast.154, bf16[2048,12,64]{0,2,1:T(8,128)(2,1)} %bitcast.143), kind=kOutput, calls=%fused_computation.8 | convolution fusion | flops 415236096 | bytes 28782592 | tf_op jit(solution)/shard_map/qhd,khd->hqk/dot_general | solution.py:494
  244.9 10.7 %pad.12 = f32[12,128,2174]{2,1,0:T(8,128)} pad(f32[12,128,2048]{2,1,0:T(8,128)} %copy-done.3, f32[]{:T(128)} %constant.27.clone.1), padding=0_0x0_0x0_126 | pad | bytes 25939972 | tf_op jit(solution)/shard_map/jit(_pad)/pad | solution.py:351
  255.7 23.4 %reshape.289 = f32[12,278272]{1,0:T(8,128)} reshape(f32[12,128,2174]{2,1,0:T(8,128)} %pad.12) | data formatting | bytes 26714112 | tf_op jit(solution)/shard_map/reshape | solution.py:352
  279.1 13.5 %pad.13 = f32[12,280575]{1,0:T(8,128)} pad(f32[12,278272]{1,0:T(8,128)} %reshape.289, f32[]{:T(128)} %constant.27.clone.1), padding=0_0x127_2176 | pad | bytes 26824660 | tf_op jit(solution)/shard_map/jit(_pad)/pad | solution.py:353
  292.6 22.2 %reshape.290 = f32[12,129,2175]{2,1,0:T(8,128)} reshape(f32[12,280575]{1,0:T(8,128)} %pad.13) | data formatting | bytes 26935200 | tf_op jit(solution)/shard_map/reshape | solution.py:354
  314.8 5.9 %reduce_sum.108 = f32[12,2175]{1,0:T(8,128)S(1)} reduce(f32[12,129,2175]{2,1,0:T(8,128)} %reshape.290, f32[]{:T(128)} %constant.27.clone.1), dimensions={1}, to_apply=%region_9.10 | reduce | flops 3340800 | bytes 13572004 | tf_op jit(solution)/shard_map/reduce_sum | solution.py:354
  325.7 19.1 %all_gather.29 = f32[2048,12]{0,1:T(8,128)} all-gather(f32[128,12]{0,1:T(8,128)S(1)} %copy-done.38), channel_id=1, replica_groups=mesh['rows'=2,'seq'=16] {'seq'}, dimensions={0}, use_global_device_ids=true | all-gather | bytes 104448 | tf_op jit(solution)/shard_map/all_gather | solution.py:483
  344.8 19.6 %all_gather.27 = f32[2048,12]{0,1:T(8,128)S(1)} all-gather(f32[128,12]{0,1:T(8,128)S(1)} %copy-done.41), channel_id=1, replica_groups=mesh['rows'=2,'seq'=16] {'seq'}, dimensions={0}, use_global_device_ids=true | all-gather | bytes 104448 | tf_op jit(solution)/shard_map/all_gather | solution.py:482
  372.3 9.9 %fusion.3 = f32[12,128,2048]{2,1,0:T(8,128)} fusion(f32[12,128,2174]{2,1,0:T(8,128)} %reshape.276, f32[12,2048]{1,0:T(8,128)S(1)} %bitcast.166, pred[128,2048]{1,0:T(8,128)(4,1)S(1)} %copy-done.12, bf16[128,12,64]{0,2,1:T(8,128)(2,1)S(1)} %bitcast.156, bf16[2048,12,64]{0,2,1:T(8,128)(2,1)S(1)} %bitcast.137), kind=kOutput, calls=%fused_computation.4 | convolution fusion | flops 415236096 | bytes 28868608 | tf_op jit(solution)/shard_map/rhd,chd->hrc/dot_general | solution.py:397
  386.8 7.8 %fusion.31 = bf16[12,64,128]{2,1,0:T(8,128)(2,1)S(1)} fusion(bf16[2048,12,64]{0,2,1:T(8,128)(2,1)} %bitcast.139, f32[12,128,2048]{2,1,0:T(8,128)} %fusion.3), kind=kOutput, calls=%fused_computation.42 | convolution fusion | flops 405897216 | bytes 15925248 | tf_op jit(solution)/shard_map/hkq,qhd->khd/dot_general | solution.py:533
  394.7 10.3 %fusion.34 = bf16[12,64,128]{2,1,0:T(8,128)(2,1)} fusion(bf16[2048,12,64]{0,2,1:T(8,128)(2,1)S(1)} %bitcast.138, f32[12,128,2048]{2,1,0:T(8,128)} %fusion.3, f32[12,2048]{1,0:T(8,128)} %bitcast.165, bf16[128,12,64]{0,2,1:T(8,128)(2,1)} %bitcast.155, bf16[2048,12,64]{0,2,1:T(8,128)(2,1)} %bitcast.140), kind=kOutput, calls=%fused_computation.43 | convolution fusion | flops 814841856 | bytes 19365888 | tf_op jit(solution)/shard_map/hkq,qhd->khd/dot_general | solution.py:527
  416.1 102.0 %weight_gradients.1 = (f32[24,768]{1,0:T(8,128)}, f32[24,768]{1,0:T(8,128)}, f32[24,768]{1,0:T(8,128)}, f32[24,768]{1,0:T(8,128)}, f32[24,2048]{1,0:T(8,128)}, /...) custom-call(bf16[4,512,128]{2,1,0:T(8,128)(2,1)} %bitcast.146, bf16[4,192,128]{2,1,0:T(8,128)(2,1)} %bitcast.158, ...), custom_call_target="tpu_custom_call" | custom-call | tf_op jit(solution)/shard_map/weight_gradients/pallas_call | solution.py:267
  (205 shorter events, 89.6 us)
Async XLA Ops:
  7.2 141.6 %copy-start = (bf16[768,2048]{1,0:T(8,128)(2,1)S(1)}, bf16[768,2048]{1,0:T(8,128)(2,1)}, u32[]{:S(2)}) copy-start(bf16[768,2048]{1,0:T(8,128)(2,1)} %param.21) | copy-start | bytes 9437188
  7.2 9.9 %copy-start.52 = (s32[1,128]{1,0:T(1,128)S(1)}, s32[1,128]{1,0:T(1,128)}, u32[]{:S(2)}) copy-start(s32[1,128]{1,0:T(1,128)} %param.14) | copy-start | bytes 1540
  7.2 34.6 %copy-start.53 = (bf16[768]{0:T(1024)(128)(2,1)S(1)}, bf16[768]{0:T(1024)(128)(2,1)}, u32[]{:S(2)}) copy-start(bf16[768]{0:T(1024)(128)(2,1)} %param.25) | copy-start | bytes 4612
  7.2 34.6 %copy-start.56 = (bf16[32,12]{0,1:T(8,128)(2,1)S(1)}, bf16[32,12]{0,1:T(8,128)(2,1)}, u32[]{:S(2)}) copy-start(bf16[32,12]{0,1:T(8,128)(2,1)} %param.23) | copy-start | bytes 2308
  7.2 111.8 %all-gather.8.cloned.1.call-start = ((), (), s32[]{:S(2)}) async-start(), calls=%async_computation.1 | async-start | bytes 3342336 | tf_op jit(solution)/shard_map/all_gather | solution.py:413
  9.0 32.9 %copy-start.42 = (f32[128]{0:T(128)}, f32[128]{0:T(128)S(1)}, u32[]{:S(2)}) copy-start(f32[128]{0:T(128)S(1)} %fusion.95) | copy-start | bytes 1540
  9.7 38.7 %copy-start.35 = (f32[768]{0:T(1024)}, f32[768]{0:T(1024)S(1)}, u32[]{:S(2)}) copy-start(f32[768]{0:T(1024)S(1)} %convert_element_type.225) | copy-start | bytes 9220
  12.1 111.7 %all-gather.6.cloned.1.call-start = ((), (), s32[]{:S(2)}) async-start(), calls=%async_computation | async-start | bytes 3342336 | tf_op jit(solution)/shard_map/all_gather | solution.py:412
  14.6 307.9 %all-gather.10.cloned.1.call-start = ((), (), s32[]{:S(2)}) async-start(), calls=%async_computation.2 | async-start | bytes 3342336 | tf_op jit(solution)/shard_map/all_gather | solution.py:556
  17.0 365.1 %all-gather.12.cloned.1.call-start = ((), (), s32[]{:S(2)}) async-start(), calls=%async_computation.3 | async-start | bytes 3342336 | tf_op jit(solution)/shard_map/all_gather | solution.py:557
  17.1 100.9 %copy-start.50 = (pred[128]{0:T(512)(128)(4,1)}, pred[128]{0:T(512)(128)(4,1)S(1)}, u32[]{:S(2)}) copy-start(pred[128]{0:T(512)(128)(4,1)S(1)} %broadcast_compare_fusion.1) | copy-start | bytes 388
  79.9 38.1 %copy-start.29 = (bf16[1,128,768]{2,1,0:T(8,128)(2,1)S(1)}, bf16[1,128,768]{2,1,0:T(8,128)(2,1)}, u32[]{:S(2)}) copy-start(bf16[1,128,768]{2,1,0:T(8,128)(2,1)} %param.15) | copy-start | bytes 589828
  119.0 21.2 %copy-start.11 = (pred[128,2048]{1,0:T(8,128)(4,1)}, pred[128,2048]{1,0:T(8,128)(4,1)S(1)}, u32[]{:S(2)}) copy-start(pred[128,2048]{1,0:T(8,128)(4,1)S(1)} %broadcast_compare_fusion) | copy-start | bytes 786436
  145.9 9.9 %copy-start.44 = (f32[128]{0:T(128)}, f32[128]{0:T(128)S(1)}, u32[]{:S(2)}) copy-start(f32[128]{0:T(128)S(1)} %fusion.96) | copy-start | bytes 1540
  198.3 26.7 %copy-start.24 = (bf16[128,768]{1,0:T(8,128)(2,1)S(1)}, bf16[128,768]{1,0:T(8,128)(2,1)}, u32[]{:S(2)}) copy-start(bf16[128,768]{1,0:T(8,128)(2,1)} %convolution_convert_fusion) | copy-start | bytes 589828
  198.3 26.9 %copy-start.33 = (bf16[128,12,64]{0,2,1:T(8,128)(2,1)S(1)}, bf16[128,12,64]{0,2,1:T(8,128)(2,1)}, u32[]{:S(2)}) copy-start(bf16[128,12,64]{0,2,1:T(8,128)(2,1)} %copy-done.32) | copy-start | bytes 589828
  198.3 27.6 %copy-start.45 = (f32[128]{0:T(128)S(1)}, f32[128]{0:T(128)}, u32[]{:S(2)}) copy-start(f32[128]{0:T(128)} %copy-done.44) | copy-start | bytes 1540
  198.3 28.6 %copy-start.17 = (bf16[2048,128]{0,1:T(8,128)(2,1)S(1)}, bf16[2048,128]{0,1:T(8,128)(2,1)}, u32[]{:S(2)}) copy-start(bf16[2048,128]{0,1:T(8,128)(2,1)} %get-tuple-element.75) | copy-start | bytes 1572868
  228.7 9.8 %copy-start.37 = (f32[128,12]{0,1:T(8,128)}, f32[128,12]{0,1:T(8,128)S(1)}, u32[]{:S(2)}) copy-start(f32[128,12]{0,1:T(8,128)S(1)} %multiply_reduce_fusion.1) | copy-start | bytes 18436
  322.5 22.3 %copy-start.41 = (f32[128,12]{0,1:T(8,128)S(1)}, f32[128,12]{0,1:T(8,128)}, u32[]{:S(2)}) copy-start(f32[128,12]{0,1:T(8,128)} %get-tuple-element.64) | copy-start | bytes 18436
  394.6 15.0 %copy-start.9 = (bf16[1,128,768]{2,1,0:T(8,128)(2,1)S(1)}, bf16[1,128,768]{2,1,0:T(8,128)(2,1)}, u32[]{:S(2)}) copy-start(bf16[1,128,768]{2,1,0:T(8,128)(2,1)} %param.13) | copy-start | bytes 589828
  394.7 15.0 %copy-start.36 = (f32[768]{0:T(1024)S(1)}, f32[768]{0:T(1024)}, u32[]{:S(2)}) copy-start(f32[768]{0:T(1024)} %copy-done.35) | copy-start | bytes 9220
  394.7 15.0 %copy-start.43 = (f32[128]{0:T(128)S(1)}, f32[128]{0:T(128)}, u32[]{:S(2)}) copy-start(f32[128]{0:T(128)} %copy-done.42) | copy-start | bytes 1540
  411.4 120.6 %copy-start.1 = (bf16[768,2048]{1,0:T(8,128)(2,1)S(1)}, bf16[768,2048]{1,0:T(8,128)(2,1)}, u32[]{:S(2)}) copy-start(bf16[768,2048]{1,0:T(8,128)(2,1)} %param.21) | copy-start | bytes 9437188
  (38 other events, 152.8 us)
Sparse Core Ops, SparseCore 0:
  12.2 48.1 all-gather.7
  63.3 43.9 all-gather.5
  110.2 44.2 all-gather.9
  158.8 42.4 all-gather.11

commit v2 on v0

--- a/solution.py
+++ b/solution.py
@@ -3,12 +3,15 @@
 import jax
 import jax.numpy as jnp
 from jax import lax
+from jax.experimental import pallas as pl
+from jax.experimental.pallas import tpu as pltpu
 from jax.sharding import PartitionSpec as P
 
 D = 768
 H = 12
 DH = 64
 NB = 32
+FF = 2048
 
 
 BORDERS = (12, 16, 23, 32, 46, 64, 91)
@@ -353,6 +356,706 @@
     )
 
 
+MESH = pl.DeviceIdType.MESH
+GATE_UNITS = 4
+GATE_COLS = FF // GATE_UNITS
+
+
+def place():
+    row = lax.axis_index("rows")
+    spot = lax.axis_index("seq")
+    return row, spot // 4, (spot // 2) % 2, spot % 2
+
+
+def device(row, zpos, xpos, core):
+    return (row, 4 * zpos + 2 * xpos + core)
+
+
+def flip(bit):
+    return 1 - bit
+
+
+def near_z(zpos):
+    return zpos + 1 - 2 * (zpos % 2)
+
+
+def far_z(zpos):
+    return (zpos + 2) % 4
+
+
+def greet(peers):
+    barrier = pltpu.get_barrier_semaphore()
+    for peer in peers:
+        pl.semaphore_signal(barrier, inc=1, device_id=peer, device_id_type=MESH)
+    pl.semaphore_wait(barrier, len(peers))
+
+
+def remote(src, dst, send_sem, recv_sem, peer):
+    return pltpu.make_async_remote_copy(
+        src_ref=src, dst_ref=dst, send_sem=send_sem, recv_sem=recv_sem, device_id=peer, device_id_type=MESH
+    )
+
+
+def weight_kernel(
+    lhs_down, lhs_gate, lhs_attn, rhs_down, rhs_gate, rhs_attn, small,
+    out_query, out_key, out_value, out_out, out_gate, out_up, out_down, out_small,
+    all_lhs_down, all_lhs_gate, all_lhs_attn, all_rhs_down, all_rhs_gate, all_rhs_attn,
+    total_down, total_gate, total_attn,
+    xs_down, xs_gate, xs_attn, xr_down, xr_gate, xr_attn,
+    ns_down, ns_gate, ns_attn, nr_down, nr_gate, nr_attn,
+    fs_down, fs_gate, fs_attn, fr_down, fr_gate, fr_attn,
+    small_send, small_recv,
+    swap_send_sem, swap_recv_sem, x_send_sem, x_recv_sem, near_send_sem, near_recv_sem, far_send_sem, far_recv_sem,
+    small_send_sem, small_recv_sem, local_sem,
+):
+    row, zpos, xpos, core = place()
+    mate = device(row, zpos, xpos, flip(core))
+    across = device(flip(row), zpos, xpos, core)
+    slant = device(flip(row), zpos, xpos, flip(core))
+    beside = device(row, zpos, flip(xpos), core)
+    near = device(row, near_z(zpos), xpos, core)
+    far = device(row, far_z(zpos), xpos, core)
+    greet((mate, across, slant, beside, near, far))
+    mine = 2 * row + core
+    mate_part = 2 * row + flip(core)
+    across_part = 2 * flip(row) + core
+    slant_part = 2 * flip(row) + flip(core)
+
+    pending = []
+    swaps = []
+    groups = ((lhs_down, rhs_down, all_lhs_down, all_rhs_down), (lhs_gate, rhs_gate, all_lhs_gate, all_rhs_gate),
+              (lhs_attn, rhs_attn, all_lhs_attn, all_rhs_attn))
+
+    def lanes(part):
+        return pl.ds(pl.multiple_of(part * 128, 128), 128)
+
+    for index, (lhs, rhs, all_lhs, all_rhs) in enumerate(groups):
+        copies = []
+        for slot, (peer, part) in enumerate(((across, across_part), (slant, slant_part), (mate, mate_part))):
+            copies.append(remote(lhs.at[part], all_lhs.at[:, lanes(mine)], swap_send_sem.at[index, slot],
+                                 swap_recv_sem.at[index, slot], peer))
+        for slot, peer in ((3, across), (4, mate)):
+            copies.append(remote(rhs, all_rhs.at[lanes(mine)], swap_send_sem.at[index, slot],
+                                 swap_recv_sem.at[index, slot], peer))
+        own_lhs = pltpu.make_async_copy(lhs.at[mine], all_lhs.at[:, lanes(mine)], local_sem.at[index, 0])
+        own_rhs = pltpu.make_async_copy(rhs, all_rhs.at[lanes(mine)], local_sem.at[index, 1])
+        for copy in copies:
+            copy.start()
+        own_lhs.start()
+        own_rhs.start()
+        onward = remote(all_rhs.at[lanes(across_part)], all_rhs.at[lanes(across_part)],
+                        swap_send_sem.at[index, 5], swap_recv_sem.at[index, 5], mate)
+        swaps.append((copies, (own_lhs, own_rhs), onward))
+
+    def finish_swap(index):
+        copies, locals_, onward = swaps[index]
+        copies[3].wait_recv()
+        onward.start()
+        for slot in (0, 1, 2, 4):
+            copies[slot].wait_recv()
+        for copy in locals_:
+            copy.wait()
+        onward.wait_recv()
+        pending.extend(copies)
+        pending.append(onward)
+
+    small_send[0] = small[...]
+    small_peers = (mate, across, beside, near, far)
+    small_step = 0
+
+    def advance_small(step):
+        copy = remote(small_send.at[step], small_recv.at[step], small_send_sem.at[step], small_recv_sem.at[step],
+                      small_peers[step])
+        copy.start()
+        copy.wait_recv()
+        summed = small_send[step] + small_recv[step]
+        if step < 4:
+            small_send[step + 1] = summed
+        else:
+            out_small[...] = summed
+        pending.append(copy)
+
+    def half_rows(x_half, height):
+        return pl.ds(pl.multiple_of(x_half * height, height), height)
+
+    def stacked(parts, height):
+        return [jnp.concatenate([part[height * block : height * (block + 1)] for part in parts], axis=0)
+                for block in range(4)]
+
+    def products(kind, unit, x_half):
+        if kind == "down":
+            lhs, rhs = all_lhs_down[half_rows(x_half, 256), :], (all_rhs_down[...],)
+            height = 64
+        elif kind == "gate":
+            lhs = all_lhs_gate[half_rows(x_half, 96), :]
+            first = unit * GATE_COLS
+            rhs = (all_rhs_gate[:, first : first + GATE_COLS], all_rhs_gate[:, FF + first : FF + first + GATE_COLS])
+            height = 24
+        else:
+            rhs = (all_rhs_attn[:, 2 * unit * D : (2 * unit + 1) * D],
+                   all_rhs_attn[:, (2 * unit + 1) * D : (2 * unit + 2) * D])
+            height = 24
+            lhs = None
+        parts = []
+        for place_in_pair, right in enumerate(rhs):
+            left = lhs
+            if left is None:
+                first = 192 if (unit == 1 and place_in_pair == 1) else 0
+                left = all_lhs_attn[pl.ds(pl.multiple_of(first + x_half * 96, 96), 96), :]
+            parts.append(jnp.dot(left, right, preferred_element_type=jnp.float32))
+        return stacked(parts, height)
+
+    units = [("down", 0)] + [("gate", unit) for unit in range(GATE_UNITS)] + [("attn", 0), ("attn", 1)]
+    buffers = {
+        "down": (total_down, xs_down, xr_down, ns_down, nr_down, fs_down, fr_down),
+        "gate": (total_gate, xs_gate, xr_gate, ns_gate, nr_gate, fs_gate, fr_gate),
+        "attn": (total_attn, xs_attn, xr_attn, ns_attn, nr_attn, fs_attn, fr_attn),
+    }
+    started = {}
+
+    def stage_x(number):
+        kind, unit = units[number]
+        total, xs, xr = buffers[kind][:3]
+        for block, value in enumerate(products(kind, unit, flip(xpos))):
+            xs[unit, block] = value.astype(jnp.bfloat16)
+        copy = remote(xs.at[unit], xr.at[unit], x_send_sem.at[number], x_recv_sem.at[number], beside)
+        copy.start()
+        started["x", number] = copy
+        for block, value in enumerate(products(kind, unit, xpos)):
+            total[unit, block] = value
+
+    def stage_near(number):
+        kind, unit = units[number]
+        total, _, xr, ns, nr = buffers[kind][:5]
+        started["x", number].wait_recv()
+        for block in range(4):
+            total[unit, block] = total[unit, block] + xr[unit, block].astype(jnp.float32)
+        ns[unit, 0] = total[unit, near_z(zpos)].astype(jnp.bfloat16)
+        ns[unit, 1] = total[unit, 3 - zpos].astype(jnp.bfloat16)
+        copy = remote(ns.at[unit], nr.at[unit], near_send_sem.at[number], near_recv_sem.at[number], near)
+        copy.start()
+        started["near", number] = copy
+
+    def stage_far(number):
+        kind, unit = units[number]
+        total, _, _, _, nr, fs, fr = buffers[kind]
+        started["near", number].wait_recv()
+        fs[unit] = (total[unit, far_z(zpos)] + nr[unit, 1].astype(jnp.float32)).astype(jnp.bfloat16)
+        copy = remote(fs.at[unit], fr.at[unit], far_send_sem.at[number], far_recv_sem.at[number], far)
+        copy.start()
+        started["far", number] = copy
+
+    def stage_last(number):
+        kind, unit = units[number]
+        total, _, _, _, nr, _, fr = buffers[kind]
+        started["far", number].wait_recv()
+        final = total[unit, zpos] + nr[unit, 0].astype(jnp.float32) + fr[unit].astype(jnp.float32)
+        if kind == "down":
+            out_down[...] = final
+        elif kind == "gate":
+            first = unit * GATE_COLS
+            out_gate[:, first : first + GATE_COLS] = final[:24]
+            out_up[:, first : first + GATE_COLS] = final[24:]
+        else:
+            outs = (out_query, out_key) if unit == 0 else (out_value, out_out)
+            outs[0][...] = final[:24]
+            outs[1][...] = final[24:]
+
+    count = len(units)
+    swap_before = {0: 0, 1: 1, 5: 2}
+    for tick in range(count + 3):
+        if tick in swap_before:
+            finish_swap(swap_before[tick])
+        if tick < count:
+            stage_x(tick)
+        if 0 <= tick - 1 < count:
+            stage_near(tick - 1)
+        if 0 <= tick - 2 < count:
+            stage_far(tick - 2)
+        if 0 <= tick - 3 < count:
+            stage_last(tick - 3)
+        if 1 <= tick <= 5:
+            advance_small(tick - 1)
+    pending.extend(started.values())
+    for copy in pending:
+        copy.wait_send()
+
+
+def weight_gradients(lhs_down, lhs_gate, lhs_attn, rhs_down, rhs_gate, rhs_attn, small):
+    own = D // 32
+    f32, low = jnp.float32, jnp.bfloat16
+    kinds = (("down", 1, 64, D), ("gate", GATE_UNITS, 48, GATE_COLS), ("attn", 2, 48, D))
+    vmem = lambda *shape: pltpu.VMEM(shape, low)
+    scratch = [vmem(512, 512), vmem(192, 512), vmem(384, 512), vmem(512, D), vmem(512, 2 * FF), vmem(512, 4 * D)]
+    scratch += [pltpu.VMEM((units, 4, high, wide), f32) for _, units, high, wide in kinds]
+    for blocks in (4, 4, 2, 2):
+        scratch += [vmem(units, blocks, high, wide) for _, units, high, wide in kinds]
+    for _ in range(2):
+        scratch += [vmem(units, high, wide) for _, units, high, wide in kinds]
+    scratch += [pltpu.VMEM((5, 8, D), f32)] * 2
+    count = 3 + GATE_UNITS
+    scratch += [pltpu.SemaphoreType.DMA((3, 6))] * 2
+    scratch += [pltpu.SemaphoreType.DMA((count,))] * 6
+    scratch += [pltpu.SemaphoreType.DMA((5,))] * 2
+    scratch += [pltpu.SemaphoreType.DMA((3, 2))]
+    outs = [jax.ShapeDtypeStruct((own, D), f32)] * 4 + [jax.ShapeDtypeStruct((own, FF), f32)] * 2
+    outs += [jax.ShapeDtypeStruct((FF // 32, D), f32), jax.ShapeDtypeStruct((8, D), f32)]
+    return pl.pallas_call(
+        weight_kernel,
+        out_shape=outs,
+        in_specs=[pl.BlockSpec(memory_space=pltpu.VMEM)] * 7,
+        out_specs=[pl.BlockSpec(memory_space=pltpu.VMEM)] * 8,
+        scratch_shapes=scratch,
+        compiler_params=pltpu.CompilerParams(collective_id=2, has_side_effects=True, vmem_limit_bytes=56 * 2**20),
+        name="weight_gradients",
+    )(lhs_down, lhs_gate, lhs_attn, rhs_down, rhs_gate, rhs_attn, small)
+
+
+def by_quarter(feature_major):
+    rows, count = feature_major.shape
+    parts = feature_major.reshape(2, 4, 2, 2, rows // 32, count)
+    return jnp.transpose(parts, (0, 3, 2, 1, 4, 5)).reshape(4, rows // 4, count)
+
+
+GROUPS = 4
+HEADS_HERE = H // GROUPS
+WIDE = HEADS_HERE * DH
+MARKS = 16
+KV_ROWS = 2 * WIDE + MARKS
+QUERIES = 512
+SEPARATE = -1e30
+
+
+def flat_block(zpos, column):
+    return 4 * zpos + column
+
+
+def bias_tiles_kernel(profile, tiles):
+    for head in range(HEADS_HERE):
+        spread = jnp.broadcast_to(profile[head : head + 1, :], (128, 512))
+        rolled = pltpu.roll(spread, 0, 1, stride=1, stride_axis=0)
+        for slot, first in ((1, 384), (2, 256), (3, 128)):
+            tiles[head, slot] = rolled[:, first : first + 128]
+        for slot, at in ((0, 511), (4, 1)):
+            tiles[head, slot] = jnp.broadcast_to(profile[head : head + 1, at : at + 1], (128, 128))
+
+
+def bias_tiles(profile):
+    return pl.pallas_call(
+        bias_tiles_kernel,
+        out_shape=jax.ShapeDtypeStruct((HEADS_HERE, 5, 128, 128), jnp.float32),
+        name="bias_tiles",
+    )(profile)
+
+
+def tile_sums_kernel(tiles, sums):
+    sums[...] = jnp.zeros_like(sums)
+    for head in range(HEADS_HERE):
+        blank = jnp.zeros((8, 128), jnp.float32)
+        carried = None
+        for step in reversed(range(16)):
+            rows = slice(8 * step, 8 * step + 8)
+            part = jnp.concatenate(
+                [blank, tiles[head, 3, rows, :], tiles[head, 2, rows, :], tiles[head, 1, rows, :]], axis=1
+            )
+            carried = part if carried is None else part + pltpu.roll(carried, 512 - 8, 1)
+        one = carried[7:8]
+        for step in reversed(range(7)):
+            one = carried[step : step + 1] + pltpu.roll(one, 512 - 1, 1)
+        sums[head, 0:1, :] = one
+        sums[head, 1:2, 0:128] = jnp.sum(tiles[head, 0], axis=0, keepdims=True)
+        sums[head, 1:2, 128:256] = jnp.sum(tiles[head, 4], axis=0, keepdims=True)
+
+
+def tile_sums(tiles):
+    return pl.pallas_call(
+        tile_sums_kernel,
+        out_shape=jax.ShapeDtypeStruct((HEADS_HERE, 8, 512), jnp.float32),
+        name="tile_sums",
+    )(tiles)
+
+
+def head_rows(head, first=0):
+    return pl.ds(pl.multiple_of(first + DH * head, DH), DH)
+
+
+def marked_queries(kv, queries, marked, zpos, column):
+    for block in range(4):
+        marks = kv[flat_block(block, column), 2 * WIDE :, :].astype(jnp.float32)
+        apart = ((1.0 - marks) * SEPARATE).astype(jnp.bfloat16)
+        for head in range(HEADS_HERE):
+            marked[head, :DH, 128 * block : 128 * block + 128] = queries[block, DH * head : DH * head + DH, :]
+            marked[head, DH:, 128 * block : 128 * block + 128] = apart
+
+
+def block_scores_t(kv, marked, tiles, head, key_spot, column):
+    keys = jnp.concatenate([kv[key_spot, head_rows(head), :], kv[key_spot, 2 * WIDE :, :]], axis=0)
+    product = lax.dot_general(keys, marked[head], (((0,), (0,)), ((), ())), preferred_element_type=jnp.float32)
+    bias = [tiles[head, bias_slot(key_spot, block, column)] for block in range(4)]
+    return product + jnp.concatenate(bias, axis=1)
+
+
+def bias_slot(key_spot, block, column):
+    return jnp.clip(key_spot - flat_block(block, column), -2, 2) + 2
+
+
+def wide_rows(kv, rows, chunk):
+    return jnp.concatenate([kv[flat_block(chunk, spot), rows, :] for spot in range(4)], axis=1)
+
+
+def forward_kernel(
+    sent, tiles, context, kv, queries, out_heads, lse,
+    marked, score_buf, weight_buf, highest, totals, summed, out_low,
+    z_send, z_recv, q_send, q_recv, x_send, x_recv, c_send, c_recv, o_send, o_recv, local_sem,
+):
+    row, zpos, xpos, core = place()
+    column = 2 * xpos + core
+    beside_column = 2 * flip(xpos) + core
+    mate = device(row, zpos, xpos, flip(core))
+    beside = device(row, zpos, flip(xpos), core)
+    along = [device(row, (zpos + step) % 4, xpos, core) for step in range(1, 4)]
+    greet([mate, beside] + along)
+    kv_part, q_part = pl.ds(0, KV_ROWS), pl.ds(KV_ROWS, WIDE)
+    here = flat_block(zpos, column)
+    sends = []
+
+    def go(copy):
+        copy.start()
+        sends.append(copy)
+        return copy
+
+    own_kv = pltpu.make_async_copy(sent.at[zpos, kv_part], kv.at[here], local_sem.at[0])
+    own_q = pltpu.make_async_copy(sent.at[zpos, q_part], queries.at[zpos], local_sem.at[1])
+    own_kv.start()
+    own_q.start()
+    x_copies, c_copies, on_copies = [None] * 4, [None] * 4, [None] * 4
+    x_copies[0] = go(remote(sent.at[zpos, kv_part], kv.at[here], x_send.at[0], x_recv.at[0], beside))
+    z_copies = [go(remote(sent.at[(zpos + step) % 4, kv_part], kv.at[here], z_send.at[step], z_recv.at[step],
+                          along[step - 1])) for step in range(1, 4)]
+    c_copies[0] = go(remote(sent.at[zpos, kv_part], kv.at[here], c_send.at[0], c_recv.at[0], mate))
+    q_copies = [go(remote(sent.at[(zpos + step) % 4, q_part], queries.at[zpos], q_send.at[step], q_recv.at[step],
+                          along[step - 1])) for step in range(1, 4)]
+
+    def pass_on(step):
+        spot = kv.at[flat_block((zpos + 4 - step) % 4, beside_column)]
+        x_copies[step].wait_recv()
+        on_copies[step] = go(remote(spot, spot, c_send.at[4 + step], c_recv.at[4 + step], mate))
+
+    for step in range(1, 4):
+        z_copies[step - 1].wait_recv()
+        spot = kv.at[flat_block((zpos + 4 - step) % 4, column)]
+        x_copies[step] = go(remote(spot, spot, x_send.at[step], x_recv.at[step], beside))
+        c_copies[step] = go(remote(spot, spot, c_send.at[step], c_recv.at[step], mate))
+        pass_on(step - 1)
+    for copy in q_copies:
+        copy.wait_recv()
+    own_q.wait()
+    own_kv.wait()
+    marked_queries(kv, queries, marked, zpos, column)
+    highest[...] = jnp.full_like(highest, -1e38)
+    totals[...] = jnp.zeros_like(totals)
+    summed[...] = jnp.zeros_like(summed)
+
+    def attend(step):
+        chunk = (zpos + 4 - step) % 4
+        c_copies[step].wait_recv()
+        on_copies[step].wait_recv()
+
+        def one_head(head, carry):
+            newest = highest[head]
+            for spot in range(4):
+                scores = block_scores_t(kv, marked, tiles, head, flat_block(chunk, spot), column)
+                score_buf[spot] = scores
+                newest = jnp.maximum(newest, jnp.max(scores, axis=0, keepdims=True))
+            rescale = jnp.exp(highest[head] - newest)
+            total = totals[head] * rescale
+            for spot in range(4):
+                weights = jnp.exp(score_buf[spot] - newest)
+                total = total + jnp.sum(weights, axis=0, keepdims=True)
+                weight_buf[128 * spot : 128 * spot + 128, :] = weights.astype(jnp.bfloat16)
+            highest[head] = newest
+            totals[head] = total
+            values = wide_rows(kv, head_rows(head, WIDE), chunk)
+            summed[head] = summed[head] * rescale + jnp.dot(
+                values, weight_buf[...], preferred_element_type=jnp.float32
+            )
+            return carry
+
+        lax.fori_loop(0, HEADS_HERE, one_head, 0)
+
+    for step in range(4):
+        if step == 3:
+            pass_on(3)
+        attend(step)
+    for head in range(HEADS_HERE):
+        done = summed[head] / totals[head]
+        out_heads[head] = done
+        lse[head] = highest[head] + jnp.log(totals[head])
+        low = done.astype(jnp.bfloat16)
+        for block in range(4):
+            out_low[block, DH * head : DH * head + DH, :] = low[:, 128 * block : 128 * block + 128]
+    context[zpos] = out_low[zpos]
+    o_copies = [go(remote(out_low.at[(zpos + step) % 4], context.at[zpos], o_send.at[step], o_recv.at[step],
+                          along[step - 1])) for step in range(1, 4)]
+    for copy in o_copies:
+        copy.wait_recv()
+    for copy in sends:
+        copy.wait_send()
+
+
+def attention_forward(sent, tiles):
+    low, f32 = jnp.bfloat16, jnp.float32
+    dma = pltpu.SemaphoreType.DMA
+    return pl.pallas_call(
+        forward_kernel,
+        out_shape=[
+            jax.ShapeDtypeStruct((GROUPS, WIDE, 128), low),
+            jax.ShapeDtypeStruct((16, KV_ROWS, 128), low),
+            jax.ShapeDtypeStruct((4, WIDE, 128), low),
+            jax.ShapeDtypeStruct((HEADS_HERE, DH, QUERIES), f32),
+            jax.ShapeDtypeStruct((HEADS_HERE, 1, QUERIES), f32),
+        ],
+        in_specs=[pl.BlockSpec(memory_space=pltpu.VMEM)] * 2,
+        out_specs=[pl.BlockSpec(memory_space=pltpu.VMEM)] * 5,
+        scratch_shapes=[
+            pltpu.VMEM((HEADS_HERE, DH + MARKS, QUERIES), low),
+            pltpu.VMEM((4, 128, QUERIES), f32),
+            pltpu.VMEM((512, QUERIES), low),
+            pltpu.VMEM((HEADS_HERE, 1, QUERIES), f32),
+            pltpu.VMEM((HEADS_HERE, 1, QUERIES), f32),
+            pltpu.VMEM((HEADS_HERE, DH, QUERIES), f32),
+            pltpu.VMEM((4, WIDE, 128), low),
+            dma((4,)), dma((4,)), dma((4,)), dma((4,)), dma((4,)), dma((4,)), dma((8,)), dma((8,)),
+            dma((4,)), dma((4,)), dma((2,)),
+        ],
+        compiler_params=pltpu.CompilerParams(collective_id=0, has_side_effects=True, vmem_limit_bytes=48 * 2**20),
+        name="attention_forward",
+    )(sent, tiles)
+
+
+def backward_kernel(
+    sent, kv, queries, out_heads, lse, tiles, grads, tile_grads,
+    marked, cotangents, weight_buf, grad_buf, deltas, query_sum, key_sum,
+    core_out, core_in, x_out, x_in, back_out, query_out,
+    d_send, d_recv, c_send, c_recv, x_send, x_recv, b_send, b_recv, q_send, q_recv,
+):
+    row, zpos, xpos, core = place()
+    column = 2 * xpos + core
+    mate = device(row, zpos, xpos, flip(core))
+    beside = device(row, zpos, flip(xpos), core)
+    along = [device(row, (zpos + step) % 4, xpos, core) for step in range(1, 4)]
+    greet([mate, beside] + along)
+    sends = []
+
+    def go(copy):
+        copy.start()
+        sends.append(copy)
+        return copy
+
+    d_copies = [go(remote(sent.at[(zpos + step) % 4], cotangents.at[zpos], d_send.at[step], d_recv.at[step],
+                          along[step - 1])) for step in range(1, 4)]
+    cotangents[zpos] = sent[zpos]
+    marked_queries(kv, queries, marked, zpos, column)
+    tile_grads[...] = jnp.zeros_like(tile_grads)
+    query_sum[...] = jnp.zeros_like(query_sum)
+    for copy in d_copies:
+        copy.wait_recv()
+
+    def wide_cotangent(head):
+        return jnp.concatenate([cotangents[block, head_rows(head), :] for block in range(4)], axis=1)
+
+    for head in range(HEADS_HERE):
+        deltas[head] = jnp.sum(wide_cotangent(head).astype(jnp.float32) * out_heads[head], axis=0, keepdims=True)
+
+    core_copies, x_copies, back_copies = [None] * 4, [None] * 4, [None] * 4
+
+    def chunk_of(step):
+        return (zpos + 1 + step) % 4
+
+    def differentiate(step):
+        chunk = chunk_of(step)
+
+        def one_head(head, carry):
+            cotangent = wide_cotangent(head)
+            for spot in range(4):
+                key_spot = flat_block(chunk, spot)
+                scores = block_scores_t(kv, marked, tiles, head, key_spot, column)
+                probs = jnp.exp(scores - lse[head])
+                grad_probs = lax.dot_general(kv[key_spot, head_rows(head, WIDE), :], cotangent,
+                                             (((0,), (0,)), ((), ())), preferred_element_type=jnp.float32)
+                grad_scores = probs * (grad_probs - deltas[head])
+                for block in range(4):
+                    slot = bias_slot(key_spot, block, column)
+                    tile_grads[head, slot] = tile_grads[head, slot] + grad_scores[:, 128 * block : 128 * block + 128]
+                weight_buf[128 * spot : 128 * spot + 128, :] = probs.astype(jnp.bfloat16)
+                grad_buf[128 * spot : 128 * spot + 128, :] = grad_scores.astype(jnp.bfloat16)
+            query_wide = marked[head, :DH, :]
+            keys = wide_rows(kv, head_rows(head), chunk)
+            query_sum[head] = query_sum[head] + jnp.dot(keys, grad_buf[...], preferred_element_type=jnp.float32)
+            over_queries = (((1,), (1,)), ((), ()))
+            grad_keys = lax.dot_general(query_wide, grad_buf[...], over_queries, preferred_element_type=jnp.float32)
+            grad_values = lax.dot_general(cotangent, weight_buf[...], over_queries, preferred_element_type=jnp.float32)
+            for spot in range(4):
+                lanes = slice(128 * spot, 128 * spot + 128)
+                key_sum[step, spot, head_rows(head), :] = grad_keys[:, lanes]
+                key_sum[step, spot, head_rows(head, WIDE), :] = grad_values[:, lanes]
+            return carry
+
+        lax.fori_loop(0, HEADS_HERE, one_head, 0)
+        for x_half in range(2):
+            core_out[step, x_half] = key_sum[step, 2 * x_half + flip(core)].astype(jnp.bfloat16)
+        core_copies[step] = go(remote(core_out.at[step], core_in.at[step], c_send.at[step], c_recv.at[step], mate))
+
+    def reduce_cores(step):
+        core_copies[step].wait_recv()
+        x_out[step] = (key_sum[step, 2 * flip(xpos) + core] + core_in[step, flip(xpos)].astype(jnp.float32)
+                       ).astype(jnp.bfloat16)
+        x_copies[step] = go(remote(x_out.at[step], x_in.at[step], x_send.at[step], x_recv.at[step], beside))
+
+    def reduce_x(step):
+        x_copies[step].wait_recv()
+        total = key_sum[step, column] + core_in[step, xpos].astype(jnp.float32) + x_in[step].astype(jnp.float32)
+        if step < 3:
+            back_out[step] = total.astype(jnp.bfloat16)
+            back_copies[step] = go(remote(back_out.at[step], grads.at[zpos, pl.ds(0, 2 * WIDE)], b_send.at[step],
+                                          b_recv.at[step], along[step]))
+        else:
+            grads[zpos, : 2 * WIDE, :] = total.astype(jnp.bfloat16)
+
+    for tick in range(6):
+        if tick < 4:
+            differentiate(tick)
+        if tick == 3:
+            for head in range(HEADS_HERE):
+                for block in range(4):
+                    query_out[block, DH * head : DH * head + DH, :] = query_sum[
+                        head, :, 128 * block : 128 * block + 128].astype(jnp.bfloat16)
+            q_copies = [go(remote(query_out.at[(zpos + step) % 4], grads.at[zpos, pl.ds(2 * WIDE, WIDE)],
+                                  q_send.at[step], q_recv.at[step], along[step - 1])) for step in range(1, 4)]
+            grads[zpos, 2 * WIDE :, :] = query_out[zpos]
+        if 0 <= tick - 1 < 4:
+            reduce_cores(tick - 1)
+        if 0 <= tick - 2 < 4:
+            reduce_x(tick - 2)
+    for copy in q_copies + back_copies[:3]:
+        copy.wait_recv()
+    for copy in sends:
+        copy.wait_send()
+
+
+def attention_backward(sent, kv, queries, out_heads, lse, tiles):
+    low, f32 = jnp.bfloat16, jnp.float32
+    dma = pltpu.SemaphoreType.DMA
+    return pl.pallas_call(
+        backward_kernel,
+        out_shape=[
+            jax.ShapeDtypeStruct((GROUPS, 3 * WIDE, 128), low),
+            jax.ShapeDtypeStruct((HEADS_HERE, 5, 128, 128), f32),
+        ],
+        in_specs=[pl.BlockSpec(memory_space=pltpu.VMEM)] * 6,
+        out_specs=[pl.BlockSpec(memory_space=pltpu.VMEM)] * 2,
+        scratch_shapes=[
+            pltpu.VMEM((HEADS_HERE, DH + MARKS, QUERIES), low),
+            pltpu.VMEM((4, WIDE, 128), low),
+            pltpu.VMEM((512, QUERIES), low),
+            pltpu.VMEM((512, QUERIES), low),
+            pltpu.VMEM((HEADS_HERE, 1, QUERIES), f32),
+            pltpu.VMEM((HEADS_HERE, DH, QUERIES), f32),
+            pltpu.VMEM((4, 4, 2 * WIDE, 128), f32),
+            pltpu.VMEM((4, 2, 2 * WIDE, 128), low),
+            pltpu.VMEM((4, 2, 2 * WIDE, 128), low),
+            pltpu.VMEM((4, 2 * WIDE, 128), low),
+            pltpu.VMEM((4, 2 * WIDE, 128), low),
+            pltpu.VMEM((3, 2 * WIDE, 128), low),
+            pltpu.VMEM((4, WIDE, 128), low),
+        ] + [dma((4,))] * 10,
+        compiler_params=pltpu.CompilerParams(collective_id=1, has_side_effects=True, vmem_limit_bytes=48 * 2**20),
+        name="attention_backward",
+    )(sent, kv, queries, out_heads, lse, tiles)
+
+
+def offset_profile(bias_table):
+    offsets = 256 - jnp.arange(512, dtype=jnp.int32)
+    hot = (bucket_of(offsets)[:, None] == jnp.arange(NB, dtype=jnp.int32)[None, :])
+    per_offset = jnp.dot(bias_table.T, hot.T.astype(jnp.bfloat16), preferred_element_type=jnp.float32)
+    first = HEADS_HERE * (lax.axis_index("seq") // 4)
+    return lax.dynamic_slice_in_dim(per_offset, first, HEADS_HERE, 0), hot
+
+
+def table_gradient(tile_grads, hot):
+    sums = tile_sums(tile_grads)
+    near = jnp.dot(sums[:, 0, :], hot.astype(jnp.float32), precision=lax.Precision.HIGHEST)
+    left = jnp.sum(sums[:, 1, :128], axis=1)
+    right = jnp.sum(sums[:, 1, 128:256], axis=1)
+    near = near.at[:, 15].add(left).at[:, 31].add(right)
+    first = HEADS_HERE * (lax.axis_index("seq") // 4)
+    return lax.dynamic_update_slice(jnp.zeros((NB, H), jnp.float32), near.T, (0, first))
+
+
+def fast_device(
+    hidden_in, segments, cotangent, w_query, w_key, w_value, w_out, w_gate, w_up, w_down, bias_table, gain_attn, gain_ffn
+):
+    low, f32 = jnp.bfloat16, jnp.float32
+    row_in = hidden_in[0].astype(f32)
+    seg_own = segments[0]
+    tok_count = row_in.shape[0]
+    is_valid = (seg_own >= 0)[:, None]
+    norm_first, norm_back_first = jax.vjp(rms_scale, row_in, gain_attn.astype(f32))
+    normed_attn = norm_first.astype(low)
+    projected = [jnp.dot(normed_attn, weight, preferred_element_type=f32).astype(low)
+                 for weight in (w_key, w_value, w_query)]
+    keys_t, values_t, queries_t = [part.T.reshape(GROUPS, WIDE, tok_count) for part in projected]
+    marks = (seg_own[None, :] + 1 == jnp.arange(MARKS, dtype=jnp.int32)[:, None]).astype(low)
+    sent = jnp.concatenate(
+        [keys_t, values_t, jnp.broadcast_to(marks[None], (GROUPS, MARKS, tok_count)), queries_t], axis=1)
+    profile, hot = offset_profile(bias_table)
+    tiles = bias_tiles(profile)
+    context_t, kv, queries, out_heads, lse = attention_forward(sent, tiles)
+    context_t = context_t.reshape(D, tok_count)
+    context_low = context_t.T
+    middle = row_in + jnp.dot(context_low, w_out, preferred_element_type=f32)
+    norm_second, norm_back_second = jax.vjp(rms_scale, middle, gain_ffn.astype(f32))
+    normed_ffn = norm_second.astype(low)
+    gate_pre = jnp.dot(normed_ffn, w_gate, preferred_element_type=f32)
+    upward = jnp.dot(normed_ffn, w_up, preferred_element_type=f32)
+    gelu_out, gelu_back = jax.vjp(gelu_tanh, gate_pre)
+    hidden_act = (gelu_out * upward).astype(low)
+    result = middle + jnp.dot(hidden_act, w_down, preferred_element_type=f32)
+    output = jnp.where(is_valid, result, 0.0).astype(low)[None]
+    grad_result = jnp.where(is_valid, cotangent[0].astype(f32), 0.0)
+    grad_branch = grad_result.astype(low)
+    grad_hidden = jnp.einsum("td,fd->tf", grad_branch, w_down, preferred_element_type=f32)
+    grad_gate = gelu_back(grad_hidden * upward)[0].astype(low)
+    grad_upward = (grad_hidden * gelu_out).astype(low)
+    grad_normed_ffn = jnp.einsum("tf,df->td", grad_gate, w_gate, preferred_element_type=f32) + jnp.einsum(
+        "tf,df->td", grad_upward, w_up, preferred_element_type=f32)
+    grad_mid_part, grad_gain_ffn = norm_back_second(grad_normed_ffn)
+    grad_middle = grad_result + grad_mid_part
+    grad_attn = grad_middle.astype(low)
+    grad_context = jnp.einsum("te,de->td", grad_attn, w_out, preferred_element_type=f32).astype(low)
+    grads_t, tile_grads = attention_backward(
+        grad_context.T.reshape(GROUPS, WIDE, tok_count), kv, queries, out_heads, lse, tiles)
+    grad_tab = table_gradient(tile_grads, hot)
+    grad_k_low, grad_v_low, grad_q_low = [
+        grads_t[:, WIDE * part : WIDE * part + WIDE].reshape(D, tok_count).T for part in range(3)]
+    grad_normed_attn = sum(jnp.einsum("te,de->td", part, weight, preferred_element_type=f32) for part, weight in (
+        (grad_q_low, w_query), (grad_k_low, w_key), (grad_v_low, w_value)))
+    grad_in_part, grad_gain_attn = norm_back_first(grad_normed_attn)
+    grad_input = (grad_middle + grad_in_part).astype(low)[None]
+    small = jnp.stack(
+        [grad_gain_attn, grad_gain_ffn, jnp.pad(grad_tab.reshape(-1), (0, D - NB * H))] + [jnp.zeros((D,), f32)] * 5)
+    *summed_weights, small_sum = weight_gradients(
+        by_quarter(hidden_act.T),
+        by_quarter(normed_ffn.T),
+        jnp.concatenate([by_quarter(normed_attn.T), by_quarter(context_t)], axis=1),
+        grad_branch,
+        jnp.concatenate([grad_gate, grad_upward], axis=1),
+        jnp.concatenate([grad_q_low, grad_k_low, grad_v_low, grad_attn], axis=1),
+        small,
+    )
+    return (output, grad_input, *summed_weights, small_sum[2, : NB * H].reshape(NB, H), small_sum[0], small_sum[1])
+
+
 def solution(mesh):
     in_specs = (
         P("rows", "seq", None),
@@ -383,6 +1086,7 @@
         P(),
         P(),
     )
+    fast = dict(mesh.shape) == {"rows": 2, "seq": 16}
     return jax.shard_map(
-        per_device, mesh=mesh, in_specs=in_specs, out_specs=out_specs, check_vma=False
-    )
+        fast_device if fast else per_device, mesh=mesh, in_specs=in_specs, out_specs=out_specs, check_vma=False
+    )

time: 992 us -> 274 us (0.28)
  waiting for transfers between devices: 504 us -> 0 us
  local copies, waits for them, and re-layouts: 231 us -> 51.4 us
  Pallas kernels: 0 us -> 173 us
  blocking collectives: 98.5 us -> 0 us
  matrix products: 112 us -> 25.9 us
  between operations: 14.9 us -> 1.04 us
    reduce_scatter x7 -> x0, waiting for transfers between devices: 503 us -> none  [the longest x1 121 us: per_device(): lax.psum_scatter(grad_w_up, ('rows', 'seq'), scatter_dimension=0, tiled=T...]
    pallas_call x0 -> x5, Pallas kernels: none -> 173 us  [the longest x1 99.4 us: weight_gradients(): pl.pallas_call(weight_kernel, out_shape=outs, in_specs=[pl.BlockSpec(memo...]
    reshape x4 -> x6, local copies, waits for them, and re-layouts: 100 us -> 5.72 us  [the longest x3 4.31 us: fast_device(): grads_t[:, WIDE * part:WIDE * part + WIDE].reshape(D, tok_count)]
    dot_general x31 -> x16, matrix products: 112 us -> 25.9 us  [the longest x3 7.09 us: fast_device(): jnp.dot(normed_attn, weight, preferred_element_type=f32).astype(low)]
    all_gather x3 -> x0, blocking collectives: 61.3 us -> none  [the longest x1 23 us: per_device(): seg_all = lax.all_gather(seg_own, 'seq', axis=0, tiled=True)]
    another operation x4 -> x8, local copies, waits for them, and re-layouts: 47.6 us -> 3.63 us  [the longest x4 1.9 us: fast_device(): jnp.stack([grad_gain_attn, grad_gain_ffn, jnp.pad(grad_tab.reshape(-1), (...]
    psum x1 -> x0, blocking collectives: 37.2 us -> none  [per_device(): lax.psum((grad_tab, grad_gain_attn, grad_gain_ffn), ('rows', 'seq'))]
    pad x2 -> x1, local copies, waits for them, and re-layouts: 24.3 us -> 0.01 us  [fast_device(): jnp.pad(grad_tab.reshape(-1), (0, D - NB * H))]
  transfers between devices with their start and end apart: 11 -> 0, of which waited for: 5 -> 0; matrix products, arithmetic and copies ran while one was open for 36% -> 0% of each run, Pallas kernels for 0% -> 0%
where the time goes in v2:
time: 274 us; the launch traced here: 271 us
  Pallas kernels  173 us (63%)
  local copies, waits for them, and re-layouts  51.4 us (19%)
  matrix products  25.9 us (9%)
  other arithmetic  19.9 us (7%)
    pallas_call x1, Pallas kernels, weight_gradients(): pl.pallas_call(weight_kernel, out_shape=outs, in_specs=[pl.BlockSpec(memo...  99.4 us
    pallas_call x1, Pallas kernels, attention_forward(): pl.pallas_call(forward_kernel, out_shape=[jax.ShapeDtypeStruct((GROUPS, W...  35.8 us
    pallas_call x1, Pallas kernels, attention_backward(): pl.pallas_call(backward_kernel, out_shape=[jax.ShapeDtypeStruct((GROUPS,...  32.3 us
    unnamed x94, local copies, waits for them, and re-layouts  22.7 us
    dot_general x3, matrix products, fast_device(): jnp.dot(normed_attn, weight, preferred_element_type=f32).astype(low)  7.09 us

profile of v2, /device:TPU:0, one launch (start us, length us, event | category | flops | bytes accessed | tf_op | source)
XLA Modules:
  0.0 271.3 jit_solution(3090143218010044532)
XLA Ops:
  7.6 1.7 fusion.32.rhs_down
  9.3 2.4 fusion.5
  12.9 2.3 fusion.4
  15.2 1.7 copy.40
  17.0 2.3 fusion.3
  19.3 1.7 copy.39
  21.0 1.9 pad_maximum_fusion.2.sent
  22.9 1.9 bias_tiles.1.tiles
  27.1 35.8 %attention_forward.1 = (bf16[4,192,128]{2,1,0:T(8,128)(2,1)S(1)}, bf16[16,400,128]{2,1,0:T(8,128)(2,1)S(1)}, bf16[4,192,128]{2,1,0:T(8,128)(2,1)S(1)}, f32[3,64,512]{2,1,0:T(8,128)S(1)}, f32[3,1,512]{2,1,0:T(1,128)S(1)}) custom-call(bf16[4,592,128]{2,1,0:T(8,128)(2,1)S(1)} %copy-done.3, f32[3,5,128,128]{3,2,1,0:T(8,128)S(1)} %copy-done.1), custom_call_target="tpu_custom_call" | custom-call | tf_op jit(solution)/shard_map/attention_forward/pallas_call | solution.py:809
  69.2 2.7 fusion.64
  72.0 2.1 fusion.22
  74.1 2.1 copy.43
  76.1 1.9 copy.44
  78.0 4.2 %fusion.2 = bf16[1,128,768]{2,1,0:T(8,128)(2,1)} fusion(f32[128,768]{1,0:T(8,128)} %copy-done.9, bf16[2048,768]{1,0:T(8,128)(2,1)} %param.26, f32[128,2048]{1,0:T(8,128)} %get-tuple-element.112, f32[128,2048]{1,0:T(8,128)} %copy-done.15, pred[128]{0:T(512)(128)(4,1)S(1)} %copy-done.37), kind=kOutput, calls=%fused_computation.14 | convolution fusion | flops 405569536 | bytes 5832832 | tf_op jit(solution)/shard_map/dot_general | solution.py:1023
  95.9 32.3 %attention_backward.1 = (bf16[4,576,128]{2,1,0:T(8,128)(2,1)S(1)}, f32[3,5,128,128]{3,2,1,0:T(8,128)S(1)}) custom-call(bf16[4,192,128]{2,1,0:T(8,128)(2,1)S(1)} %bitcast.104, bf16[16,400,128]{2,1,0:T(8,128)(2,1)S(1)} %copy-done.5, bf16[4,192,128]{2,1,0:T(8,128)(2,1)S(1)} %get-tuple-element.53.queries, f32[3,64,512]{2,1,0:T(8,128)S(1)} %copy-done.8, ...), custom_call_target="tpu_custom_call" | custom-call | tf_op jit(solution)/shard_map/attention_backward/pallas_call | solution.py:949
  130.0 3.5 %tile_sums.1 = f32[3,8,512]{2,1,0:T(8,128)} custom-call(f32[3,5,128,128]{3,2,1,0:T(8,128)} %copy-done.6), custom_call_target="tpu_custom_call" | custom-call | tf_op jit(solution)/shard_map/tile_sums/pallas_call | solution.py:671
  141.9 1.8 copy.51
  144.4 1.7 copy.50
  146.2 2.2 pad_maximum_fusion.1.rhs_attn
  151.0 1.8 fusion.26
  154.9 2.0 fusion.57
  157.1 1.7 pad_maximum_fusion.3.lhs_attn
  158.8 99.4 %weight_gradients.1 = (f32[24,768]{1,0:T(8,128)}, f32[24,768]{1,0:T(8,128)}, f32[24,768]{1,0:T(8,128)}, f32[24,768]{1,0:T(8,128)}, f32[24,2048]{1,0:T(8,128)}, /...) custom-call(bf16[4,512,128]{2,1,0:T(8,128)(2,1)} %bitcast.106, bf16[4,192,128]{2,1,0:T(8,128)(2,1)} %bitcast.113, ...), custom_call_target="tpu_custom_call" | custom-call | tf_op jit(solution)/shard_map/weight_gradients/pallas_call | solution.py:603
  269.0 1.6 copy.77
  (150 shorter events, 57.3 us)
Async XLA Ops:
  0.6 71.3 %copy-start = (bf16[768,2048]{1,0:T(8,128)(2,1)S(1)}, bf16[768,2048]{1,0:T(8,128)(2,1)}, u32[]{:S(2)}) copy-start(bf16[768,2048]{1,0:T(8,128)(2,1)} %param.25) | copy-start | bytes 9437188
  2.3 10.6 %copy-start.36 = (pred[128]{0:T(512)(128)(4,1)}, pred[128]{0:T(512)(128)(4,1)S(1)}, u32[]{:S(2)}) copy-start(pred[128]{0:T(512)(128)(4,1)S(1)} %compare_bitcast_fusion) | copy-start | bytes 388
  3.3 13.6 %copy-start.31 = (f32[128]{0:T(128)}, f32[128]{0:T(128)S(1)}, u32[]{:S(2)}) copy-start(f32[128]{0:T(128)S(1)} %fusion.51) | copy-start | bytes 1540
  4.0 3.6 %copy-start.38 = (s32[512]{0:T(512)}, s32[512]{0:T(512)S(1)}, u32[]{:S(2)}) copy-start(s32[512]{0:T(512)S(1)} %fusion.41) | copy-start | bytes 6148
  6.0 6.9 %copy-start.13 = (bf16[1,128,768]{2,1,0:T(8,128)(2,1)S(1)}, bf16[1,128,768]{2,1,0:T(8,128)(2,1)}, u32[]{:S(2)}) copy-start(bf16[1,128,768]{2,1,0:T(8,128)(2,1)} %param.17) | copy-start | bytes 589828
  27.1 37.8 %copy-start.17 = (bf16[768,768]{1,0:T(8,128)(2,1)S(1)}, bf16[768,768]{1,0:T(8,128)(2,1)}, u32[]{:S(2)}) copy-start(bf16[768,768]{1,0:T(8,128)(2,1)} %param.23) | copy-start | bytes 3538948
  69.2 2.7 %copy-start.10 = (f32[128,768]{1,0:T(8,128)S(1)}, f32[128,768]{1,0:T(8,128)}, u32[]{:S(2)}) copy-start(f32[128,768]{1,0:T(8,128)} %copy-done.9) | copy-start | bytes 1179652
  69.2 2.7 %copy-start.34 = (f32[128]{0:T(128)S(1)}, f32[128]{0:T(128)}, u32[]{:S(2)}) copy-start(f32[128]{0:T(128)} %copy-done.33) | copy-start | bytes 1540
  72.0 2.1 copy-start.15
  74.1 4.0 %copy-start.37 = (pred[128]{0:T(512)(128)(4,1)S(1)}, pred[128]{0:T(512)(128)(4,1)}, u32[]{:S(2)}) copy-start(pred[128]{0:T(512)(128)(4,1)} %copy-done.36) | copy-start | bytes 388
  78.0 4.2 %copy-start.16 = (f32[128,2048]{1,0:T(8,128)S(1)}, f32[128,2048]{1,0:T(8,128)}, u32[]{:S(2)}) copy-start(f32[128,2048]{1,0:T(8,128)} %copy-done.15) | copy-start | bytes 3145732
  78.0 4.2 %copy-start.22 = (f32[128,2048]{1,0:T(8,128)S(1)}, f32[128,2048]{1,0:T(8,128)}, u32[]{:S(2)}) copy-start(f32[128,2048]{1,0:T(8,128)} %get-tuple-element.112) | copy-start | bytes 3145732
  78.0 4.2 %copy-start.23 = (bf16[2048,768]{1,0:T(8,128)(2,1)S(1)}, bf16[2048,768]{1,0:T(8,128)(2,1)}, u32[]{:S(2)}) copy-start(bf16[2048,768]{1,0:T(8,128)(2,1)} %param.26) | copy-start | bytes 9437188
  78.0 4.2 %copy-start.29 = (bf16[128,768]{1,0:T(8,128)(2,1)S(1)}, bf16[128,768]{1,0:T(8,128)(2,1)}, u32[]{:S(2)}) copy-start(bf16[128,768]{1,0:T(8,128)(2,1)} %fusion.32.rhs_down) | copy-start | bytes 589828
  82.2 1.9 copy-start.12
  86.7 1.7 copy-start.42
  86.7 1.7 copy-start.28
  87.7 2.2 copy-start.18
  129.2 6.4 %copy-start.39 = (s32[512]{0:T(512)S(1)}, s32[512]{0:T(512)}, u32[]{:S(2)}) copy-start(s32[512]{0:T(512)} %copy-done.38) | copy-start | bytes 6148
  130.0 16.2 %copy-start.25 = (bf16[128,768]{1,0:T(8,128)(2,1)S(1)}, bf16[128,768]{1,0:T(8,128)(2,1)}, u32[]{:S(2)}) copy-start(bf16[128,768]{1,0:T(8,128)(2,1)} %copy-done.24) | copy-start | bytes 589828
  146.2 2.2 copy-start.19
  146.2 2.2 copy-start.27
  151.0 1.9 copy-start.35
  258.3 12.3 %copy-start.30 = (f32[64,768]{1,0:T(8,128)S(1)}, f32[64,768]{1,0:T(8,128)}, u32[]{:S(2)}) copy-start(f32[64,768]{1,0:T(8,128)} %get-tuple-element.133) | copy-start | bytes 589828
  (19 other events, 20.1 us)

commit v3 on v0

--- a/solution.py
+++ b/solution.py
@@ -1,14 +1,19 @@
+import functools
 import math
+from types import SimpleNamespace
 
 import jax
 import jax.numpy as jnp
 from jax import lax
+from jax.experimental import pallas as pl
+from jax.experimental.pallas import tpu as pltpu
 from jax.sharding import PartitionSpec as P
 
 D = 768
 H = 12
 DH = 64
 NB = 32
+FF = 2048
 
 
 BORDERS = (12, 16, 23, 32, 46, 64, 91)
@@ -353,6 +358,796 @@
     )
 
 
+MESH = pl.DeviceIdType.MESH
+GROUPS = 4
+HEADS_HERE = H // GROUPS
+WIDE = HEADS_HERE * DH
+MARKS = 16
+KV_ROWS = 2 * WIDE + MARKS
+SENT_ROWS = KV_ROWS + WIDE
+TOK = 128
+QUERIES = 512
+CUT = 4
+CUT_COLS = FF // CUT
+OWN = D // 32
+OWN_DOWN = FF // 32
+SEPARATE = -1e30
+GELU_SLOPE = 0.7978845608
+GELU_CUBE = 0.044715
+F32 = jnp.float32
+LOW = jnp.bfloat16
+
+
+def place():
+    row = lax.axis_index("rows")
+    spot = lax.axis_index("seq")
+    return row, spot // 4, (spot // 2) % 2, spot % 2
+
+
+def device(row, zpos, xpos, core):
+    return (row, 4 * zpos + 2 * xpos + core)
+
+
+def flip(bit):
+    return 1 - bit
+
+
+def near_z(zpos):
+    return zpos + 1 - 2 * (zpos % 2)
+
+
+def far_z(zpos):
+    return (zpos + 2) % 4
+
+
+def flat_block(zpos, column):
+    return 4 * zpos + column
+
+
+def bias_slot(key_spot, block, column):
+    return jnp.clip(key_spot - flat_block(block, column), -2, 2) + 2
+
+
+def span(index, size):
+    return pl.ds(pl.multiple_of(index * size, size), size)
+
+
+def head_rows(head, first=0):
+    return pl.ds(pl.multiple_of(first + DH * head, DH), DH)
+
+
+def remote(src, dst, send_sem, recv_sem, peer):
+    return pltpu.make_async_remote_copy(
+        src_ref=src, dst_ref=dst, send_sem=send_sem, recv_sem=recv_sem, device_id=peer, device_id_type=MESH
+    )
+
+
+def dot(left, right, left_dim=1, right_dim=0):
+    return lax.dot_general(left, right, (((left_dim,), (right_dim,)), ((), ())), preferred_element_type=F32)
+
+
+def rms(values):
+    return lax.rsqrt(jnp.mean(values * values, axis=-1, keepdims=True) + EPSILON)
+
+
+def rms_back(values, scale, gain, grad):
+    grad_gain = jnp.sum(grad * values * scale, axis=0, keepdims=True)
+    inner = grad * gain
+    mean = jnp.mean(inner * values, axis=-1, keepdims=True)
+    return scale * inner - values * (scale * scale * scale * mean), grad_gain
+
+
+def gelu_and_slope(values):
+    square = values * values
+    bent = jnp.tanh(GELU_SLOPE * values * (1.0 + GELU_CUBE * square))
+    half = 0.5 * (1.0 + bent)
+    slope = half + 0.5 * values * (1.0 - bent * bent) * (GELU_SLOPE * (1.0 + 3.0 * GELU_CUBE * square))
+    return values * half, slope
+
+
+def layer_kernel(names, *refs):
+    s = SimpleNamespace(**dict(zip(names, refs)))
+    row, zpos, xpos, core = place()
+    column = 2 * xpos + core
+    beside_column = 2 * flip(xpos) + core
+    mate = device(row, zpos, xpos, flip(core))
+    beside = device(row, zpos, flip(xpos), core)
+    across = device(flip(row), zpos, xpos, core)
+    slant = device(flip(row), zpos, xpos, flip(core))
+    near = device(row, near_z(zpos), xpos, core)
+    far = device(row, far_z(zpos), xpos, core)
+    along = [device(row, (zpos + step) % 4, xpos, core) for step in range(1, 4)]
+    mine = 2 * row + core
+    parts = (2 * flip(row) + core, 2 * flip(row) + flip(core), 2 * row + flip(core))
+    here = flat_block(zpos, column)
+    peers = [mate, beside, across, slant] + along
+    barrier = pltpu.get_barrier_semaphore()
+    for peer in peers:
+        pl.semaphore_signal(barrier, inc=1, device_id=peer, device_id_type=MESH)
+
+    sends = []
+
+    def go(copy):
+        copy.start()
+        sends.append(copy)
+        return copy
+
+    def load(index):
+        name = ("w_key", "w_value", "w_query", "w_out", "w_gate", "w_up", "w_down")[index]
+        return pltpu.make_async_copy(getattr(s, name), getattr(s, "v" + name), s.load_sem.at[index])
+
+    loads = [load(index) for index in range(7)]
+    for index in range(3):
+        loads[index].start()
+
+    row_in = s.hidden[...].astype(F32)
+    scale_first = rms(row_in)
+    gain_first = s.gain_attn[...].astype(F32)
+    gain_second = s.gain_ffn[...].astype(F32)
+    normed = (row_in * scale_first * gain_first).astype(LOW)
+    seg_row = s.segments[...]
+    marks = (seg_row + 1 == lax.broadcasted_iota(jnp.int32, (MARKS, TOK), 0)).astype(F32).astype(LOW)
+
+    def project(index, weight, first):
+        loads[index].wait()
+        turned = dot(normed, weight[...]).astype(LOW).T
+        for group in range(GROUPS):
+            s.sent[group, first : first + WIDE, :] = turned[WIDE * group : WIDE * group + WIDE]
+
+    project(0, s.vw_key, 0)
+    project(1, s.vw_value, WIDE)
+    for group in range(GROUPS):
+        s.sent[group, 2 * WIDE : KV_ROWS, :] = marks
+    pl.semaphore_wait(barrier, len(peers))
+    kv_part, q_part = pl.ds(0, KV_ROWS), pl.ds(KV_ROWS, WIDE)
+    x_copies, c_copies, on_copies = [None] * 4, [None] * 4, [None] * 4
+    z_copies = [go(remote(s.sent.at[(zpos + step) % 4, kv_part], s.kv.at[here], s.z_send.at[step], s.z_recv.at[step],
+                          along[step - 1])) for step in range(1, 4)]
+    x_copies[0] = go(remote(s.sent.at[zpos, kv_part], s.kv.at[here], s.x_send.at[0], s.x_recv.at[0], beside))
+    c_copies[0] = go(remote(s.sent.at[zpos, kv_part], s.kv.at[here], s.c_send.at[0], s.c_recv.at[0], mate))
+    project(2, s.vw_query, KV_ROWS)
+    q_copies = [go(remote(s.sent.at[(zpos + step) % 4, q_part], s.queries.at[zpos], s.q_send.at[step],
+                          s.q_recv.at[step], along[step - 1])) for step in range(1, 4)]
+    for index in range(3, 7):
+        loads[index].start()
+    s.kv[here] = s.sent[zpos, :KV_ROWS, :]
+    s.queries[zpos] = s.sent[zpos, KV_ROWS:, :]
+
+    offsets = 256 - lax.broadcasted_iota(jnp.int32, (NB, QUERIES), 1)
+    hot = (bucket_of(offsets) == lax.broadcasted_iota(jnp.int32, (NB, QUERIES), 0)).astype(F32)
+    profile = dot(s.table[...], hot.astype(LOW), 0, 0)
+    for head in range(H):
+        s.profile[head] = profile[head : head + 1]
+    for head in range(HEADS_HERE):
+        line = s.profile[HEADS_HERE * zpos + head]
+        rolled = pltpu.roll(jnp.broadcast_to(line, (TOK, QUERIES)), 0, 1, stride=1, stride_axis=0)
+        for slot, first in ((1, 384), (2, 256), (3, 128)):
+            s.tiles[head, slot] = rolled[:, first : first + 128]
+        for slot, at in ((0, 511), (4, 1)):
+            s.tiles[head, slot] = jnp.broadcast_to(line[:, at : at + 1], (TOK, TOK))
+
+    def pass_on(step):
+        spot = s.kv.at[flat_block((zpos + 4 - step) % 4, beside_column)]
+        x_copies[step].wait_recv()
+        on_copies[step] = go(remote(spot, spot, s.c_send.at[4 + step], s.c_recv.at[4 + step], mate))
+
+    def relay(step):
+        z_copies[step - 1].wait_recv()
+        spot = s.kv.at[flat_block((zpos + 4 - step) % 4, column)]
+        x_copies[step] = go(remote(spot, spot, s.x_send.at[step], s.x_recv.at[step], beside))
+        c_copies[step] = go(remote(spot, spot, s.c_send.at[step], s.c_recv.at[step], mate))
+
+    seg_column = jnp.broadcast_to(seg_row.astype(F32), (TOK, TOK)).T
+    valid = seg_column[:, 0:1] >= 0
+    grad_result = jnp.where(valid, s.cotangent[...].astype(F32), 0.0)
+    grad_branch = grad_result.astype(LOW)
+
+    right_copies, left_copies, onward = {}, {}, {}
+
+    def share_right(index, buffer, value):
+        spot = buffer.at[span(mine, TOK)]
+        buffer[span(mine, TOK), :] = value
+        right_copies[index] = (
+            go(remote(spot, spot, s.right_send.at[index, 0], s.right_recv.at[index, 0], across)),
+            go(remote(spot, spot, s.right_send.at[index, 1], s.right_recv.at[index, 1], mate)),
+        )
+
+    def pass_right(index, buffer):
+        right_copies[index][0].wait_recv()
+        spot = buffer.at[span(parts[0], TOK)]
+        onward[index] = go(remote(spot, spot, s.right_send.at[index, 2], s.right_recv.at[index, 2], mate))
+
+    def take_right(index):
+        right_copies[index][1].wait_recv()
+        onward[index].wait_recv()
+
+    def share_left(index, staged, buffer):
+        lanes = span(mine, TOK)
+        buffer[:, lanes] = staged[mine]
+        left_copies[index] = [
+            go(remote(staged.at[part], buffer.at[:, lanes], s.left_send.at[index, slot], s.left_recv.at[index, slot], peer))
+            for slot, (peer, part) in enumerate(zip((across, slant, mate), parts))
+        ]
+
+    def take_left(index):
+        for copy in left_copies[index]:
+            copy.wait_recv()
+
+    def stage_quarters(staged, turned, height):
+        for part in range(4):
+            for x_half in range(2):
+                blocks = []
+                for z_at in range(4):
+                    first = height * (16 * (part // 2) + 4 * z_at + 2 * x_half + part % 2)
+                    blocks.append(turned[first : first + height])
+                staged[part, 4 * height * x_half : 4 * height * (x_half + 1), :] = jnp.concatenate(
+                    blocks, axis=0).astype(LOW)
+
+    share_right(0, s.right_down, grad_branch)
+    relay(1)
+    pass_on(0)
+    pass_right(0, s.right_down)
+    relay(2)
+    pass_on(1)
+    turned = normed.astype(F32).T
+    order = [16 * r + 4 * z + 2 * x + c for c in range(2) for x in range(2) for r in range(2) for z in range(4)]
+    s.normed_all[:, span(zpos, TOK)] = jnp.concatenate(
+        [turned[OWN * at : OWN * at + OWN] for at in order], axis=0).astype(LOW)
+    relay(3)
+    pass_on(2)
+    for copy in q_copies:
+        copy.wait_recv()
+    n_copies = [go(remote(s.normed_all.at[:, span(zpos, TOK)], s.normed_all.at[:, span(zpos, TOK)],
+                          s.n_send.at[step], s.n_recv.at[step], along[step - 1])) for step in range(1, 4)]
+
+    for block in range(4):
+        lanes = slice(TOK * block, TOK * block + TOK)
+        apart = ((1.0 - s.kv[flat_block(block, column), 2 * WIDE :, :].astype(F32)) * SEPARATE).astype(LOW)
+        for head in range(HEADS_HERE):
+            s.marked[head, :DH, lanes] = s.queries[block, DH * head : DH * head + DH, :]
+            s.marked[head, DH:, lanes] = apart
+    s.highest[...] = jnp.full_like(s.highest, -1e38)
+    s.totals[...] = jnp.zeros_like(s.totals)
+    s.summed[...] = jnp.zeros_like(s.summed)
+
+    def block_scores(head, key_spot):
+        keys = jnp.concatenate([s.kv[key_spot, head_rows(head), :], s.kv[key_spot, 2 * WIDE :, :]], axis=0)
+        bias = [s.tiles[head, bias_slot(key_spot, block, column)] for block in range(4)]
+        return dot(keys, s.marked[head], 0, 0) + jnp.concatenate(bias, axis=1)
+
+    def wide_rows(rows, chunk):
+        return jnp.concatenate([s.kv[flat_block(chunk, spot), rows, :] for spot in range(4)], axis=1)
+
+    def attend(step):
+        chunk = (zpos + 4 - step) % 4
+        c_copies[step].wait_recv()
+        on_copies[step].wait_recv()
+
+        def one_head(head, carry):
+            newest = s.highest[head]
+            for spot in range(4):
+                scores = block_scores(head, flat_block(chunk, spot))
+                s.score_buf[spot] = scores
+                newest = jnp.maximum(newest, jnp.max(scores, axis=0, keepdims=True))
+            rescale = jnp.exp(s.highest[head] - newest)
+            total = s.totals[head] * rescale
+            for spot in range(4):
+                weights = jnp.exp(s.score_buf[spot] - newest)
+                total = total + jnp.sum(weights, axis=0, keepdims=True)
+                s.weight_buf[TOK * spot : TOK * spot + TOK, :] = weights.astype(LOW)
+            s.highest[head] = newest
+            s.totals[head] = total
+            values = wide_rows(head_rows(head, WIDE), chunk)
+            s.summed[head] = s.summed[head] * rescale + dot(values, s.weight_buf[...])
+            return carry
+
+        lax.fori_loop(0, HEADS_HERE, one_head, 0)
+
+    for step in range(4):
+        attend(step)
+        if step == 0:
+            pass_on(3)
+    for head in range(HEADS_HERE):
+        done = s.summed[head] / s.totals[head]
+        s.summed[head] = done
+        s.lse[head] = s.highest[head] + jnp.log(s.totals[head])
+        low = done.astype(LOW)
+        for block in range(4):
+            s.context_out[block, DH * head : DH * head + DH, :] = low[:, TOK * block : TOK * block + TOK]
+    o_copies = [go(remote(s.context_out.at[(zpos + step) % 4], s.context.at[zpos], s.o_send.at[step], s.o_recv.at[step],
+                          along[step - 1])) for step in range(1, 4)]
+    s.context[zpos] = s.context_out[zpos]
+
+    loads[6].wait()
+    for cut in range(CUT):
+        s.grad_hidden[cut] = dot(grad_branch, s.vw_down[CUT_COLS * cut : CUT_COLS * cut + CUT_COLS, :], 1, 1)
+    for index in range(3, 6):
+        loads[index].wait()
+    for copy in o_copies:
+        copy.wait_recv()
+
+    context_t = jnp.concatenate([s.context[group] for group in range(GROUPS)], axis=0)
+    middle = row_in + dot(context_t, s.vw_out[...], 0, 0)
+    scale_second = rms(middle)
+    normed_ffn = (middle * scale_second * gain_second).astype(LOW)
+    stage_quarters(s.left_gate, normed_ffn.astype(F32).T, OWN)
+    share_left(1, s.left_gate, s.all_left_gate)
+    grad_normed = jnp.zeros((TOK, D), F32)
+    for cut in range(CUT):
+        cols = slice(CUT_COLS * cut, CUT_COLS * cut + CUT_COLS)
+        gelu, slope = gelu_and_slope(dot(normed_ffn, s.vw_gate[:, cols]))
+        upward = dot(normed_ffn, s.vw_up[:, cols])
+        grad_hidden = s.grad_hidden[cut]
+        s.hidden_act[:, cols] = (gelu * upward).astype(LOW)
+        grad_gate = (grad_hidden * upward * slope).astype(LOW)
+        grad_upward = (grad_hidden * gelu).astype(LOW)
+        share_right(1 + cut, s.right_gate.at[cut], jnp.concatenate([grad_gate, grad_upward], axis=1))
+        grad_normed = grad_normed + dot(grad_gate, s.vw_gate[:, cols], 1, 1) + dot(grad_upward, s.vw_up[:, cols], 1, 1)
+    grad_mid_part, grad_gain_ffn = rms_back(middle, scale_second, gain_second, grad_normed)
+    grad_middle = grad_result + grad_mid_part
+    grad_attn = grad_middle.astype(LOW)
+    grad_context = dot(s.vw_out[...], grad_attn, 1, 1).astype(LOW)
+    for group in range(GROUPS):
+        s.d_out[group] = grad_context[WIDE * group : WIDE * group + WIDE]
+    d_copies = [go(remote(s.d_out.at[(zpos + step) % 4], s.cotangents.at[zpos], s.d_send.at[step], s.d_recv.at[step],
+                          along[step - 1])) for step in range(1, 4)]
+    s.cotangents[zpos] = s.d_out[zpos]
+    s.grad_middle[...] = grad_middle
+    s.small_out[0] = jnp.zeros((8, D), F32)
+    s.small_out[0, 1:2, :] = grad_gain_ffn
+    share_right(5, s.right_out, grad_attn)
+    stage_quarters(s.left_down, s.hidden_act[...].T, OWN_DOWN)
+    share_left(0, s.left_down, s.all_left_down)
+    stage_quarters(s.left_out, context_t.astype(F32), OWN)
+    share_left(2, s.left_out, s.all_left_out)
+    result = middle + dot(s.hidden_act[...], s.vw_down[...])
+    s.output[...] = jnp.where(valid, result, 0.0).astype(LOW)
+    s.tile_grads[...] = jnp.zeros_like(s.tile_grads)
+    s.query_sum[...] = jnp.zeros_like(s.query_sum)
+
+    def wide_cotangent(head):
+        return jnp.concatenate([s.cotangents[block, head_rows(head), :] for block in range(4)], axis=1)
+
+    def chunk_of(step):
+        return (zpos + 1 + step) % 4
+
+    core_copies, xg_copies, back_copies, started = {}, {}, {}, {}
+
+    def begin_backward():
+        for copy in d_copies:
+            copy.wait_recv()
+        for head in range(HEADS_HERE):
+            s.deltas[head] = jnp.sum(wide_cotangent(head).astype(F32) * s.summed[head], axis=0, keepdims=True)
+
+    def differentiate(step):
+        chunk = chunk_of(step)
+
+        def one_head(head, carry):
+            cotangent = wide_cotangent(head)
+            for spot in range(4):
+                key_spot = flat_block(chunk, spot)
+                probs = jnp.exp(block_scores(head, key_spot) - s.lse[head])
+                grad_probs = dot(s.kv[key_spot, head_rows(head, WIDE), :], cotangent, 0, 0)
+                grad_scores = probs * (grad_probs - s.deltas[head])
+                for block in range(4):
+                    slot = bias_slot(key_spot, block, column)
+                    s.tile_grads[head, slot] = s.tile_grads[head, slot] + grad_scores[:, TOK * block : TOK * block + TOK]
+                s.weight_buf[TOK * spot : TOK * spot + TOK, :] = probs.astype(LOW)
+                s.grad_buf[TOK * spot : TOK * spot + TOK, :] = grad_scores.astype(LOW)
+            keys = wide_rows(head_rows(head), chunk)
+            s.query_sum[head] = s.query_sum[head] + dot(keys, s.grad_buf[...])
+            grad_keys = dot(s.marked[head, :DH, :], s.grad_buf[...], 1, 1)
+            grad_values = dot(cotangent, s.weight_buf[...], 1, 1)
+            for spot in range(4):
+                lanes = slice(TOK * spot, TOK * spot + TOK)
+                s.key_sum[step, spot, head_rows(head), :] = grad_keys[:, lanes]
+                s.key_sum[step, spot, head_rows(head, WIDE), :] = grad_values[:, lanes]
+            return carry
+
+        lax.fori_loop(0, HEADS_HERE, one_head, 0)
+        for x_half in range(2):
+            s.core_out[step, x_half] = s.key_sum[step, 2 * x_half + flip(core)].astype(LOW)
+        core_copies[step] = go(remote(s.core_out.at[step], s.core_in.at[step], s.cg_send.at[step], s.cg_recv.at[step], mate))
+
+    def reduce_cores(step):
+        core_copies[step].wait_recv()
+        s.x_out[step] = (s.key_sum[step, beside_column] + s.core_in[step, flip(xpos)].astype(F32)).astype(LOW)
+        xg_copies[step] = go(remote(s.x_out.at[step], s.x_in.at[step], s.xg_send.at[step], s.xg_recv.at[step], beside))
+
+    def reduce_x(step):
+        xg_copies[step].wait_recv()
+        total = s.key_sum[step, column] + s.core_in[step, xpos].astype(F32) + s.x_in[step].astype(F32)
+        low = total.astype(LOW)
+        s.column_grads[: 2 * WIDE, span(chunk_of(step), TOK)] = low
+        if step < 3:
+            s.back_out[step] = low
+            back_copies[step] = go(remote(s.back_out.at[step], s.grads.at[zpos, pl.ds(0, 2 * WIDE)], s.b_send.at[step],
+                                          s.b_recv.at[step], along[step]))
+        else:
+            s.grads[zpos, : 2 * WIDE, :] = low
+
+    def finish_queries():
+        for head in range(HEADS_HERE):
+            low = s.query_sum[head].astype(LOW)
+            s.column_grads[2 * WIDE + DH * head : 2 * WIDE + DH * head + DH, :] = low
+            for block in range(4):
+                s.query_out[block, DH * head : DH * head + DH, :] = low[:, TOK * block : TOK * block + TOK]
+        for step in range(1, 4):
+            back_copies["query", step] = go(remote(
+                s.query_out.at[(zpos + step) % 4], s.grads.at[zpos, pl.ds(2 * WIDE, WIDE)], s.qb_send.at[step],
+                s.qb_recv.at[step], along[step - 1]))
+        s.grads[zpos, 2 * WIDE :, :] = s.query_out[zpos]
+
+    pieces = {
+        "query": (0, 2 * WIDE, WIDE, s.pq_core, s.pq_core_out, s.pq_core_in, s.pq_x_out, s.pq_x_in, s.pq_y_out, s.pq_y_in,
+                  s.pq_z_out, s.pq_z_in),
+        "pair": (1, 0, 2 * WIDE, s.pp_core, s.pp_core_out, s.pp_core_in, s.pp_x_out, s.pp_x_in, s.pp_y_out, s.pp_y_in,
+                 s.pp_z_out, s.pp_z_in),
+    }
+
+    def piece_core(name):
+        index, first, width, total, out, into = pieces[name][:6]
+        right = s.column_grads[first : first + width, :]
+        out[...] = dot(s.normed_all[span(flip(core), D // 2), :], right, 1, 1).astype(LOW)
+        started[name, "core"] = go(remote(out, into, s.p_send.at[index, 0], s.p_recv.at[index, 0], mate))
+        total[...] = dot(s.normed_all[span(core, D // 2), :], right, 1, 1)
+
+    def piece_x(name):
+        index, _, _, total, _, core_in, out, into = pieces[name][:8]
+        started[name, "core"].wait_recv()
+        total[...] = total[...] + core_in[...].astype(F32)
+        out[...] = total[span(flip(xpos), D // 4), :].astype(LOW)
+        started[name, "x"] = go(remote(out, into, s.p_send.at[index, 1], s.p_recv.at[index, 1], beside))
+
+    def piece_y(name):
+        index, _, _, total, _, _, _, x_in, out, into = pieces[name][:10]
+        started[name, "x"].wait_recv()
+        half = span(xpos, D // 4)
+        total[half, :] = total[half, :] + x_in[...].astype(F32)
+        out[...] = total[span(2 * xpos + flip(row), D // 8), :].astype(LOW)
+        started[name, "y"] = go(remote(out, into, s.p_send.at[index, 2], s.p_recv.at[index, 2], across))
+
+    def piece_z(name):
+        index, _, width, total, _, _, _, _, _, y_in, out, into = pieces[name]
+        started[name, "y"].wait_recv()
+        eighth = total[span(2 * xpos + row, D // 8), :] + y_in[...].astype(F32)
+        pad = jnp.zeros((8, width), F32)
+        for z_at in range(4):
+            out[z_at] = jnp.concatenate([eighth[OWN * z_at : OWN * z_at + OWN], pad], axis=0).astype(LOW)
+        started[name, "z"] = [go(remote(out.at[(zpos + step) % 4], into.at[zpos], s.p_send.at[index, 2 + step],
+                                        s.p_recv.at[index, 2 + step], along[step - 1])) for step in range(1, 4)]
+        into[zpos] = out[zpos]
+
+    def piece_last(name):
+        into = pieces[name][11]
+        for copy in started[name, "z"]:
+            copy.wait_recv()
+        if name == "query":
+            s.g_query[...] = jnp.concatenate([into[at, :OWN, :].astype(F32) for at in range(4)], axis=1)
+        else:
+            s.g_key[...] = jnp.concatenate([into[at, :OWN, :WIDE].astype(F32) for at in range(4)], axis=1)
+            s.g_value[...] = jnp.concatenate([into[at, :OWN, WIDE:].astype(F32) for at in range(4)], axis=1)
+
+    def finish_input():
+        for copy in back_copies.values():
+            copy.wait_recv()
+        grad_normed_attn = jnp.zeros((TOK, D), F32)
+        for part, weight in enumerate((s.vw_key, s.vw_value, s.vw_query)):
+            turned_back = jnp.concatenate(
+                [s.grads[group, WIDE * part : WIDE * part + WIDE, :] for group in range(GROUPS)], axis=0).T
+            grad_normed_attn = grad_normed_attn + dot(turned_back, weight[...], 1, 1)
+        row_again = s.hidden[...].astype(F32)
+        grad_in_part, grad_gain_attn = rms_back(row_again, rms(row_again), gain_first, grad_normed_attn)
+        s.grad_input[...] = (s.grad_middle[...] + grad_in_part).astype(LOW)
+        s.small_out[0, 0:1, :] = grad_gain_attn
+
+    def finish_table():
+        blank = jnp.zeros((8, TOK), F32)
+        carried = None
+        for step in reversed(range(16)):
+            rows = slice(8 * step, 8 * step + 8)
+            part = jnp.concatenate([
+                jnp.concatenate([blank, s.tile_grads[head, 3, rows, :], s.tile_grads[head, 2, rows, :],
+                                 s.tile_grads[head, 1, rows, :]], axis=1) for head in range(HEADS_HERE)], axis=0)
+            carried = part if carried is None else part + pltpu.roll(carried, QUERIES - 8, 1)
+        lane = lax.broadcasted_iota(jnp.int32, (1, TOK), 1)
+        hot_padded = jnp.concatenate([hot, jnp.zeros((TOK - NB, QUERIES), F32)], axis=0)
+        for head in range(HEADS_HERE):
+            one = carried[8 * head + 7 : 8 * head + 8]
+            for step in reversed(range(7)):
+                one = carried[8 * head + step : 8 * head + step + 1] + pltpu.roll(one, QUERIES - 1, 1)
+            line = lax.dot_general(jnp.broadcast_to(one, (8, QUERIES)), hot_padded, (((1,), (1,)), ((), ())),
+                                   precision=lax.Precision.HIGHEST, preferred_element_type=F32)[0:1]
+            left = jnp.sum(s.tile_grads[head, 0], keepdims=True)
+            right = jnp.sum(s.tile_grads[head, 4], keepdims=True)
+            line = line + jnp.where(lane == 15, left, 0.0) + jnp.where(lane == 31, right, 0.0)
+            s.small_out[0, 2 + head : 3 + head, span(zpos, TOK)] = line
+
+    small_peers = (mate, across, beside, near, far)
+
+    def small_go(step):
+        started["small", step] = go(remote(s.small_out.at[step], s.small_in.at[step], s.s_send.at[step], s.s_recv.at[step],
+                                           small_peers[step]))
+
+    def small_next(step):
+        started["small", step].wait_recv()
+        summed = s.small_out[step] + s.small_in[step]
+        if step < 4:
+            s.small_out[step + 1] = summed
+            small_go(step + 1)
+        else:
+            s.small_sum[...] = summed
+
+    buffers = {
+        "down": (s.down_total, s.down_xs, s.down_xr, s.down_ns, s.down_nr, s.down_fs, s.down_fr),
+        "gate": (s.gate_total, s.gate_xs, s.gate_xr, s.gate_ns, s.gate_nr, s.gate_fs, s.gate_fr),
+        "out": (s.out_total, s.out_xs, s.out_xr, s.out_ns, s.out_nr, s.out_fs, s.out_fr),
+    }
+    numbers = {("down", 0): 0, ("out", 0): 5}
+    numbers.update({("gate", cut): 1 + cut for cut in range(CUT)})
+    taken = set()
+
+    def products(kind, unit, x_half):
+        if kind == "down":
+            product = dot(s.all_left_down[span(x_half, 4 * OWN_DOWN), :], s.right_down[...])
+            return [product[OWN_DOWN * at : OWN_DOWN * at + OWN_DOWN] for at in range(4)]
+        if kind == "out":
+            product = dot(s.all_left_out[span(x_half, 4 * OWN), :], s.right_out[...])
+            pair = (product[:, : D // 2], product[:, D // 2 :])
+        else:
+            product = dot(s.all_left_gate[span(x_half, 4 * OWN), :], s.right_gate[unit])
+            pair = (product[:, :CUT_COLS], product[:, CUT_COLS:])
+        return [jnp.concatenate([part[OWN * at : OWN * at + OWN] for part in pair], axis=0) for at in range(4)]
+
+    def unit_x(kind, unit):
+        number = numbers[kind, unit]
+        total, xs, xr = buffers[kind][:3]
+        if kind not in taken:
+            taken.add(kind)
+            take_left({"down": 0, "gate": 1, "out": 2}[kind])
+        take_right(number)
+        for block, value in enumerate(products(kind, unit, flip(xpos))):
+            xs[unit, block] = value.astype(LOW)
+        started["x", number] = go(remote(xs.at[unit], xr.at[unit], s.ux_send.at[number], s.ux_recv.at[number], beside))
+        for block, value in enumerate(products(kind, unit, xpos)):
+            total[unit, block] = value
+
+    def unit_near(kind, unit):
+        number = numbers[kind, unit]
+        total, _, xr, ns, nr = buffers[kind][:5]
+        started["x", number].wait_recv()
+        for block in range(4):
+            total[unit, block] = total[unit, block] + xr[unit, block].astype(F32)
+        ns[unit, 0] = total[unit, near_z(zpos)].astype(LOW)
+        ns[unit, 1] = total[unit, 3 - zpos].astype(LOW)
+        started["near", number] = go(remote(ns.at[unit], nr.at[unit], s.un_send.at[number], s.un_recv.at[number], near))
+
+    def unit_far(kind, unit):
+        number = numbers[kind, unit]
+        total, _, _, _, nr, fs, fr = buffers[kind]
+        started["near", number].wait_recv()
+        fs[unit] = (total[unit, far_z(zpos)] + nr[unit, 1].astype(F32)).astype(LOW)
+        started["far", number] = go(remote(fs.at[unit], fr.at[unit], s.uf_send.at[number], s.uf_recv.at[number], far))
+
+    def unit_last(kind, unit):
+        number = numbers[kind, unit]
+        total, _, _, _, nr, _, fr = buffers[kind]
+        started["far", number].wait_recv()
+        final = total[unit, zpos] + nr[unit, 0].astype(F32) + fr[unit].astype(F32)
+        if kind == "down":
+            s.g_down[...] = final
+        elif kind == "gate":
+            cols = slice(CUT_COLS * unit, CUT_COLS * unit + CUT_COLS)
+            s.g_gate[:, cols] = final[:OWN]
+            s.g_up[:, cols] = final[OWN:]
+        else:
+            s.g_out[:, : D // 2] = final[:OWN]
+            s.g_out[:, D // 2 :] = final[OWN:]
+
+    def pass_gate(cut):
+        pass_right(1 + cut, s.right_gate.at[cut])
+
+    def wait_normed():
+        for copy in n_copies:
+            copy.wait_recv()
+
+    begin_backward()
+    differentiate(0)
+    pass_gate(0)
+    reduce_cores(0)
+    unit_x("gate", 0)
+    differentiate(1)
+    pass_gate(1)
+    reduce_cores(1)
+    reduce_x(0)
+    unit_x("gate", 1)
+    differentiate(2)
+    pass_gate(2)
+    reduce_cores(2)
+    reduce_x(1)
+    unit_near("gate", 0)
+    differentiate(3)
+    finish_queries()
+    wait_normed()
+    piece_core("query")
+    reduce_cores(3)
+    reduce_x(2)
+    unit_near("gate", 1)
+    unit_far("gate", 0)
+    piece_x("query")
+    reduce_x(3)
+    piece_core("pair")
+    unit_x("gate", 2)
+    pass_gate(3)
+    piece_y("query")
+    piece_x("pair")
+    pass_right(5, s.right_out)
+    finish_input()
+    finish_table()
+    small_go(0)
+    piece_z("query")
+    piece_y("pair")
+    unit_x("gate", 3)
+    small_next(0)
+    unit_near("gate", 2)
+    piece_z("pair")
+    unit_x("down", 0)
+    small_next(1)
+    unit_x("out", 0)
+    unit_near("gate", 3)
+    small_next(2)
+    unit_far("gate", 1)
+    unit_far("gate", 2)
+    unit_near("down", 0)
+    small_next(3)
+    unit_near("out", 0)
+    unit_far("gate", 3)
+    unit_last("gate", 0)
+    unit_last("gate", 1)
+    piece_last("query")
+    unit_far("down", 0)
+    unit_far("out", 0)
+    small_next(4)
+    unit_last("gate", 2)
+    piece_last("pair")
+    unit_last("gate", 3)
+    unit_last("down", 0)
+    unit_last("out", 0)
+    for copy in sends:
+        copy.wait_send()
+
+
+def layer_scratch():
+    scratch = {}
+
+    def low(name, *shape):
+        scratch[name] = pltpu.VMEM(shape, LOW)
+
+    def wide(name, *shape):
+        scratch[name] = pltpu.VMEM(shape, F32)
+
+    def sem(name, *shape):
+        scratch[name + "_send"] = pltpu.SemaphoreType.DMA(shape)
+        scratch[name + "_recv"] = pltpu.SemaphoreType.DMA(shape)
+
+    for name in ("query", "key", "value", "out"):
+        low("vw_" + name, D, D)
+    low("vw_gate", D, FF)
+    low("vw_up", D, FF)
+    low("vw_down", FF, D)
+    scratch["load_sem"] = pltpu.SemaphoreType.DMA((7,))
+    low("sent", GROUPS, SENT_ROWS, TOK)
+    low("kv", 16, KV_ROWS, TOK)
+    low("queries", 4, WIDE, TOK)
+    low("normed_all", D, QUERIES)
+    wide("profile", H, 1, QUERIES)
+    wide("tiles", HEADS_HERE, 5, TOK, TOK)
+    low("marked", HEADS_HERE, DH + MARKS, QUERIES)
+    wide("score_buf", 4, TOK, QUERIES)
+    low("weight_buf", QUERIES, QUERIES)
+    low("grad_buf", QUERIES, QUERIES)
+    for name in ("highest", "totals", "lse", "deltas"):
+        wide(name, HEADS_HERE, 1, QUERIES)
+    wide("summed", HEADS_HERE, DH, QUERIES)
+    low("context_out", 4, WIDE, TOK)
+    low("context", GROUPS, WIDE, TOK)
+    wide("grad_hidden", CUT, TOK, CUT_COLS)
+    low("hidden_act", TOK, FF)
+    wide("grad_middle", TOK, D)
+    low("d_out", GROUPS, WIDE, TOK)
+    low("cotangents", 4, WIDE, TOK)
+    wide("tile_grads", HEADS_HERE, 5, TOK, TOK)
+    wide("query_sum", HEADS_HERE, DH, QUERIES)
+    wide("key_sum", 4, 4, 2 * WIDE, TOK)
+    low("core_out", 4, 2, 2 * WIDE, TOK)
+    low("core_in", 4, 2, 2 * WIDE, TOK)
+    low("x_out", 4, 2 * WIDE, TOK)
+    low("x_in", 4, 2 * WIDE, TOK)
+    low("back_out", 3, 2 * WIDE, TOK)
+    low("query_out", 4, WIDE, TOK)
+    low("grads", GROUPS, 3 * WIDE, TOK)
+    low("column_grads", 3 * WIDE, QUERIES)
+    for name, width in (("pq", WIDE), ("pp", 2 * WIDE)):
+        wide(name + "_core", D // 2, width)
+        for stage, rows in (("core", D // 2), ("x", D // 4), ("y", D // 8)):
+            low(f"{name}_{stage}_out", rows, width)
+            low(f"{name}_{stage}_in", rows, width)
+        low(name + "_z_out", 4, OWN + 8, width)
+        low(name + "_z_in", 4, OWN + 8, width)
+    wide("small_out", 5, 8, D)
+    wide("small_in", 5, 8, D)
+    low("right_down", QUERIES, D)
+    low("right_gate", CUT, QUERIES, 2 * CUT_COLS)
+    low("right_out", QUERIES, D)
+    for name, rows in (("down", FF // 4), ("gate", D // 4), ("out", D // 4)):
+        low("left_" + name, 4, rows, TOK)
+        low("all_left_" + name, rows, QUERIES)
+    for name, units, rows, width in (("down", 1, OWN_DOWN, D), ("gate", CUT, 2 * OWN, CUT_COLS), ("out", 1, 2 * OWN, D // 2)):
+        wide(name + "_total", units, 4, rows, width)
+        for stage, blocks in (("x", 4), ("n", 2)):
+            low(f"{name}_{stage}s", units, blocks, rows, width)
+            low(f"{name}_{stage}r", units, blocks, rows, width)
+        low(name + "_fs", units, rows, width)
+        low(name + "_fr", units, rows, width)
+    sem("z", 4)
+    sem("q", 4)
+    sem("x", 4)
+    sem("c", 8)
+    sem("n", 4)
+    sem("o", 4)
+    sem("d", 4)
+    sem("cg", 4)
+    sem("xg", 4)
+    sem("b", 4)
+    sem("qb", 4)
+    sem("p", 2, 6)
+    sem("s", 5)
+    sem("right", 6, 3)
+    sem("left", 3, 3)
+    sem("ux", 6)
+    sem("un", 6)
+    sem("uf", 6)
+    return scratch
+
+
+def hand_over_kernel(*refs):
+    half = len(refs) // 2
+    for source, target in zip(refs[:half], refs[half:]):
+        target[...] = source[...]
+
+
+def fast_device(
+    hidden_in, segments, cotangent, w_query, w_key, w_value, w_out, w_gate, w_up, w_down, bias_table, gain_attn, gain_ffn
+):
+    ins = {
+        "hidden": hidden_in[0], "segments": segments, "cotangent": cotangent[0], "table": bias_table,
+        "gain_attn": gain_attn[None], "gain_ffn": gain_ffn[None], "w_query": w_query, "w_key": w_key, "w_value": w_value,
+        "w_out": w_out, "w_gate": w_gate, "w_up": w_up, "w_down": w_down,
+    }
+    outs = {
+        "output": ((TOK, D), LOW), "grad_input": ((TOK, D), LOW), "g_query": ((OWN, D), F32), "g_key": ((OWN, D), F32),
+        "g_value": ((OWN, D), F32), "g_out": ((OWN, D), F32), "g_gate": ((OWN, FF), F32), "g_up": ((OWN, FF), F32),
+        "g_down": ((OWN_DOWN, D), F32), "small_sum": ((8, D), F32),
+    }
+    scratch = layer_scratch()
+    names = tuple(ins) + tuple(outs) + tuple(scratch)
+    vmem, anywhere = pl.BlockSpec(memory_space=pltpu.VMEM), pl.BlockSpec(memory_space=pl.ANY)
+    shapes = [jax.ShapeDtypeStruct(shape, kind) for shape, kind in outs.values()]
+    found = pl.pallas_call(
+        functools.partial(layer_kernel, names),
+        out_shape=shapes,
+        in_specs=[anywhere if name.startswith("w_") else vmem for name in ins],
+        out_specs=[vmem] * len(outs),
+        scratch_shapes=list(scratch.values()),
+        compiler_params=pltpu.CompilerParams(collective_id=0, has_side_effects=True, vmem_limit_bytes=60 * 2**20),
+        name="encoder_layer",
+    )(*ins.values())
+    found = pl.pallas_call(hand_over_kernel, out_shape=shapes, name="hand_over")(*found)
+    small = found[9]
+    table = small[2:5, :QUERIES].reshape(HEADS_HERE, GROUPS, TOK)[:, :, :NB].transpose(2, 1, 0).reshape(NB, H)
+    return (found[0][None], found[1][None], *found[2:9], table, small[0], small[1])
+
+
 def solution(mesh):
     in_specs = (
         P("rows", "seq", None),
@@ -383,6 +1178,7 @@
         P(),
         P(),
     )
+    fast = dict(mesh.shape) == {"rows": 2, "seq": 16}
     return jax.shard_map(
-        per_device, mesh=mesh, in_specs=in_specs, out_specs=out_specs, check_vma=False
-    )
+        fast_device if fast else per_device, mesh=mesh, in_specs=in_specs, out_specs=out_specs, check_vma=False
+    )

time: 992 us -> 128 us (0.13)
  waiting for transfers between devices: 504 us -> 0 us
  local copies, waits for them, and re-layouts: 231 us -> 6.65 us
  Pallas kernels: 0 us -> 121 us
  matrix products: 112 us -> 0 us
  blocking collectives: 98.5 us -> 0 us
  other arithmetic: 24.4 us -> 0 us
  between operations: 14.9 us -> 0.66 us
    reduce_scatter x7 -> x0, waiting for transfers between devices: 503 us -> none  [the longest x1 121 us: per_device(): lax.psum_scatter(grad_w_up, ('rows', 'seq'), scatter_dimension=0, tiled=T...]
    pallas_call x0 -> x2, Pallas kernels: none -> 121 us  [the longest x1 118 us: fast_device(): pl.pallas_call(functools.partial(layer_kernel, names), out_shape=shapes,...]
    dot_general x31 -> x0, matrix products: 112 us -> none  [the longest x2 26.9 us: block_scores(): jnp.einsum('rhd,chd->hrc', row_heads, col_heads, preferred_element_type=j...]
    reshape x4 -> x2, local copies, waits for them, and re-layouts: 100 us -> 1.33 us  [fast_device(): small[2:5, :QUERIES].reshape(HEADS_HERE, GROUPS, TOK)[:, :, :NB]]
    all_gather x3 -> x0, blocking collectives: 61.3 us -> none  [the longest x1 23 us: per_device(): seg_all = lax.all_gather(seg_own, 'seq', axis=0, tiled=True)]
    another operation x4 -> x0, local copies, waits for them, and re-layouts: 47.6 us -> none  [toeplitz_bias(): tiled_vec = jnp.tile(per_offset, (1, row_count + 1))]
    psum x1 -> x0, blocking collectives: 37.2 us -> none  [per_device(): lax.psum((grad_tab, grad_gain_attn, grad_gain_ffn), ('rows', 'seq'))]
    slice x2 -> x1, local copies, waits for them, and re-layouts: 27.5 us -> 1.43 us  [fast_device(): small[1]]
  transfers between devices with their start and end apart: 11 -> 0, of which waited for: 5 -> 0; matrix products, arithmetic and copies ran while one was open for 36% -> 0% of each run, Pallas kernels for 0% -> 0%
where the time goes in v3:
time: 128 us
  Pallas kernels  121 us (95%)
  local copies, waits for them, and re-layouts  6.65 us (5%)
    pallas_call x1, Pallas kernels, fast_device(): pl.pallas_call(functools.partial(layer_kernel, names), out_shape=shapes,...  118 us

profile of v3, /device:TPU:0, one launch (start us, length us, event | category | flops | bytes accessed | tf_op | source)
XLA Modules:
  0.0 128.1 jit_solution(7020495766801442338)
XLA Ops:
  0.6 1.3 broadcast_in_dim.12.refs_4_
  1.9 1.3 broadcast_in_dim.13.refs_5_
  3.2 1.4 %copy.27.refs_3_ = bf16[32,12]{1,0:T(8,128)(2,1)} copy(bf16[32,12]{0,1:T(8,128)(2,1)} %param.23) | data formatting | bytes 1536 | tf_op args[10]
  4.5 118.4 %encoder_layer.1 = (bf16[128,768]{1,0:T(8,128)(2,1)}, bf16[128,768]{1,0:T(8,128)(2,1)}, f32[24,768]{1,0:T(8,128)}, f32[24,768]{1,0:T(8,128)}, f32[24,768]{1,0:T(...) custom-call(bf16[128,768]{1,0:T(8,128)(2,1)} %bitcast.10, ...), custom_call_target="tpu_custom_call" | custom-call | tf_op jit(solution)/shard_map/encoder_layer/pallas_call | solution.py:1136
  122.9 2.4 %hand_over.1 = (bf16[128,768]{1,0:T(8,128)(2,1)}, bf16[128,768]{1,0:T(8,128)(2,1)}, f32[24,768]{1,0:T(8,128)}, f32[24,768]{1,0:T(8,128)}, f32[24,768]{1,0:T(8,12...) custom-call(bf16[128,768]{1,0:T(8,128)(2,1)} %get-tuple-element.32.r, ...), custom_call_target="tpu_custom_call" | custom-call | tf_op jit(solution)/shard_map/hand_over/pallas_call | solution.py:1145
  125.3 0.7 slice_bitcast_fusion.1
  126.1 1.4 %slice_reduce_fusion = (f32[768]{0:T(1024)}, f32[768]{0:T(1024)}) fusion(f32[8,768]{1,0:T(8,128)} %get-tuple-element.51), kind=kLoop, calls=%fused_computation.2 | loop fusion | bytes 12288 | tf_op jit(solution)/shard_map/slice | solution.py:1148
  127.5 0.6 reshape.31
  (1 shorter events, 0.0 us)

commit v4 on v3

--- a/solution.py
+++ b/solution.py
@@ -364,11 +364,14 @@
 WIDE = HEADS_HERE * DH
 MARKS = 16
 KV_ROWS = 2 * WIDE + MARKS
-SENT_ROWS = KV_ROWS + WIDE
+Q_ROWS = WIDE + MARKS
+SENT_ROWS = KV_ROWS + Q_ROWS
 TOK = 128
 QUERIES = 512
 CUT = 4
 CUT_COLS = FF // CUT
+AXES = ("x", "y", "x", "y")
+DOWN_AXIS, OUT_AXIS = "x", "y"
 OWN = D // 32
 OWN_DOWN = FF // 32
 SEPARATE = -1e30
@@ -413,6 +416,8 @@
 
 
 def head_rows(head, first=0):
+    if isinstance(head, int):
+        return pl.ds(first + DH * head, DH)
     return pl.ds(pl.multiple_of(first + DH * head, DH), DH)
 
 
@@ -457,10 +462,16 @@
     near = device(row, near_z(zpos), xpos, core)
     far = device(row, far_z(zpos), xpos, core)
     along = [device(row, (zpos + step) % 4, xpos, core) for step in range(1, 4)]
-    mine = 2 * row + core
-    parts = (2 * flip(row) + core, 2 * flip(row) + flip(core), 2 * row + flip(core))
+    aslant = device(row, zpos, flip(xpos), flip(core))
+    groups = {
+        "y": SimpleNamespace(bit=row, other=xpos, peers=(across, slant, mate), partner=beside),
+        "x": SimpleNamespace(bit=xpos, other=row, peers=(beside, aslant, mate), partner=across),
+    }
+    for group in groups.values():
+        group.mine = 2 * group.bit + core
+        group.parts = (2 * flip(group.bit) + core, 2 * flip(group.bit) + flip(core), 2 * group.bit + flip(core))
     here = flat_block(zpos, column)
-    peers = [mate, beside, across, slant] + along
+    peers = [mate, beside, across, slant, aslant] + along
     barrier = pltpu.get_barrier_semaphore()
     for peer in peers:
         pl.semaphore_signal(barrier, inc=1, device_id=peer, device_id_type=MESH)
@@ -473,7 +484,7 @@
         return copy
 
     def load(index):
-        name = ("w_key", "w_value", "w_query", "w_out", "w_gate", "w_up", "w_down")[index]
+        name = ("w_query", "w_key", "w_value", "w_out", "w_gate", "w_up", "w_down")[index]
         return pltpu.make_async_copy(getattr(s, name), getattr(s, "v" + name), s.load_sem.at[index])
 
     loads = [load(index) for index in range(7)]
@@ -482,8 +493,8 @@
 
     row_in = s.hidden[...].astype(F32)
     scale_first = rms(row_in)
-    gain_first = s.gain_attn[...].astype(F32)
-    gain_second = s.gain_ffn[...].astype(F32)
+    gain_first = s.gain_attn[...].astype(F32).reshape(1, D)
+    gain_second = s.gain_ffn[...].astype(F32).reshape(1, D)
     normed = (row_in * scale_first * gain_first).astype(LOW)
     seg_row = s.segments[...]
     marks = (seg_row + 1 == lax.broadcasted_iota(jnp.int32, (MARKS, TOK), 0)).astype(F32).astype(LOW)
@@ -494,20 +505,21 @@
         for group in range(GROUPS):
             s.sent[group, first : first + WIDE, :] = turned[WIDE * group : WIDE * group + WIDE]
 
-    project(0, s.vw_key, 0)
-    project(1, s.vw_value, WIDE)
+    project(0, s.vw_query, KV_ROWS)
+    project(1, s.vw_key, 0)
     for group in range(GROUPS):
         s.sent[group, 2 * WIDE : KV_ROWS, :] = marks
+        s.sent[group, KV_ROWS + WIDE :, :] = marks
     pl.semaphore_wait(barrier, len(peers))
-    kv_part, q_part = pl.ds(0, KV_ROWS), pl.ds(KV_ROWS, WIDE)
+    kv_part, q_part = pl.ds(0, KV_ROWS), pl.ds(KV_ROWS, Q_ROWS)
     x_copies, c_copies, on_copies = [None] * 4, [None] * 4, [None] * 4
+    q_copies = [go(remote(s.sent.at[(zpos + step) % 4, q_part], s.queries.at[zpos], s.q_send.at[step],
+                          s.q_recv.at[step], along[step - 1])) for step in range(1, 4)]
+    project(2, s.vw_value, WIDE)
     z_copies = [go(remote(s.sent.at[(zpos + step) % 4, kv_part], s.kv.at[here], s.z_send.at[step], s.z_recv.at[step],
                           along[step - 1])) for step in range(1, 4)]
     x_copies[0] = go(remote(s.sent.at[zpos, kv_part], s.kv.at[here], s.x_send.at[0], s.x_recv.at[0], beside))
     c_copies[0] = go(remote(s.sent.at[zpos, kv_part], s.kv.at[here], s.c_send.at[0], s.c_recv.at[0], mate))
-    project(2, s.vw_query, KV_ROWS)
-    q_copies = [go(remote(s.sent.at[(zpos + step) % 4, q_part], s.queries.at[zpos], s.q_send.at[step],
-                          s.q_recv.at[step], along[step - 1])) for step in range(1, 4)]
     for index in range(3, 7):
         loads[index].start()
     s.kv[here] = s.sent[zpos, :KV_ROWS, :]
@@ -515,7 +527,7 @@
 
     offsets = 256 - lax.broadcasted_iota(jnp.int32, (NB, QUERIES), 1)
     hot = (bucket_of(offsets) == lax.broadcasted_iota(jnp.int32, (NB, QUERIES), 0)).astype(F32)
-    profile = dot(s.table[...], hot.astype(LOW), 0, 0)
+    profile = dot(s.table[...], hot.astype(LOW))
     for head in range(H):
         s.profile[head] = profile[head : head + 1]
     for head in range(HEADS_HERE):
@@ -544,65 +556,65 @@
 
     right_copies, left_copies, onward = {}, {}, {}
 
-    def share_right(index, buffer, value):
-        spot = buffer.at[span(mine, TOK)]
-        buffer[span(mine, TOK), :] = value
+    def share_right(index, buffer, value, axis="y"):
+        group = groups[axis]
+        spot = buffer.at[span(group.mine, TOK)]
+        buffer[span(group.mine, TOK), :] = value
         right_copies[index] = (
-            go(remote(spot, spot, s.right_send.at[index, 0], s.right_recv.at[index, 0], across)),
+            go(remote(spot, spot, s.right_send.at[index, 0], s.right_recv.at[index, 0], group.peers[0])),
             go(remote(spot, spot, s.right_send.at[index, 1], s.right_recv.at[index, 1], mate)),
         )
 
-    def pass_right(index, buffer):
+    def pass_right(index, buffer, axis="y"):
         right_copies[index][0].wait_recv()
-        spot = buffer.at[span(parts[0], TOK)]
+        spot = buffer.at[span(groups[axis].parts[0], TOK)]
         onward[index] = go(remote(spot, spot, s.right_send.at[index, 2], s.right_recv.at[index, 2], mate))
 
     def take_right(index):
         right_copies[index][1].wait_recv()
         onward[index].wait_recv()
 
-    def share_left(index, staged, buffer):
-        lanes = span(mine, TOK)
-        buffer[:, lanes] = staged[mine]
+    def share_left(index, staged, buffer, axis="y"):
+        group = groups[axis]
+        lanes = span(group.mine, TOK)
+        buffer[:, lanes] = staged[group.mine]
         left_copies[index] = [
             go(remote(staged.at[part], buffer.at[:, lanes], s.left_send.at[index, slot], s.left_recv.at[index, slot], peer))
-            for slot, (peer, part) in enumerate(zip((across, slant, mate), parts))
+            for slot, (peer, part) in enumerate(zip(group.peers, group.parts))
         ]
 
     def take_left(index):
         for copy in left_copies[index]:
             copy.wait_recv()
 
-    def stage_quarters(staged, turned, height):
+    def stage_quarters(staged, turned, height, axis="y"):
+        weights = (16, 2) if axis == "y" else (2, 16)
         for part in range(4):
-            for x_half in range(2):
-                blocks = []
-                for z_at in range(4):
-                    first = height * (16 * (part // 2) + 4 * z_at + 2 * x_half + part % 2)
-                    blocks.append(turned[first : first + height])
-                staged[part, 4 * height * x_half : 4 * height * (x_half + 1), :] = jnp.concatenate(
-                    blocks, axis=0).astype(LOW)
-
-    share_right(0, s.right_down, grad_branch)
-    relay(1)
-    pass_on(0)
-    pass_right(0, s.right_down)
-    relay(2)
-    pass_on(1)
+            for half in range(2):
+                firsts = [height * (weights[0] * (part // 2) + 4 * z_at + weights[1] * half + part % 2) for z_at in range(4)]
+                staged[part, 4 * height * half : 4 * height * (half + 1), :] = jnp.concatenate(
+                    [turned[first : first + height] for first in firsts], axis=0).astype(LOW)
+
+    share_right(0, s.right_down, grad_branch, DOWN_AXIS)
     turned = normed.astype(F32).T
     order = [16 * r + 4 * z + 2 * x + c for c in range(2) for x in range(2) for r in range(2) for z in range(4)]
     s.normed_all[:, span(zpos, TOK)] = jnp.concatenate(
         [turned[OWN * at : OWN * at + OWN] for at in order], axis=0).astype(LOW)
-    relay(3)
-    pass_on(2)
+    n_copies = []
+
+    def share_normed(piece):
+        rows = pl.ds(D // 4 * piece, D // 4)
+        for step in range(1, 4):
+            spot = s.normed_all.at[rows, span(zpos, TOK)]
+            n_copies.append(go(remote(spot, spot, s.n_send.at[piece, step], s.n_recv.at[piece, step], along[step - 1])))
+
+    pass_on(0)
     for copy in q_copies:
         copy.wait_recv()
-    n_copies = [go(remote(s.normed_all.at[:, span(zpos, TOK)], s.normed_all.at[:, span(zpos, TOK)],
-                          s.n_send.at[step], s.n_recv.at[step], along[step - 1])) for step in range(1, 4)]
 
     for block in range(4):
         lanes = slice(TOK * block, TOK * block + TOK)
-        apart = ((1.0 - s.kv[flat_block(block, column), 2 * WIDE :, :].astype(F32)) * SEPARATE).astype(LOW)
+        apart = ((1.0 - s.queries[block, WIDE:, :].astype(F32)) * SEPARATE).astype(LOW)
         for head in range(HEADS_HERE):
             s.marked[head, :DH, lanes] = s.queries[block, DH * head : DH * head + DH, :]
             s.marked[head, DH:, lanes] = apart
@@ -617,6 +629,8 @@
 
     def wide_rows(rows, chunk):
         return jnp.concatenate([s.kv[flat_block(chunk, spot), rows, :] for spot in range(4)], axis=1)
+
+    o_copies = []
 
     def attend(step):
         chunk = (zpos + 4 - step) % 4
@@ -635,29 +649,45 @@
                 weights = jnp.exp(s.score_buf[spot] - newest)
                 total = total + jnp.sum(weights, axis=0, keepdims=True)
                 s.weight_buf[TOK * spot : TOK * spot + TOK, :] = weights.astype(LOW)
-            s.highest[head] = newest
-            s.totals[head] = total
             values = wide_rows(head_rows(head, WIDE), chunk)
-            s.summed[head] = s.summed[head] * rescale + dot(values, s.weight_buf[...])
+            summed = s.summed[head] * rescale + dot(values, s.weight_buf[...])
+            if step < 3:
+                s.highest[head] = newest
+                s.totals[head] = total
+                s.summed[head] = summed
+                return carry
+            summed = summed / total
+            s.summed[head] = summed
+            s.lse[head] = newest + jnp.log(total)
+            low = summed.astype(LOW)
+            rows = slice(DH * head, DH * head + DH)
+            for block in range(4):
+                s.context_out[block, rows, :] = low[:, TOK * block : TOK * block + TOK]
+            for hop in range(1, 4):
+                o_copies.append(go(remote(s.context_out.at[(zpos + hop) % 4, rows], s.context.at[zpos, rows],
+                                          s.o_send.at[head, hop], s.o_recv.at[head, hop], along[hop - 1])))
             return carry
 
-        lax.fori_loop(0, HEADS_HERE, one_head, 0)
-
-    for step in range(4):
-        attend(step)
-        if step == 0:
-            pass_on(3)
-    for head in range(HEADS_HERE):
-        done = s.summed[head] / s.totals[head]
-        s.summed[head] = done
-        s.lse[head] = s.highest[head] + jnp.log(s.totals[head])
-        low = done.astype(LOW)
-        for block in range(4):
-            s.context_out[block, DH * head : DH * head + DH, :] = low[:, TOK * block : TOK * block + TOK]
-    o_copies = [go(remote(s.context_out.at[(zpos + step) % 4], s.context.at[zpos], s.o_send.at[step], s.o_recv.at[step],
-                          along[step - 1])) for step in range(1, 4)]
+        if step < 3:
+            lax.fori_loop(0, HEADS_HERE, one_head, 0)
+        else:
+            for head in range(HEADS_HERE):
+                one_head(head, 0)
+
+    attend(0)
+    relay(1)
+    relay(2)
+    pass_on(1)
+    relay(3)
+    share_normed(0)
+    share_normed(1)
+    pass_on(2)
+    attend(1)
+    pass_right(0, s.right_down, DOWN_AXIS)
+    pass_on(3)
+    attend(2)
+    attend(3)
     s.context[zpos] = s.context_out[zpos]
-
     loads[6].wait()
     for cut in range(CUT):
         s.grad_hidden[cut] = dot(grad_branch, s.vw_down[CUT_COLS * cut : CUT_COLS * cut + CUT_COLS, :], 1, 1)
@@ -670,8 +700,11 @@
     middle = row_in + dot(context_t, s.vw_out[...], 0, 0)
     scale_second = rms(middle)
     normed_ffn = (middle * scale_second * gain_second).astype(LOW)
-    stage_quarters(s.left_gate, normed_ffn.astype(F32).T, OWN)
-    share_left(1, s.left_gate, s.all_left_gate)
+    share_normed(2)
+    turned = normed_ffn.astype(F32).T
+    for index, axis in ((1, "y"), (3, "x")):
+        stage_quarters(s.left_gate.at[index // 2], turned, OWN, axis)
+        share_left(index, s.left_gate.at[index // 2], s.all_left_gate.at[index // 2], axis)
     grad_normed = jnp.zeros((TOK, D), F32)
     for cut in range(CUT):
         cols = slice(CUT_COLS * cut, CUT_COLS * cut + CUT_COLS)
@@ -681,7 +714,7 @@
         s.hidden_act[:, cols] = (gelu * upward).astype(LOW)
         grad_gate = (grad_hidden * upward * slope).astype(LOW)
         grad_upward = (grad_hidden * gelu).astype(LOW)
-        share_right(1 + cut, s.right_gate.at[cut], jnp.concatenate([grad_gate, grad_upward], axis=1))
+        share_right(1 + cut, s.right_gate.at[cut], jnp.concatenate([grad_gate, grad_upward], axis=1), AXES[cut])
         grad_normed = grad_normed + dot(grad_gate, s.vw_gate[:, cols], 1, 1) + dot(grad_upward, s.vw_up[:, cols], 1, 1)
     grad_mid_part, grad_gain_ffn = rms_back(middle, scale_second, gain_second, grad_normed)
     grad_middle = grad_result + grad_mid_part
@@ -689,17 +722,18 @@
     grad_context = dot(s.vw_out[...], grad_attn, 1, 1).astype(LOW)
     for group in range(GROUPS):
         s.d_out[group] = grad_context[WIDE * group : WIDE * group + WIDE]
-    d_copies = [go(remote(s.d_out.at[(zpos + step) % 4], s.cotangents.at[zpos], s.d_send.at[step], s.d_recv.at[step],
-                          along[step - 1])) for step in range(1, 4)]
+    d_copies = [[go(remote(s.d_out.at[(zpos + step) % 4, pl.ds(DH * head, DH)], s.cotangents.at[zpos, pl.ds(DH * head, DH)],
+                           s.d_send.at[head, step], s.d_recv.at[head, step], along[step - 1])) for step in range(1, 4)]
+                for head in range(HEADS_HERE)]
     s.cotangents[zpos] = s.d_out[zpos]
     s.grad_middle[...] = grad_middle
     s.small_out[0] = jnp.zeros((8, D), F32)
     s.small_out[0, 1:2, :] = grad_gain_ffn
-    share_right(5, s.right_out, grad_attn)
-    stage_quarters(s.left_down, s.hidden_act[...].T, OWN_DOWN)
-    share_left(0, s.left_down, s.all_left_down)
-    stage_quarters(s.left_out, context_t.astype(F32), OWN)
-    share_left(2, s.left_out, s.all_left_out)
+    share_right(5, s.right_out, grad_attn, OUT_AXIS)
+    stage_quarters(s.left_down, s.hidden_act[...].T, OWN_DOWN, DOWN_AXIS)
+    share_left(0, s.left_down, s.all_left_down, DOWN_AXIS)
+    stage_quarters(s.left_out, context_t.astype(F32), OWN, OUT_AXIS)
+    share_left(2, s.left_out, s.all_left_out, OUT_AXIS)
     result = middle + dot(s.hidden_act[...], s.vw_down[...])
     s.output[...] = jnp.where(valid, result, 0.0).astype(LOW)
     s.tile_grads[...] = jnp.zeros_like(s.tile_grads)
@@ -713,16 +747,14 @@
 
     core_copies, xg_copies, back_copies, started = {}, {}, {}, {}
 
-    def begin_backward():
-        for copy in d_copies:
-            copy.wait_recv()
-        for head in range(HEADS_HERE):
-            s.deltas[head] = jnp.sum(wide_cotangent(head).astype(F32) * s.summed[head], axis=0, keepdims=True)
-
     def differentiate(step):
         chunk = chunk_of(step)
 
         def one_head(head, carry):
+            if step == 0:
+                for copy in d_copies[head]:
+                    copy.wait_recv()
+                s.deltas[head] = jnp.sum(wide_cotangent(head).astype(F32) * s.summed[head], axis=0, keepdims=True)
             cotangent = wide_cotangent(head)
             for spot in range(4):
                 key_spot = flat_block(chunk, spot)
@@ -744,7 +776,11 @@
                 s.key_sum[step, spot, head_rows(head, WIDE), :] = grad_values[:, lanes]
             return carry
 
-        lax.fori_loop(0, HEADS_HERE, one_head, 0)
+        if step > 0:
+            lax.fori_loop(0, HEADS_HERE, one_head, 0)
+        else:
+            for head in range(HEADS_HERE):
+                one_head(head, 0)
         for x_half in range(2):
             s.core_out[step, x_half] = s.key_sum[step, 2 * x_half + flip(core)].astype(LOW)
         core_copies[step] = go(remote(s.core_out.at[step], s.core_in.at[step], s.cg_send.at[step], s.cg_recv.at[step], mate))
@@ -863,16 +899,21 @@
             line = line + jnp.where(lane == 15, left, 0.0) + jnp.where(lane == 31, right, 0.0)
             s.small_out[0, 2 + head : 3 + head, span(zpos, TOK)] = line
 
-    small_peers = (mate, across, beside, near, far)
+    small_rounds = ((mate, across, slant), (beside,), tuple(along))
+    small_first = (0, 3, 4)
 
     def small_go(step):
-        started["small", step] = go(remote(s.small_out.at[step], s.small_in.at[step], s.s_send.at[step], s.s_recv.at[step],
-                                           small_peers[step]))
+        first = small_first[step]
+        started["small", step] = [
+            go(remote(s.small_out.at[step], s.small_in.at[first + slot], s.s_send.at[first + slot], s.s_recv.at[first + slot],
+                      peer)) for slot, peer in enumerate(small_rounds[step])]
 
     def small_next(step):
-        started["small", step].wait_recv()
-        summed = s.small_out[step] + s.small_in[step]
-        if step < 4:
+        summed = s.small_out[step]
+        for slot, copy in enumerate(started["small", step]):
+            copy.wait_recv()
+            summed = summed + s.small_in[small_first[step] + slot]
+        if step < 2:
             s.small_out[step + 1] = summed
             small_go(step + 1)
         else:
@@ -883,33 +924,41 @@
         "gate": (s.gate_total, s.gate_xs, s.gate_xr, s.gate_ns, s.gate_nr, s.gate_fs, s.gate_fr),
         "out": (s.out_total, s.out_xs, s.out_xr, s.out_ns, s.out_nr, s.out_fs, s.out_fr),
     }
-    numbers = {("down", 0): 0, ("out", 0): 5}
+    numbers = {("down", 0): 0, ("down", 1): 6, ("out", 0): 5}
     numbers.update({("gate", cut): 1 + cut for cut in range(CUT)})
+    axes = {("down", 0): DOWN_AXIS, ("down", 1): DOWN_AXIS, ("out", 0): OUT_AXIS}
+    axes.update({("gate", cut): AXES[cut] for cut in range(CUT)})
     taken = set()
 
     def products(kind, unit, x_half):
         if kind == "down":
-            product = dot(s.all_left_down[span(x_half, 4 * OWN_DOWN), :], s.right_down[...])
+            cols = slice(D // 2 * unit, D // 2 * unit + D // 2)
+            product = dot(s.all_left_down[span(x_half, 4 * OWN_DOWN), :], s.right_down[:, cols])
             return [product[OWN_DOWN * at : OWN_DOWN * at + OWN_DOWN] for at in range(4)]
         if kind == "out":
             product = dot(s.all_left_out[span(x_half, 4 * OWN), :], s.right_out[...])
             pair = (product[:, : D // 2], product[:, D // 2 :])
         else:
-            product = dot(s.all_left_gate[span(x_half, 4 * OWN), :], s.right_gate[unit])
+            left = s.all_left_gate.at["yx".index(AXES[unit])]
+            product = dot(left[span(x_half, 4 * OWN), :], s.right_gate[unit])
             pair = (product[:, :CUT_COLS], product[:, CUT_COLS:])
         return [jnp.concatenate([part[OWN * at : OWN * at + OWN] for part in pair], axis=0) for at in range(4)]
 
     def unit_x(kind, unit):
         number = numbers[kind, unit]
         total, xs, xr = buffers[kind][:3]
-        if kind not in taken:
-            taken.add(kind)
-            take_left({"down": 0, "gate": 1, "out": 2}[kind])
-        take_right(number)
-        for block, value in enumerate(products(kind, unit, flip(xpos))):
+        group = groups[axes[kind, unit]]
+        left = {"down": 0, "out": 2, "gate": 1 + 2 * (axes[kind, unit] == "x")}[kind]
+        if left not in taken:
+            taken.add(left)
+            take_left(left)
+        if kind != "down" or unit == 0:
+            take_right(number)
+        for block, value in enumerate(products(kind, unit, flip(group.other))):
             xs[unit, block] = value.astype(LOW)
-        started["x", number] = go(remote(xs.at[unit], xr.at[unit], s.ux_send.at[number], s.ux_recv.at[number], beside))
-        for block, value in enumerate(products(kind, unit, xpos)):
+        started["x", number] = go(remote(xs.at[unit], xr.at[unit], s.ux_send.at[number], s.ux_recv.at[number],
+                                         group.partner))
+        for block, value in enumerate(products(kind, unit, group.other)):
             total[unit, block] = value
 
     def unit_near(kind, unit):
@@ -935,7 +984,7 @@
         started["far", number].wait_recv()
         final = total[unit, zpos] + nr[unit, 0].astype(F32) + fr[unit].astype(F32)
         if kind == "down":
-            s.g_down[...] = final
+            s.g_down[:, D // 2 * unit : D // 2 * unit + D // 2] = final
         elif kind == "gate":
             cols = slice(CUT_COLS * unit, CUT_COLS * unit + CUT_COLS)
             s.g_gate[:, cols] = final[:OWN]
@@ -945,74 +994,83 @@
             s.g_out[:, D // 2 :] = final[OWN:]
 
     def pass_gate(cut):
-        pass_right(1 + cut, s.right_gate.at[cut])
+        pass_right(1 + cut, s.right_gate.at[cut], AXES[cut])
+
+    def pass_out():
+        pass_right(5, s.right_out, OUT_AXIS)
 
     def wait_normed():
         for copy in n_copies:
             copy.wait_recv()
 
-    begin_backward()
-    differentiate(0)
-    pass_gate(0)
-    reduce_cores(0)
-    unit_x("gate", 0)
-    differentiate(1)
-    pass_gate(1)
-    reduce_cores(1)
-    reduce_x(0)
-    unit_x("gate", 1)
-    differentiate(2)
-    pass_gate(2)
-    reduce_cores(2)
-    reduce_x(1)
-    unit_near("gate", 0)
-    differentiate(3)
-    finish_queries()
-    wait_normed()
-    piece_core("query")
-    reduce_cores(3)
-    reduce_x(2)
-    unit_near("gate", 1)
-    unit_far("gate", 0)
-    piece_x("query")
-    reduce_x(3)
-    piece_core("pair")
-    unit_x("gate", 2)
-    pass_gate(3)
-    piece_y("query")
-    piece_x("pair")
-    pass_right(5, s.right_out)
-    finish_input()
-    finish_table()
-    small_go(0)
-    piece_z("query")
-    piece_y("pair")
-    unit_x("gate", 3)
-    small_next(0)
-    unit_near("gate", 2)
-    piece_z("pair")
-    unit_x("down", 0)
-    small_next(1)
-    unit_x("out", 0)
-    unit_near("gate", 3)
-    small_next(2)
-    unit_far("gate", 1)
-    unit_far("gate", 2)
-    unit_near("down", 0)
-    small_next(3)
-    unit_near("out", 0)
-    unit_far("gate", 3)
-    unit_last("gate", 0)
-    unit_last("gate", 1)
-    piece_last("query")
-    unit_far("down", 0)
-    unit_far("out", 0)
-    small_next(4)
-    unit_last("gate", 2)
-    piece_last("pair")
-    unit_last("gate", 3)
-    unit_last("down", 0)
-    unit_last("out", 0)
+    plan = (
+        (differentiate, 0),
+        (share_normed, 3),
+        (pass_gate, 0),
+        (differentiate, 1),
+        (unit_x, "gate", 0),
+        (differentiate, 2),
+        (wait_normed,),
+        (reduce_cores, 1),
+        (differentiate, 3),
+        (pass_gate, 2),
+        (finish_queries,),
+        (pass_out,),
+        (reduce_cores, 0),
+        (unit_x, "down", 0),
+        (pass_gate, 3),
+        (unit_x, "down", 1),
+        (reduce_cores, 2),
+        (reduce_x, 1),
+        (reduce_cores, 3),
+        (piece_core, "query"),
+        (unit_near, "gate", 0),
+        (reduce_x, 0),
+        (pass_gate, 1),
+        (unit_x, "gate", 2),
+        (reduce_x, 2),
+        (piece_x, "query"),
+        (unit_x, "gate", 3),
+        (reduce_x, 3),
+        (finish_table,),
+        (unit_near, "down", 1),
+        (piece_core, "pair"),
+        (unit_x, "gate", 1),
+        (unit_far, "gate", 0),
+        (unit_near, "down", 0),
+        (unit_near, "gate", 2),
+        (unit_x, "out", 0),
+        (unit_near, "gate", 3),
+        (unit_far, "down", 1),
+        (finish_input,),
+        (piece_x, "pair"),
+        (unit_last, "gate", 0),
+        (unit_far, "down", 0),
+        (unit_far, "gate", 2),
+        (piece_y, "query"),
+        (small_go, 0),
+        (unit_far, "gate", 3),
+        (unit_near, "out", 0),
+        (piece_y, "pair"),
+        (piece_z, "query"),
+        (small_next, 0),
+        (unit_near, "gate", 1),
+        (small_next, 1),
+        (piece_z, "pair"),
+        (unit_last, "down", 1),
+        (unit_far, "out", 0),
+        (unit_last, "gate", 2),
+        (unit_far, "gate", 1),
+        (piece_last, "query"),
+        (piece_last, "pair"),
+        (unit_last, "out", 0),
+        (small_next, 2),
+        (unit_last, "down", 0),
+        (unit_last, "gate", 3),
+        (unit_last, "gate", 1),
+    )
+    for act, *values in plan:
+        act(*values)
     for copy in sends:
         copy.wait_send()
 
@@ -1038,7 +1096,7 @@
     scratch["load_sem"] = pltpu.SemaphoreType.DMA((7,))
     low("sent", GROUPS, SENT_ROWS, TOK)
     low("kv", 16, KV_ROWS, TOK)
-    low("queries", 4, WIDE, TOK)
+    low("queries", 4, Q_ROWS, TOK)
     low("normed_all", D, QUERIES)
     wide("profile", H, 1, QUERIES)
     wide("tiles", HEADS_HERE, 5, TOK, TOK)
@@ -1074,15 +1132,17 @@
             low(f"{name}_{stage}_in", rows, width)
         low(name + "_z_out", 4, OWN + 8, width)
         low(name + "_z_in", 4, OWN + 8, width)
-    wide("small_out", 5, 8, D)
-    wide("small_in", 5, 8, D)
+    wide("small_out", 3, 8, D)
+    wide("small_in", 7, 8, D)
     low("right_down", QUERIES, D)
     low("right_gate", CUT, QUERIES, 2 * CUT_COLS)
     low("right_out", QUERIES, D)
-    for name, rows in (("down", FF // 4), ("gate", D // 4), ("out", D // 4)):
+    for name, rows in (("down", FF // 4), ("out", D // 4)):
         low("left_" + name, 4, rows, TOK)
         low("all_left_" + name, rows, QUERIES)
-    for name, units, rows, width in (("down", 1, OWN_DOWN, D), ("gate", CUT, 2 * OWN, CUT_COLS), ("out", 1, 2 * OWN, D // 2)):
+    low("left_gate", 2, 4, D // 4, TOK)
+    low("all_left_gate", 2, D // 4, QUERIES)
+    for name, units, rows, width in (("down", 2, OWN_DOWN, D // 2), ("gate", CUT, 2 * OWN, CUT_COLS), ("out", 1, 2 * OWN, D // 2)):
         wide(name + "_total", units, 4, rows, width)
         for stage, blocks in (("x", 4), ("n", 2)):
             low(f"{name}_{stage}s", units, blocks, rows, width)
@@ -1093,35 +1153,41 @@
     sem("q", 4)
     sem("x", 4)
     sem("c", 8)
-    sem("n", 4)
-    sem("o", 4)
-    sem("d", 4)
+    sem("n", 4, 4)
+    sem("o", HEADS_HERE, 4)
+    sem("d", HEADS_HERE, 4)
     sem("cg", 4)
     sem("xg", 4)
     sem("b", 4)
     sem("qb", 4)
     sem("p", 2, 6)
-    sem("s", 5)
+    sem("s", 7)
     sem("right", 6, 3)
-    sem("left", 3, 3)
-    sem("ux", 6)
-    sem("un", 6)
-    sem("uf", 6)
+    sem("left", 4, 3)
+    sem("ux", 7)
+    sem("un", 7)
+    sem("uf", 7)
     return scratch
 
 
 def hand_over_kernel(*refs):
-    half = len(refs) // 2
-    for source, target in zip(refs[:half], refs[half:]):
+    count = len(refs) // 2 - 1
+    for source, target in zip(refs[: count - 1], refs[count : 2 * count - 1]):
         target[...] = source[...]
+    small = refs[count - 1]
+    table, gain_attn, gain_ffn = refs[2 * count - 1 :]
+    lines = [small[2 + head : 3 + head, TOK * group : TOK * group + NB] for group in range(GROUPS) for head in range(HEADS_HERE)]
+    table[...] = jnp.concatenate(lines, axis=0)
+    gain_attn[...] = small[0:1, :].reshape(D)
+    gain_ffn[...] = small[1:2, :].reshape(D)
 
 
 def fast_device(
     hidden_in, segments, cotangent, w_query, w_key, w_value, w_out, w_gate, w_up, w_down, bias_table, gain_attn, gain_ffn
 ):
     ins = {
-        "hidden": hidden_in[0], "segments": segments, "cotangent": cotangent[0], "table": bias_table,
-        "gain_attn": gain_attn[None], "gain_ffn": gain_ffn[None], "w_query": w_query, "w_key": w_key, "w_value": w_value,
+        "hidden": hidden_in[0], "segments": segments, "cotangent": cotangent[0], "table": bias_table.T,
+        "gain_attn": gain_attn, "gain_ffn": gain_ffn, "w_query": w_query, "w_key": w_key, "w_value": w_value,
         "w_out": w_out, "w_gate": w_gate, "w_up": w_up, "w_down": w_down,
     }
     outs = {
@@ -1142,10 +1208,9 @@
         compiler_params=pltpu.CompilerParams(collective_id=0, has_side_effects=True, vmem_limit_bytes=60 * 2**20),
         name="encoder_layer",
     )(*ins.values())
-    found = pl.pallas_call(hand_over_kernel, out_shape=shapes, name="hand_over")(*found)
-    small = found[9]
-    table = small[2:5, :QUERIES].reshape(HEADS_HERE, GROUPS, TOK)[:, :, :NB].transpose(2, 1, 0).reshape(NB, H)
-    return (found[0][None], found[1][None], *found[2:9], table, small[0], small[1])
+    ends = [jax.ShapeDtypeStruct(shape, F32) for shape in ((H, NB), (D,), (D,))]
+    found = pl.pallas_call(hand_over_kernel, out_shape=shapes[:-1] + ends, name="hand_over")(*found)
+    return (found[0][None], found[1][None], *found[2:9], found[9].T, *found[10:])
 
 
 def solution(mesh):

time: 128 us -> 107 us (0.84)
  Pallas kernels: 121 us -> 106 us
  local copies, waits for them, and re-layouts: 6.65 us -> 0 us
    pallas_call x1, Pallas kernels: 118 us -> 104 us  [fast_device(): pl.pallas_call(functools.partial(layer_kernel, names), out_shape=shapes,...]
    broadcast_in_dim x2 -> x0, local copies, waits for them, and re-layouts: 2.52 us -> none  [the longest x1 1.26 us: fast_device(): gain_attn[None]]
    slice x1 -> x0, local copies, waits for them, and re-layouts: 1.43 us -> none  [fast_device(): small[1]]
    unnamed x1 -> x0, local copies, waits for them, and re-layouts: 1.37 us -> none
    reshape x2 -> x0, local copies, waits for them, and re-layouts: 1.33 us -> none  [fast_device(): small[2:5, :QUERIES].reshape(HEADS_HERE, GROUPS, TOK)[:, :, :NB]]
where the time goes in v4:
time: 107 us
  Pallas kernels  106 us (99%)
    pallas_call x1, Pallas kernels, fast_device(): pl.pallas_call(functools.partial(layer_kernel, names), out_shape=shapes,...  104 us
    pallas_call x1, Pallas kernels, fast_device(): pl.pallas_call(hand_over_kernel, out_shape=shapes[:-1] + ends, name='hand...  2.43 us

profile of v4, /device:TPU:0, one launch (start us, length us, event | category | flops | bytes accessed | tf_op | source)
XLA Modules:
  0.0 106.9 jit_solution(6226595629649892190)
XLA Ops:
  0.6 103.6 %encoder_layer.1 = (bf16[128,768]{1,0:T(8,128)(2,1)}, bf16[128,768]{1,0:T(8,128)(2,1)}, f32[24,768]{1,0:T(8,128)}, f32[24,768]{1,0:T(8,128)}, f32[24,768]{1,0:T(...) custom-call(bf16[128,768]{1,0:T(8,128)(2,1)} %bitcast.6, ...), custom_call_target="tpu_custom_call" | custom-call | tf_op jit(solution)/shard_map/encoder_layer/pallas_call | solution.py:1202
  104.3 2.4 %hand_over.1 = (bf16[128,768]{1,0:T(8,128)(2,1)}, bf16[128,768]{1,0:T(8,128)(2,1)}, f32[24,768]{1,0:T(8,128)}, f32[24,768]{1,0:T(8,128)}, f32[24,768]{1,0:T(8,12...) custom-call(bf16[128,768]{1,0:T(8,128)(2,1)} %get-tuple-element.34.r, ...), custom_call_target="tpu_custom_call" | custom-call | tf_op jit(solution)/shard_map/hand_over/pallas_call | solution.py:1212

commit v5 on v4

--- a/solution.py
+++ b/solution.py
@@ -363,15 +363,18 @@
 HEADS_HERE = H // GROUPS
 WIDE = HEADS_HERE * DH
 MARKS = 16
-KV_ROWS = 2 * WIDE + MARKS
+VALUES_AT = WIDE + MARKS
+KV_ROWS = VALUES_AT + WIDE
 Q_ROWS = WIDE + MARKS
 SENT_ROWS = KV_ROWS + Q_ROWS
 TOK = 128
 QUERIES = 512
 CUT = 4
+SMALL_ROWS = 24
 CUT_COLS = FF // CUT
-AXES = ("x", "y", "x", "y")
+AXES = ("y", "x", "y", "x")
 DOWN_AXIS, OUT_AXIS = "x", "y"
+LEFTS = {"y": 1, "x": 3, "z": 4, "w": 5}
 OWN = D // 32
 OWN_DOWN = FF // 32
 SEPARATE = -1e30
@@ -416,9 +419,7 @@
 
 
 def head_rows(head, first=0):
-    if isinstance(head, int):
-        return pl.ds(first + DH * head, DH)
-    return pl.ds(pl.multiple_of(first + DH * head, DH), DH)
+    return slice(first + DH * head, first + DH * head + DH)
 
 
 def remote(src, dst, send_sem, recv_sem, peer):
@@ -463,15 +464,26 @@
     far = device(row, far_z(zpos), xpos, core)
     along = [device(row, (zpos + step) % 4, xpos, core) for step in range(1, 4)]
     aslant = device(row, zpos, flip(xpos), flip(core))
+    low_z, high_z = zpos % 2, zpos // 2
+    near_slant = device(row, near_z(zpos), xpos, flip(core))
+    corner = device(flip(row), zpos, flip(xpos), core)
+    far_corner = device(flip(row), zpos, flip(xpos), flip(core))
+    by_z = (zpos, near_z(zpos), far_z(zpos), 3 - zpos)
     groups = {
-        "y": SimpleNamespace(bit=row, other=xpos, peers=(across, slant, mate), partner=beside),
-        "x": SimpleNamespace(bit=xpos, other=row, peers=(beside, aslant, mate), partner=across),
+        "y": SimpleNamespace(bit=row, other=xpos, peers=(across, slant, mate), partner=beside, second=near, blocks=by_z),
+        "x": SimpleNamespace(bit=xpos, other=row, peers=(beside, aslant, mate), partner=across, second=near, blocks=by_z),
+        "z": SimpleNamespace(bit=low_z, other=xpos, peers=(near, near_slant, mate), partner=beside, second=across,
+                             blocks=(2 * row + high_z, 2 * flip(row) + high_z, 2 * row + flip(high_z),
+                                     2 * flip(row) + flip(high_z))),
+        "w": SimpleNamespace(bit=low_z, other=row, peers=(near, near_slant, mate), partner=across, second=beside,
+                             blocks=(2 * xpos + high_z, 2 * flip(xpos) + high_z, 2 * xpos + flip(high_z),
+                                     2 * flip(xpos) + flip(high_z))),
     }
     for group in groups.values():
         group.mine = 2 * group.bit + core
         group.parts = (2 * flip(group.bit) + core, 2 * flip(group.bit) + flip(core), 2 * group.bit + flip(core))
     here = flat_block(zpos, column)
-    peers = [mate, beside, across, slant, aslant] + along
+    peers = [mate, beside, across, slant, aslant, near_slant, corner, far_corner] + along
     barrier = pltpu.get_barrier_semaphore()
     for peer in peers:
         pl.semaphore_signal(barrier, inc=1, device_id=peer, device_id_type=MESH)
@@ -508,18 +520,27 @@
     project(0, s.vw_query, KV_ROWS)
     project(1, s.vw_key, 0)
     for group in range(GROUPS):
-        s.sent[group, 2 * WIDE : KV_ROWS, :] = marks
+        s.sent[group, WIDE:VALUES_AT, :] = marks
         s.sent[group, KV_ROWS + WIDE :, :] = marks
     pl.semaphore_wait(barrier, len(peers))
-    kv_part, q_part = pl.ds(0, KV_ROWS), pl.ds(KV_ROWS, Q_ROWS)
-    x_copies, c_copies, on_copies = [None] * 4, [None] * 4, [None] * 4
+    q_part = pl.ds(KV_ROWS, Q_ROWS)
+    part_rows = {"k": pl.ds(0, VALUES_AT), "v": pl.ds(VALUES_AT, WIDE)}
+    z_copies, x_copies, c_copies, on_copies = {}, {}, {}, {}
     q_copies = [go(remote(s.sent.at[(zpos + step) % 4, q_part], s.queries.at[zpos], s.q_send.at[step],
                           s.q_recv.at[step], along[step - 1])) for step in range(1, 4)]
-    project(2, s.vw_value, WIDE)
-    z_copies = [go(remote(s.sent.at[(zpos + step) % 4, kv_part], s.kv.at[here], s.z_send.at[step], s.z_recv.at[step],
-                          along[step - 1])) for step in range(1, 4)]
-    x_copies[0] = go(remote(s.sent.at[zpos, kv_part], s.kv.at[here], s.x_send.at[0], s.x_recv.at[0], beside))
-    c_copies[0] = go(remote(s.sent.at[zpos, kv_part], s.kv.at[here], s.c_send.at[0], s.c_recv.at[0], mate))
+
+    def send_part(part):
+        rows, at = part_rows[part], "kv".index(part)
+        for step in range(1, 4):
+            z_copies[part, step] = go(remote(s.sent.at[(zpos + step) % 4, rows], s.kv.at[here, rows], s.z_send.at[at, step],
+                                             s.z_recv.at[at, step], along[step - 1]))
+        own = s.sent.at[zpos, rows]
+        x_copies[part, 0] = go(remote(own, s.kv.at[here, rows], s.x_send.at[at, 0], s.x_recv.at[at, 0], beside))
+        c_copies[part, 0] = go(remote(own, s.kv.at[here, rows], s.c_send.at[at, 0], s.c_recv.at[at, 0], mate))
+
+    send_part("k")
+    project(2, s.vw_value, VALUES_AT)
+    send_part("v")
     for index in range(3, 7):
         loads[index].start()
     s.kv[here] = s.sent[zpos, :KV_ROWS, :]
@@ -538,16 +559,22 @@
         for slot, at in ((0, 511), (4, 1)):
             s.tiles[head, slot] = jnp.broadcast_to(line[:, at : at + 1], (TOK, TOK))
 
-    def pass_on(step):
-        spot = s.kv.at[flat_block((zpos + 4 - step) % 4, beside_column)]
-        x_copies[step].wait_recv()
-        on_copies[step] = go(remote(spot, spot, s.c_send.at[4 + step], s.c_recv.at[4 + step], mate))
-
-    def relay(step):
-        z_copies[step - 1].wait_recv()
-        spot = s.kv.at[flat_block((zpos + 4 - step) % 4, column)]
-        x_copies[step] = go(remote(spot, spot, s.x_send.at[step], s.x_recv.at[step], beside))
-        c_copies[step] = go(remote(spot, spot, s.c_send.at[step], s.c_recv.at[step], mate))
+    def pass_on(part, step):
+        at = "kv".index(part)
+        spot = s.kv.at[flat_block((zpos + 4 - step) % 4, beside_column), part_rows[part]]
+        x_copies[part, step].wait_recv()
+        on_copies[part, step] = go(remote(spot, spot, s.c_send.at[at, 4 + step], s.c_recv.at[at, 4 + step], mate))
+
+    def relay(part, step):
+        at = "kv".index(part)
+        z_copies[part, step].wait_recv()
+        spot = s.kv.at[flat_block((zpos + 4 - step) % 4, column), part_rows[part]]
+        x_copies[part, step] = go(remote(spot, spot, s.x_send.at[at, step], s.x_recv.at[at, step], beside))
+        c_copies[part, step] = go(remote(spot, spot, s.c_send.at[at, step], s.c_recv.at[at, step], mate))
+
+    def arrive(part, step):
+        c_copies[part, step].wait_recv()
+        on_copies[part, step].wait_recv()
 
     seg_column = jnp.broadcast_to(seg_row.astype(F32), (TOK, TOK)).T
     valid = seg_column[:, 0:1] >= 0
@@ -559,7 +586,8 @@
     def share_right(index, buffer, value, axis="y"):
         group = groups[axis]
         spot = buffer.at[span(group.mine, TOK)]
-        buffer[span(group.mine, TOK), :] = value
+        if value is not None:
+            buffer[span(group.mine, TOK), :] = value
         right_copies[index] = (
             go(remote(spot, spot, s.right_send.at[index, 0], s.right_recv.at[index, 0], group.peers[0])),
             go(remote(spot, spot, s.right_send.at[index, 1], s.right_recv.at[index, 1], mate)),
@@ -588,10 +616,15 @@
             copy.wait_recv()
 
     def stage_quarters(staged, turned, height, axis="y"):
-        weights = (16, 2) if axis == "y" else (2, 16)
         for part in range(4):
             for half in range(2):
-                firsts = [height * (weights[0] * (part // 2) + 4 * z_at + weights[1] * half + part % 2) for z_at in range(4)]
+                firsts = []
+                for at in range(4):
+                    bit, core_at = part // 2, part % 2
+                    row_at, z_at, x_at = {"y": (bit, at, half), "x": (half, at, bit),
+                                          "z": (at // 2, 2 * (at % 2) + bit, half),
+                                          "w": (half, 2 * (at % 2) + bit, at // 2)}[axis]
+                    firsts.append(height * (16 * row_at + 4 * z_at + 2 * x_at + core_at))
                 staged[part, 4 * height * half : 4 * height * (half + 1), :] = jnp.concatenate(
                     [turned[first : first + height] for first in firsts], axis=0).astype(LOW)
 
@@ -608,7 +641,7 @@
             spot = s.normed_all.at[rows, span(zpos, TOK)]
             n_copies.append(go(remote(spot, spot, s.n_send.at[piece, step], s.n_recv.at[piece, step], along[step - 1])))
 
-    pass_on(0)
+    pass_on("k", 0)
     for copy in q_copies:
         copy.wait_recv()
 
@@ -622,89 +655,125 @@
     s.totals[...] = jnp.zeros_like(s.totals)
     s.summed[...] = jnp.zeros_like(s.summed)
 
-    def block_scores(head, key_spot):
-        keys = jnp.concatenate([s.kv[key_spot, head_rows(head), :], s.kv[key_spot, 2 * WIDE :, :]], axis=0)
-        bias = [s.tiles[head, bias_slot(key_spot, block, column)] for block in range(4)]
-        return dot(keys, s.marked[head], 0, 0) + jnp.concatenate(bias, axis=1)
+    def chunk_scores(head, chunk):
+        keys = jnp.concatenate([wide_rows(head_rows(head), chunk), wide_rows(slice(WIDE, VALUES_AT), chunk)], axis=0)
+        return dot(keys, s.marked[head], 0, 0)
+
+    def with_bias(scores, head, chunk, spot):
+        bias = [s.tiles[head, bias_slot(flat_block(chunk, spot), block, column)] for block in range(4)]
+        return scores[TOK * spot : TOK * spot + TOK] + jnp.concatenate(bias, axis=1)
 
     def wide_rows(rows, chunk):
         return jnp.concatenate([s.kv[flat_block(chunk, spot), rows, :] for spot in range(4)], axis=1)
 
     o_copies = []
 
-    def attend(step):
-        chunk = (zpos + 4 - step) % 4
-        c_copies[step].wait_recv()
-        on_copies[step].wait_recv()
-
-        def one_head(head, carry):
-            newest = s.highest[head]
-            for spot in range(4):
-                scores = block_scores(head, flat_block(chunk, spot))
-                s.score_buf[spot] = scores
-                newest = jnp.maximum(newest, jnp.max(scores, axis=0, keepdims=True))
-            rescale = jnp.exp(s.highest[head] - newest)
-            total = s.totals[head] * rescale
-            for spot in range(4):
-                weights = jnp.exp(s.score_buf[spot] - newest)
-                total = total + jnp.sum(weights, axis=0, keepdims=True)
-                s.weight_buf[TOK * spot : TOK * spot + TOK, :] = weights.astype(LOW)
-            values = wide_rows(head_rows(head, WIDE), chunk)
-            summed = s.summed[head] * rescale + dot(values, s.weight_buf[...])
-            if step < 3:
-                s.highest[head] = newest
-                s.totals[head] = total
-                s.summed[head] = summed
-                return carry
-            summed = summed / total
+    def chunk_at(step):
+        return (zpos + 4 - step) % 4
+
+    def score(step, head):
+        product = chunk_scores(head, chunk_at(step))
+        old = newest = s.highest[head]
+        for spot in range(4):
+            scores = with_bias(product, head, chunk_at(step), spot)
+            s.score_buf[head, spot] = scores
+            newest = jnp.maximum(newest, jnp.max(scores, axis=0, keepdims=True))
+        s.highest[head] = newest
+        s.chunk_highest[step, head] = newest
+        return old, newest
+
+    def weigh(step, head, old, newest):
+        total = s.totals[head] * jnp.exp(old - newest)
+        for spot in range(4):
+            weights = jnp.exp(s.score_buf[head, spot] - newest)
+            total = total + jnp.sum(weights, axis=0, keepdims=True)
+            s.probs[chunk_at(step), head, TOK * spot : TOK * spot + TOK, :] = weights.astype(LOW)
+        s.totals[head] = total
+
+    def weigh_chunk(step):
+        arrive("k", step)
+        scored = [score(step, 0)]
+        for head in range(HEADS_HERE):
+            if head + 1 < HEADS_HERE:
+                scored.append(score(step, head + 1))
+            weigh(step, head, *scored[head])
+
+    def gather(step, head):
+        values = wide_rows(head_rows(head, VALUES_AT), chunk_at(step))
+        rescale = jnp.exp(s.chunk_highest[step, head] - s.highest[head])
+        summed = s.summed[head] + rescale * dot(values, s.probs[chunk_at(step), head])
+        if step < 3:
             s.summed[head] = summed
-            s.lse[head] = newest + jnp.log(total)
-            low = summed.astype(LOW)
-            rows = slice(DH * head, DH * head + DH)
-            for block in range(4):
-                s.context_out[block, rows, :] = low[:, TOK * block : TOK * block + TOK]
-            for hop in range(1, 4):
-                o_copies.append(go(remote(s.context_out.at[(zpos + hop) % 4, rows], s.context.at[zpos, rows],
-                                          s.o_send.at[head, hop], s.o_recv.at[head, hop], along[hop - 1])))
-            return carry
-
-        if step < 3:
-            lax.fori_loop(0, HEADS_HERE, one_head, 0)
-        else:
-            for head in range(HEADS_HERE):
-                one_head(head, 0)
-
-    attend(0)
-    relay(1)
-    relay(2)
-    pass_on(1)
-    relay(3)
+            return
+        summed = summed / s.totals[head]
+        s.summed[head] = summed
+        s.lse[head] = s.highest[head] + jnp.log(s.totals[head])
+        low = summed.astype(LOW)
+        rows = slice(DH * head, DH * head + DH)
+        for block in range(4):
+            s.context_out[block, rows, :] = low[:, TOK * block : TOK * block + TOK]
+        for hop in range(1, 4):
+            o_copies.append(go(remote(s.context_out.at[(zpos + hop) % 4, rows], s.context.at[zpos, rows],
+                                      s.o_send.at[head, hop], s.o_recv.at[head, hop], along[hop - 1])))
+
+    def gather_chunk(step):
+        arrive("v", step)
+        for head in range(HEADS_HERE):
+            gather(step, head)
+
+    weigh_chunk(0)
+    relay("k", 1)
+    relay("k", 2)
+    pass_on("k", 1)
+    relay("k", 3)
+    pass_on("v", 0)
+    weigh_chunk(1)
+    relay("v", 1)
+    pass_on("k", 2)
+    pass_on("k", 3)
+    relay("v", 2)
+    relay("v", 3)
     share_normed(0)
-    share_normed(1)
-    pass_on(2)
-    attend(1)
+    weigh_chunk(2)
+    pass_on("v", 1)
+    weigh_chunk(3)
+    pass_on("v", 2)
+    gather_chunk(0)
+    gather_chunk(1)
+    pass_on("v", 3)
+    gather_chunk(2)
     pass_right(0, s.right_down, DOWN_AXIS)
-    pass_on(3)
-    attend(2)
-    attend(3)
+    gather_chunk(3)
     s.context[zpos] = s.context_out[zpos]
     loads[6].wait()
     for cut in range(CUT):
         s.grad_hidden[cut] = dot(grad_branch, s.vw_down[CUT_COLS * cut : CUT_COLS * cut + CUT_COLS, :], 1, 1)
+    for chunk in range(4):
+        for head in range(HEADS_HERE):
+            product = chunk_scores(head, chunk)
+            for spot in range(4):
+                probs = jnp.exp(with_bias(product, head, chunk, spot) - s.lse[head])
+                s.probs[chunk, head, TOK * spot : TOK * spot + TOK, :] = probs.astype(LOW)
     for index in range(3, 6):
         loads[index].wait()
     for copy in o_copies:
         copy.wait_recv()
 
+    def pack_small(first, line):
+        for at in range(D // TOK):
+            s.small_out[0, first + at : first + at + 1, :] = line[:, TOK * at : TOK * at + TOK]
+
     context_t = jnp.concatenate([s.context[group] for group in range(GROUPS)], axis=0)
     middle = row_in + dot(context_t, s.vw_out[...], 0, 0)
     scale_second = rms(middle)
     normed_ffn = (middle * scale_second * gain_second).astype(LOW)
-    share_normed(2)
+    share_normed(1)
     turned = normed_ffn.astype(F32).T
-    for index, axis in ((1, "y"), (3, "x")):
-        stage_quarters(s.left_gate.at[index // 2], turned, OWN, axis)
-        share_left(index, s.left_gate.at[index // 2], s.all_left_gate.at[index // 2], axis)
+    for axis in sorted(set(AXES)):
+        at = "yxzw".index(axis)
+        stage_quarters(s.left_gate.at[at], turned, OWN, axis)
+        if axis in "xy":
+            share_left(LEFTS[axis], s.left_gate.at[at], s.all_left_gate.at[at], axis)
     grad_normed = jnp.zeros((TOK, D), F32)
     for cut in range(CUT):
         cols = slice(CUT_COLS * cut, CUT_COLS * cut + CUT_COLS)
@@ -714,7 +783,11 @@
         s.hidden_act[:, cols] = (gelu * upward).astype(LOW)
         grad_gate = (grad_hidden * upward * slope).astype(LOW)
         grad_upward = (grad_hidden * gelu).astype(LOW)
-        share_right(1 + cut, s.right_gate.at[cut], jnp.concatenate([grad_gate, grad_upward], axis=1), AXES[cut])
+        both = jnp.concatenate([grad_gate, grad_upward], axis=1)
+        if AXES[cut] in "zw":
+            s.right_gate[cut, span(low_z * 2 + core, TOK), :] = both
+        else:
+            share_right(1 + cut, s.right_gate.at[cut], both, AXES[cut])
         grad_normed = grad_normed + dot(grad_gate, s.vw_gate[:, cols], 1, 1) + dot(grad_upward, s.vw_up[:, cols], 1, 1)
     grad_mid_part, grad_gain_ffn = rms_back(middle, scale_second, gain_second, grad_normed)
     grad_middle = grad_result + grad_mid_part
@@ -727,8 +800,15 @@
                 for head in range(HEADS_HERE)]
     s.cotangents[zpos] = s.d_out[zpos]
     s.grad_middle[...] = grad_middle
-    s.small_out[0] = jnp.zeros((8, D), F32)
-    s.small_out[0, 1:2, :] = grad_gain_ffn
+    s.small_out[0] = jnp.zeros((SMALL_ROWS, TOK), F32)
+    pack_small(6, grad_gain_ffn)
+    for axis in "zw":
+        if axis in AXES:
+            at = "yxzw".index(axis)
+            share_left(LEFTS[axis], s.left_gate.at[at], s.all_left_gate.at[at], axis)
+    for cut in range(CUT):
+        if AXES[cut] in "zw":
+            share_right(1 + cut, s.right_gate.at[cut], None, AXES[cut])
     share_right(5, s.right_out, grad_attn, OUT_AXIS)
     stage_quarters(s.left_down, s.hidden_act[...].T, OWN_DOWN, DOWN_AXIS)
     share_left(0, s.left_down, s.all_left_down, DOWN_AXIS)
@@ -750,37 +830,35 @@
     def differentiate(step):
         chunk = chunk_of(step)
 
-        def one_head(head, carry):
+        def local(head):
             if step == 0:
                 for copy in d_copies[head]:
                     copy.wait_recv()
                 s.deltas[head] = jnp.sum(wide_cotangent(head).astype(F32) * s.summed[head], axis=0, keepdims=True)
-            cotangent = wide_cotangent(head)
+            grad_product = dot(wide_rows(head_rows(head, VALUES_AT), chunk), wide_cotangent(head), 0, 0)
             for spot in range(4):
-                key_spot = flat_block(chunk, spot)
-                probs = jnp.exp(block_scores(head, key_spot) - s.lse[head])
-                grad_probs = dot(s.kv[key_spot, head_rows(head, WIDE), :], cotangent, 0, 0)
-                grad_scores = probs * (grad_probs - s.deltas[head])
+                rows = slice(TOK * spot, TOK * spot + TOK)
+                grad_scores = s.probs[chunk, head, rows, :].astype(F32) * (grad_product[rows] - s.deltas[head])
                 for block in range(4):
-                    slot = bias_slot(key_spot, block, column)
+                    slot = bias_slot(flat_block(chunk, spot), block, column)
                     s.tile_grads[head, slot] = s.tile_grads[head, slot] + grad_scores[:, TOK * block : TOK * block + TOK]
-                s.weight_buf[TOK * spot : TOK * spot + TOK, :] = probs.astype(LOW)
-                s.grad_buf[TOK * spot : TOK * spot + TOK, :] = grad_scores.astype(LOW)
-            keys = wide_rows(head_rows(head), chunk)
-            s.query_sum[head] = s.query_sum[head] + dot(keys, s.grad_buf[...])
-            grad_keys = dot(s.marked[head, :DH, :], s.grad_buf[...], 1, 1)
-            grad_values = dot(cotangent, s.weight_buf[...], 1, 1)
+                s.grad_buf[head, rows, :] = grad_scores.astype(LOW)
+
+        def products_of(head):
+            s.query_sum[head] = s.query_sum[head] + dot(wide_rows(head_rows(head), chunk), s.grad_buf[head])
+            grad_keys = dot(s.marked[head, :DH, :], s.grad_buf[head], 1, 1)
+            grad_values = dot(wide_cotangent(head), s.probs[chunk, head], 1, 1)
             for spot in range(4):
                 lanes = slice(TOK * spot, TOK * spot + TOK)
                 s.key_sum[step, spot, head_rows(head), :] = grad_keys[:, lanes]
                 s.key_sum[step, spot, head_rows(head, WIDE), :] = grad_values[:, lanes]
-            return carry
-
-        if step > 0:
-            lax.fori_loop(0, HEADS_HERE, one_head, 0)
-        else:
-            for head in range(HEADS_HERE):
-                one_head(head, 0)
+
+        local(0)
+        local(1)
+        products_of(0)
+        local(2)
+        products_of(1)
+        products_of(2)
         for x_half in range(2):
             s.core_out[step, x_half] = s.key_sum[step, 2 * x_half + flip(core)].astype(LOW)
         core_copies[step] = go(remote(s.core_out.at[step], s.core_in.at[step], s.cg_send.at[step], s.cg_recv.at[step], mate))
@@ -815,10 +893,8 @@
         s.grads[zpos, 2 * WIDE :, :] = s.query_out[zpos]
 
     pieces = {
-        "query": (0, 2 * WIDE, WIDE, s.pq_core, s.pq_core_out, s.pq_core_in, s.pq_x_out, s.pq_x_in, s.pq_y_out, s.pq_y_in,
-                  s.pq_z_out, s.pq_z_in),
-        "pair": (1, 0, 2 * WIDE, s.pp_core, s.pp_core_out, s.pp_core_in, s.pp_x_out, s.pp_x_in, s.pp_y_out, s.pp_y_in,
-                 s.pp_z_out, s.pp_z_in),
+        "query": (0, 2 * WIDE, WIDE, s.pq_core, s.pq_core_out, s.pq_core_in, s.pq_chip_out, s.pq_chip_in, s.pq_z_out, s.pq_z_in),
+        "pair": (1, 0, 2 * WIDE, s.pp_core, s.pp_core_out, s.pp_core_in, s.pp_chip_out, s.pp_chip_in, s.pp_z_out, s.pp_z_in),
     }
 
     def piece_core(name):
@@ -828,34 +904,32 @@
         started[name, "core"] = go(remote(out, into, s.p_send.at[index, 0], s.p_recv.at[index, 0], mate))
         total[...] = dot(s.normed_all[span(core, D // 2), :], right, 1, 1)
 
-    def piece_x(name):
+    def piece_chips(name):
         index, _, _, total, _, core_in, out, into = pieces[name][:8]
         started[name, "core"].wait_recv()
         total[...] = total[...] + core_in[...].astype(F32)
-        out[...] = total[span(flip(xpos), D // 4), :].astype(LOW)
-        started[name, "x"] = go(remote(out, into, s.p_send.at[index, 1], s.p_recv.at[index, 1], beside))
-
-    def piece_y(name):
-        index, _, _, total, _, _, _, x_in, out, into = pieces[name][:10]
-        started[name, "x"].wait_recv()
-        half = span(xpos, D // 4)
-        total[half, :] = total[half, :] + x_in[...].astype(F32)
-        out[...] = total[span(2 * xpos + flip(row), D // 8), :].astype(LOW)
-        started[name, "y"] = go(remote(out, into, s.p_send.at[index, 2], s.p_recv.at[index, 2], across))
+        places = ((beside, flip(xpos), row), (across, xpos, flip(row)), (corner, flip(xpos), flip(row)))
+        started[name, "chips"] = []
+        for slot, (peer, x_at, row_at) in enumerate(places):
+            out[slot] = total[span(2 * x_at + row_at, D // 8), :].astype(LOW)
+            started[name, "chips"].append(go(remote(out.at[slot], into.at[slot], s.p_send.at[index, 1 + slot],
+                                                    s.p_recv.at[index, 1 + slot], peer)))
 
     def piece_z(name):
-        index, _, width, total, _, _, _, _, _, y_in, out, into = pieces[name]
-        started[name, "y"].wait_recv()
-        eighth = total[span(2 * xpos + row, D // 8), :] + y_in[...].astype(F32)
+        index, _, width, total, _, _, _, chip_in, out, into = pieces[name]
+        eighth = total[span(2 * xpos + row, D // 8), :]
+        for slot, copy in enumerate(started[name, "chips"]):
+            copy.wait_recv()
+            eighth = eighth + chip_in[slot].astype(F32)
         pad = jnp.zeros((8, width), F32)
         for z_at in range(4):
             out[z_at] = jnp.concatenate([eighth[OWN * z_at : OWN * z_at + OWN], pad], axis=0).astype(LOW)
-        started[name, "z"] = [go(remote(out.at[(zpos + step) % 4], into.at[zpos], s.p_send.at[index, 2 + step],
-                                        s.p_recv.at[index, 2 + step], along[step - 1])) for step in range(1, 4)]
+        started[name, "z"] = [go(remote(out.at[(zpos + step) % 4], into.at[zpos], s.p_send.at[index, 4 + step],
+                                        s.p_recv.at[index, 4 + step], along[step - 1])) for step in range(1, 4)]
         into[zpos] = out[zpos]
 
     def piece_last(name):
-        into = pieces[name][11]
+        into = pieces[name][9]
         for copy in started[name, "z"]:
             copy.wait_recv()
         if name == "query":
@@ -875,7 +949,7 @@
         row_again = s.hidden[...].astype(F32)
         grad_in_part, grad_gain_attn = rms_back(row_again, rms(row_again), gain_first, grad_normed_attn)
         s.grad_input[...] = (s.grad_middle[...] + grad_in_part).astype(LOW)
-        s.small_out[0, 0:1, :] = grad_gain_attn
+        pack_small(0, grad_gain_attn)
 
     def finish_table():
         blank = jnp.zeros((8, TOK), F32)
@@ -897,10 +971,12 @@
             left = jnp.sum(s.tile_grads[head, 0], keepdims=True)
             right = jnp.sum(s.tile_grads[head, 4], keepdims=True)
             line = line + jnp.where(lane == 15, left, 0.0) + jnp.where(lane == 31, right, 0.0)
-            s.small_out[0, 2 + head : 3 + head, span(zpos, TOK)] = line
-
-    small_rounds = ((mate, across, slant), (beside,), tuple(along))
-    small_first = (0, 3, 4)
+            for group in range(GROUPS):
+                at = 12 + HEADS_HERE * group + head
+                s.small_out[0, at : at + 1, :] = jnp.where(zpos == group, line, 0.0)
+
+    small_rounds = ((mate, across, slant, beside, aslant, corner, far_corner), tuple(along))
+    small_first = (0, 7)
 
     def small_go(step):
         first = small_first[step]
@@ -913,7 +989,7 @@
         for slot, copy in enumerate(started["small", step]):
             copy.wait_recv()
             summed = summed + s.small_in[small_first[step] + slot]
-        if step < 2:
+        if step < 1:
             s.small_out[step + 1] = summed
             small_go(step + 1)
         else:
@@ -939,7 +1015,7 @@
             product = dot(s.all_left_out[span(x_half, 4 * OWN), :], s.right_out[...])
             pair = (product[:, : D // 2], product[:, D // 2 :])
         else:
-            left = s.all_left_gate.at["yx".index(AXES[unit])]
+            left = s.all_left_gate.at["yxzw".index(AXES[unit])]
             product = dot(left[span(x_half, 4 * OWN), :], s.right_gate[unit])
             pair = (product[:, :CUT_COLS], product[:, CUT_COLS:])
         return [jnp.concatenate([part[OWN * at : OWN * at + OWN] for part in pair], axis=0) for at in range(4)]
@@ -948,7 +1024,7 @@
         number = numbers[kind, unit]
         total, xs, xr = buffers[kind][:3]
         group = groups[axes[kind, unit]]
-        left = {"down": 0, "out": 2, "gate": 1 + 2 * (axes[kind, unit] == "x")}[kind]
+        left = {"down": 0, "out": 2, "gate": LEFTS[axes[kind, unit]]}[kind]
         if left not in taken:
             taken.add(left)
             take_left(left)
@@ -967,22 +1043,24 @@
         started["x", number].wait_recv()
         for block in range(4):
             total[unit, block] = total[unit, block] + xr[unit, block].astype(F32)
-        ns[unit, 0] = total[unit, near_z(zpos)].astype(LOW)
-        ns[unit, 1] = total[unit, 3 - zpos].astype(LOW)
-        started["near", number] = go(remote(ns.at[unit], nr.at[unit], s.un_send.at[number], s.un_recv.at[number], near))
+        group = groups[axes[kind, unit]]
+        ns[unit, 0] = total[unit, group.blocks[1]].astype(LOW)
+        ns[unit, 1] = total[unit, group.blocks[3]].astype(LOW)
+        started["near", number] = go(remote(ns.at[unit], nr.at[unit], s.un_send.at[number], s.un_recv.at[number],
+                                            group.second))
 
     def unit_far(kind, unit):
         number = numbers[kind, unit]
         total, _, _, _, nr, fs, fr = buffers[kind]
         started["near", number].wait_recv()
-        fs[unit] = (total[unit, far_z(zpos)] + nr[unit, 1].astype(F32)).astype(LOW)
+        fs[unit] = (total[unit, groups[axes[kind, unit]].blocks[2]] + nr[unit, 1].astype(F32)).astype(LOW)
         started["far", number] = go(remote(fs.at[unit], fr.at[unit], s.uf_send.at[number], s.uf_recv.at[number], far))
 
     def unit_last(kind, unit):
         number = numbers[kind, unit]
         total, _, _, _, nr, _, fr = buffers[kind]
         started["far", number].wait_recv()
-        final = total[unit, zpos] + nr[unit, 0].astype(F32) + fr[unit].astype(F32)
+        final = total[unit, groups[axes[kind, unit]].blocks[0]] + nr[unit, 0].astype(F32) + fr[unit].astype(F32)
         if kind == "down":
             s.g_down[:, D // 2 * unit : D // 2 * unit + D // 2] = final
         elif kind == "gate":
@@ -1005,69 +1083,67 @@
 
     plan = (
         (differentiate, 0),
+        (share_normed, 2),
         (share_normed, 3),
+        (differentiate, 1),
+        (pass_gate, 3),
+        (differentiate, 2),
+        (reduce_cores, 0),
+        (pass_gate, 1),
+        (differentiate, 3),
+        (reduce_cores, 1),
+        (finish_queries,),
+        (pass_gate, 2),
+        (pass_out,),
+        (unit_x, "gate", 3),
+        (finish_table,),
+        (reduce_cores, 2),
+        (reduce_x, 0),
         (pass_gate, 0),
-        (differentiate, 1),
+        (unit_x, "out", 0),
+        (unit_x, "down", 0),
+        (reduce_x, 1),
+        (unit_near, "gate", 3),
+        (reduce_x, 2),
+        (unit_x, "gate", 2),
+        (wait_normed,),
+        (unit_x, "down", 1),
+        (unit_near, "down", 0),
+        (reduce_cores, 3),
+        (unit_near, "out", 0),
+        (unit_x, "gate", 1),
+        (piece_core, "query"),
+        (unit_far, "gate", 3),
         (unit_x, "gate", 0),
-        (differentiate, 2),
-        (wait_normed,),
-        (reduce_cores, 1),
-        (differentiate, 3),
-        (pass_gate, 2),
-        (finish_queries,),
-        (pass_out,),
-        (reduce_cores, 0),
-        (unit_x, "down", 0),
-        (pass_gate, 3),
-        (unit_x, "down", 1),
-        (reduce_cores, 2),
-        (reduce_x, 1),
-        (reduce_cores, 3),
-        (piece_core, "query"),
-        (unit_near, "gate", 0),
-        (reduce_x, 0),
-        (pass_gate, 1),
-        (unit_x, "gate", 2),
-        (reduce_x, 2),
-        (piece_x, "query"),
-        (unit_x, "gate", 3),
+        (unit_near, "gate", 2),
         (reduce_x, 3),
-        (finish_table,),
+        (unit_far, "down", 0),
         (unit_near, "down", 1),
         (piece_core, "pair"),
-        (unit_x, "gate", 1),
+        (piece_chips, "query"),
+        (unit_far, "out", 0),
+        (finish_input,),
+        (unit_near, "gate", 1),
+        (piece_chips, "pair"),
+        (unit_far, "gate", 2),
+        (unit_near, "gate", 0),
+        (piece_z, "query"),
+        (unit_far, "down", 1),
+        (piece_z, "pair"),
+        (small_go, 0),
+        (unit_last, "gate", 3),
+        (unit_far, "gate", 1),
         (unit_far, "gate", 0),
-        (unit_near, "down", 0),
-        (unit_near, "gate", 2),
-        (unit_x, "out", 0),
-        (unit_near, "gate", 3),
-        (unit_far, "down", 1),
-        (finish_input,),
-        (piece_x, "pair"),
+        (small_next, 0),
+        (unit_last, "out", 0),
+        (piece_last, "pair"),
+        (unit_last, "gate", 1),
+        (unit_last, "down", 1),
+        (unit_last, "gate", 2),
+        (piece_last, "query"),
         (unit_last, "gate", 0),
-        (unit_far, "down", 0),
-        (unit_far, "gate", 2),
-        (piece_y, "query"),
-        (small_go, 0),
-        (unit_far, "gate", 3),
-        (unit_near, "out", 0),
-        (piece_y, "pair"),
-        (piece_z, "query"),
-        (small_next, 0),
-        (unit_near, "gate", 1),
+        (unit_last, "down", 0),
         (small_next, 1),
-        (piece_z, "pair"),
-        (unit_last, "down", 1),
-        (unit_far, "out", 0),
-        (unit_last, "gate", 2),
-        (unit_far, "gate", 1),
-        (piece_last, "query"),
-        (piece_last, "pair"),
-        (unit_last, "out", 0),
-        (small_next, 2),
-        (unit_last, "down", 0),
-        (unit_last, "gate", 3),
-        (unit_last, "gate", 1),
     )
     for act, *values in plan:
         act(*values)
@@ -1101,9 +1177,10 @@
     wide("profile", H, 1, QUERIES)
     wide("tiles", HEADS_HERE, 5, TOK, TOK)
     low("marked", HEADS_HERE, DH + MARKS, QUERIES)
-    wide("score_buf", 4, TOK, QUERIES)
-    low("weight_buf", QUERIES, QUERIES)
-    low("grad_buf", QUERIES, QUERIES)
+    wide("score_buf", HEADS_HERE, 4, TOK, QUERIES)
+    wide("chunk_highest", 4, HEADS_HERE, 1, QUERIES)
+    low("grad_buf", HEADS_HERE, QUERIES, QUERIES)
+    low("probs", 4, HEADS_HERE, QUERIES, QUERIES)
     for name in ("highest", "totals", "lse", "deltas"):
         wide(name, HEADS_HERE, 1, QUERIES)
     wide("summed", HEADS_HERE, DH, QUERIES)
@@ -1127,21 +1204,21 @@
     low("column_grads", 3 * WIDE, QUERIES)
     for name, width in (("pq", WIDE), ("pp", 2 * WIDE)):
         wide(name + "_core", D // 2, width)
-        for stage, rows in (("core", D // 2), ("x", D // 4), ("y", D // 8)):
-            low(f"{name}_{stage}_out", rows, width)
-            low(f"{name}_{stage}_in", rows, width)
+        for side in ("out", "in"):
+            low(f"{name}_core_{side}", D // 2, width)
+            low(f"{name}_chip_{side}", 3, D // 8, width)
         low(name + "_z_out", 4, OWN + 8, width)
         low(name + "_z_in", 4, OWN + 8, width)
-    wide("small_out", 3, 8, D)
-    wide("small_in", 7, 8, D)
+    wide("small_out", 2, SMALL_ROWS, TOK)
+    wide("small_in", 10, SMALL_ROWS, TOK)
     low("right_down", QUERIES, D)
     low("right_gate", CUT, QUERIES, 2 * CUT_COLS)
     low("right_out", QUERIES, D)
     for name, rows in (("down", FF // 4), ("out", D // 4)):
         low("left_" + name, 4, rows, TOK)
         low("all_left_" + name, rows, QUERIES)
-    low("left_gate", 2, 4, D // 4, TOK)
-    low("all_left_gate", 2, D // 4, QUERIES)
+    low("left_gate", 4, 4, D // 4, TOK)
+    low("all_left_gate", 4, D // 4, QUERIES)
     for name, units, rows, width in (("down", 2, OWN_DOWN, D // 2), ("gate", CUT, 2 * OWN, CUT_COLS), ("out", 1, 2 * OWN, D // 2)):
         wide(name + "_total", units, 4, rows, width)
         for stage, blocks in (("x", 4), ("n", 2)):
@@ -1149,10 +1226,10 @@
             low(f"{name}_{stage}r", units, blocks, rows, width)
         low(name + "_fs", units, rows, width)
         low(name + "_fr", units, rows, width)
-    sem("z", 4)
+    sem("z", 2, 4)
     sem("q", 4)
-    sem("x", 4)
-    sem("c", 8)
+    sem("x", 2, 4)
+    sem("c", 2, 8)
     sem("n", 4, 4)
     sem("o", HEADS_HERE, 4)
     sem("d", HEADS_HERE, 4)
@@ -1160,10 +1237,10 @@
     sem("xg", 4)
     sem("b", 4)
     sem("qb", 4)
-    sem("p", 2, 6)
-    sem("s", 7)
+    sem("p", 2, 8)
+    sem("s", 10)
     sem("right", 6, 3)
-    sem("left", 4, 3)
+    sem("left", 6, 3)
     sem("ux", 7)
     sem("un", 7)
     sem("uf", 7)
@@ -1176,10 +1253,9 @@
         target[...] = source[...]
     small = refs[count - 1]
     table, gain_attn, gain_ffn = refs[2 * count - 1 :]
-    lines = [small[2 + head : 3 + head, TOK * group : TOK * group + NB] for group in range(GROUPS) for head in range(HEADS_HERE)]
-    table[...] = jnp.concatenate(lines, axis=0)
-    gain_attn[...] = small[0:1, :].reshape(D)
-    gain_ffn[...] = small[1:2, :].reshape(D)
+    table[...] = small[12:24, :NB]
+    gain_attn[...] = jnp.concatenate([small[at : at + 1, :] for at in range(6)], axis=1).reshape(D)
+    gain_ffn[...] = jnp.concatenate([small[at : at + 1, :] for at in range(6, 12)], axis=1).reshape(D)
 
 
 def fast_device(
@@ -1193,7 +1269,7 @@
     outs = {
         "output": ((TOK, D), LOW), "grad_input": ((TOK, D), LOW), "g_query": ((OWN, D), F32), "g_key": ((OWN, D), F32),
         "g_value": ((OWN, D), F32), "g_out": ((OWN, D), F32), "g_gate": ((OWN, FF), F32), "g_up": ((OWN, FF), F32),
-        "g_down": ((OWN_DOWN, D), F32), "small_sum": ((8, D), F32),
+        "g_down": ((OWN_DOWN, D), F32), "small_sum": ((SMALL_ROWS, TOK), F32),
     }
     scratch = layer_scratch()
     names = tuple(ins) + tuple(outs) + tuple(scratch)

time: 107 us -> 102 us (0.953)
  Pallas kernels: 106 us -> 101 us
    pallas_call x1, Pallas kernels: 104 us -> 98.5 us  [fast_device(): pl.pallas_call(functools.partial(layer_kernel, names), out_shape=shapes,...]
where the time goes in v5:
time: 102 us
  Pallas kernels  101 us (99%)
    pallas_call x1, Pallas kernels, fast_device(): pl.pallas_call(functools.partial(layer_kernel, names), out_shape=shapes,...  98.5 us
    pallas_call x1, Pallas kernels, fast_device(): pl.pallas_call(hand_over_kernel, out_shape=shapes[:-1] + ends, name='hand...  2.43 us

profile of v5, /device:TPU:0, one launch (start us, length us, event | category | flops | bytes accessed | tf_op | source)
XLA Modules:
  0.0 101.7 jit_solution(6140430458886852926)
XLA Ops:
  0.6 98.5 %encoder_layer.1 = (bf16[128,768]{1,0:T(8,128)(2,1)}, bf16[128,768]{1,0:T(8,128)(2,1)}, f32[24,768]{1,0:T(8,128)}, f32[24,768]{1,0:T(8,128)}, f32[24,768]{1,0:T(...) custom-call(bf16[128,768]{1,0:T(8,128)(2,1)} %bitcast.6, ...), custom_call_target="tpu_custom_call" | custom-call | tf_op jit(solution)/shard_map/encoder_layer/pallas_call | solution.py:1278
  99.1 2.4 %hand_over.1 = (bf16[128,768]{1,0:T(8,128)(2,1)}, bf16[128,768]{1,0:T(8,128)(2,1)}, f32[24,768]{1,0:T(8,128)}, f32[24,768]{1,0:T(8,128)}, f32[24,768]{1,0:T(8,12...) custom-call(bf16[128,768]{1,0:T(8,128)(2,1)} %get-tuple-element.34.r, ...), custom_call_target="tpu_custom_call" | custom-call | tf_op jit(solution)/shard_map/hand_over/pallas_call | solution.py:1288

commit v6 on v5

--- a/solution.py
+++ b/solution.py
@@ -384,6 +384,10 @@
 LOW = jnp.bfloat16
 
 
+SUMS = (("g_query", 0, D), ("g_key", D, D), ("g_value", 2 * D, D), ("g_out", 3 * D, D), ("g_gate", 4 * D, FF),
+        ("g_up", 4 * D + FF, FF))
+
+
 def place():
     row = lax.axis_index("rows")
     spot = lax.axis_index("seq")
@@ -453,6 +457,9 @@
 
 def layer_kernel(names, *refs):
     s = SimpleNamespace(**dict(zip(names, refs)))
+    s.output, s.grad_input = s.rows_out.at[0], s.rows_out.at[1]
+    for name, first, width in SUMS:
+        setattr(s, name, s.sums_out.at[:, first : first + width])
     row, zpos, xpos, core = place()
     column = 2 * xpos + core
     beside_column = 2 * flip(xpos) + core
@@ -526,21 +533,33 @@
     q_part = pl.ds(KV_ROWS, Q_ROWS)
     part_rows = {"k": pl.ds(0, VALUES_AT), "v": pl.ds(VALUES_AT, WIDE)}
     z_copies, x_copies, c_copies, on_copies = {}, {}, {}, {}
-    q_copies = [go(remote(s.sent.at[(zpos + step) % 4, q_part], s.queries.at[zpos], s.q_send.at[step],
-                          s.q_recv.at[step], along[step - 1])) for step in range(1, 4)]
+    q_copies = [remote(s.sent.at[(zpos + step) % 4, q_part], s.queries.at[zpos], s.q_send.at[step],
+                       s.q_recv.at[step], along[step - 1]) for step in range(1, 4)]
+    for copy in q_copies:
+        copy.start()
+
+    def start_part(part, which):
+        @pl.when(core == which)
+        def _():
+            for step in range(1, 4):
+                z_copies[part, step].start()
 
     def send_part(part):
         rows, at = part_rows[part], "kv".index(part)
         for step in range(1, 4):
-            z_copies[part, step] = go(remote(s.sent.at[(zpos + step) % 4, rows], s.kv.at[here, rows], s.z_send.at[at, step],
-                                             s.z_recv.at[at, step], along[step - 1]))
+            z_copies[part, step] = remote(s.sent.at[(zpos + step) % 4, rows], s.kv.at[here, rows], s.z_send.at[at, step],
+                                          s.z_recv.at[at, step], along[step - 1])
+            sends.append(z_copies[part, step])
         own = s.sent.at[zpos, rows]
         x_copies[part, 0] = go(remote(own, s.kv.at[here, rows], s.x_send.at[at, 0], s.x_recv.at[at, 0], beside))
         c_copies[part, 0] = go(remote(own, s.kv.at[here, rows], s.c_send.at[at, 0], s.c_recv.at[at, 0], mate))
 
     send_part("k")
+    start_part("k", 0)
     project(2, s.vw_value, VALUES_AT)
     send_part("v")
+
+    start_part("v", 0)
     for index in range(3, 7):
         loads[index].start()
     s.kv[here] = s.sent[zpos, :KV_ROWS, :]
@@ -604,10 +623,9 @@
 
     def share_left(index, staged, buffer, axis="y"):
         group = groups[axis]
-        lanes = span(group.mine, TOK)
-        buffer[:, lanes] = staged[group.mine]
+        buffer[group.mine] = staged[group.mine]
         left_copies[index] = [
-            go(remote(staged.at[part], buffer.at[:, lanes], s.left_send.at[index, slot], s.left_recv.at[index, slot], peer))
+            go(remote(staged.at[part], buffer.at[group.mine], s.left_send.at[index, slot], s.left_recv.at[index, slot], peer))
             for slot, (peer, part) in enumerate(zip(group.peers, group.parts))
         ]
 
@@ -629,21 +647,29 @@
                     [turned[first : first + height] for first in firsts], axis=0).astype(LOW)
 
     share_right(0, s.right_down, grad_branch, DOWN_AXIS)
+
+    @pl.when(core == 1)
+    def _():
+        for copy in q_copies:
+            copy.wait_send()
+
+    start_part("k", 1)
     turned = normed.astype(F32).T
     order = [16 * r + 4 * z + 2 * x + c for c in range(2) for x in range(2) for r in range(2) for z in range(4)]
-    s.normed_all[:, span(zpos, TOK)] = jnp.concatenate(
+    s.normed_all[zpos] = jnp.concatenate(
         [turned[OWN * at : OWN * at + OWN] for at in order], axis=0).astype(LOW)
     n_copies = []
 
     def share_normed(piece):
         rows = pl.ds(D // 4 * piece, D // 4)
         for step in range(1, 4):
-            spot = s.normed_all.at[rows, span(zpos, TOK)]
+            spot = s.normed_all.at[zpos, rows]
             n_copies.append(go(remote(spot, spot, s.n_send.at[piece, step], s.n_recv.at[piece, step], along[step - 1])))
 
     pass_on("k", 0)
     for copy in q_copies:
         copy.wait_recv()
+    start_part("v", 1)
 
     for block in range(4):
         lanes = slice(TOK * block, TOK * block + TOK)
@@ -897,12 +923,15 @@
         "pair": (1, 0, 2 * WIDE, s.pp_core, s.pp_core_out, s.pp_core_in, s.pp_chip_out, s.pp_chip_in, s.pp_z_out, s.pp_z_in),
     }
 
+    def members(buffer, rows):
+        return jnp.concatenate([buffer[at, rows, :] for at in range(4)], axis=1)
+
     def piece_core(name):
         index, first, width, total, out, into = pieces[name][:6]
         right = s.column_grads[first : first + width, :]
-        out[...] = dot(s.normed_all[span(flip(core), D // 2), :], right, 1, 1).astype(LOW)
+        out[...] = dot(members(s.normed_all, span(flip(core), D // 2)), right, 1, 1).astype(LOW)
         started[name, "core"] = go(remote(out, into, s.p_send.at[index, 0], s.p_recv.at[index, 0], mate))
-        total[...] = dot(s.normed_all[span(core, D // 2), :], right, 1, 1)
+        total[...] = dot(members(s.normed_all, span(core, D // 2)), right, 1, 1)
 
     def piece_chips(name):
         index, _, _, total, _, core_in, out, into = pieces[name][:8]
@@ -1009,14 +1038,14 @@
     def products(kind, unit, x_half):
         if kind == "down":
             cols = slice(D // 2 * unit, D // 2 * unit + D // 2)
-            product = dot(s.all_left_down[span(x_half, 4 * OWN_DOWN), :], s.right_down[:, cols])
+            product = dot(members(s.all_left_down, span(x_half, 4 * OWN_DOWN)), s.right_down[:, cols])
             return [product[OWN_DOWN * at : OWN_DOWN * at + OWN_DOWN] for at in range(4)]
         if kind == "out":
-            product = dot(s.all_left_out[span(x_half, 4 * OWN), :], s.right_out[...])
+            product = dot(members(s.all_left_out, span(x_half, 4 * OWN)), s.right_out[...])
             pair = (product[:, : D // 2], product[:, D // 2 :])
         else:
             left = s.all_left_gate.at["yxzw".index(AXES[unit])]
-            product = dot(left[span(x_half, 4 * OWN), :], s.right_gate[unit])
+            product = dot(members(left, span(x_half, 4 * OWN)), s.right_gate[unit])
             pair = (product[:, :CUT_COLS], product[:, CUT_COLS:])
         return [jnp.concatenate([part[OWN * at : OWN * at + OWN] for part in pair], axis=0) for at in range(4)]
 
@@ -1095,13 +1124,14 @@
         (finish_queries,),
         (pass_gate, 2),
         (pass_out,),
+        (reduce_cores, 2),
         (unit_x, "gate", 3),
-        (finish_table,),
-        (reduce_cores, 2),
         (reduce_x, 0),
         (pass_gate, 0),
+        (reduce_cores, 3),
         (unit_x, "out", 0),
         (unit_x, "down", 0),
+        (finish_table,),
         (reduce_x, 1),
         (unit_near, "gate", 3),
         (reduce_x, 2),
@@ -1109,44 +1139,48 @@
         (wait_normed,),
         (unit_x, "down", 1),
         (unit_near, "down", 0),
-        (reduce_cores, 3),
         (unit_near, "out", 0),
         (unit_x, "gate", 1),
         (piece_core, "query"),
         (unit_far, "gate", 3),
+        (reduce_x, 3),
+        (piece_core, "pair"),
         (unit_x, "gate", 0),
         (unit_near, "gate", 2),
-        (reduce_x, 3),
         (unit_far, "down", 0),
         (unit_near, "down", 1),
-        (piece_core, "pair"),
         (piece_chips, "query"),
         (unit_far, "out", 0),
         (finish_input,),
+        (small_go, 0),
+        (piece_chips, "pair"),
         (unit_near, "gate", 1),
-        (piece_chips, "pair"),
         (unit_far, "gate", 2),
         (unit_near, "gate", 0),
         (piece_z, "query"),
         (unit_far, "down", 1),
+        (small_next, 0),
         (piece_z, "pair"),
-        (small_go, 0),
         (unit_last, "gate", 3),
         (unit_far, "gate", 1),
+        (unit_last, "out", 0),
         (unit_far, "gate", 0),
-        (small_next, 0),
-        (unit_last, "out", 0),
+        (piece_last, "query"),
+        (small_next, 1),
+        (unit_last, "gate", 2),
+        (unit_last, "down", 1),
+        (unit_last, "down", 0),
         (piece_last, "pair"),
         (unit_last, "gate", 1),
-        (unit_last, "down", 1),
-        (unit_last, "gate", 2),
-        (piece_last, "query"),
         (unit_last, "gate", 0),
-        (unit_last, "down", 0),
-        (small_next, 1),
     )
     for act, *values in plan:
         act(*values)
+    @pl.when(core == 0)
+    def _():
+        for copy in q_copies:
+            copy.wait_send()
+
     for copy in sends:
         copy.wait_send()
 
@@ -1173,7 +1207,7 @@
     low("sent", GROUPS, SENT_ROWS, TOK)
     low("kv", 16, KV_ROWS, TOK)
     low("queries", 4, Q_ROWS, TOK)
-    low("normed_all", D, QUERIES)
+    low("normed_all", 4, D, TOK)
     wide("profile", H, 1, QUERIES)
     wide("tiles", HEADS_HERE, 5, TOK, TOK)
     low("marked", HEADS_HERE, DH + MARKS, QUERIES)
@@ -1216,9 +1250,9 @@
     low("right_out", QUERIES, D)
     for name, rows in (("down", FF // 4), ("out", D // 4)):
         low("left_" + name, 4, rows, TOK)
-        low("all_left_" + name, rows, QUERIES)
+        low("all_left_" + name, 4, rows, TOK)
     low("left_gate", 4, 4, D // 4, TOK)
-    low("all_left_gate", 4, D // 4, QUERIES)
+    low("all_left_gate", 4, 4, D // 4, TOK)
     for name, units, rows, width in (("down", 2, OWN_DOWN, D // 2), ("gate", CUT, 2 * OWN, CUT_COLS), ("out", 1, 2 * OWN, D // 2)):
         wide(name + "_total", units, 4, rows, width)
         for stage, blocks in (("x", 4), ("n", 2)):
@@ -1247,12 +1281,13 @@
     return scratch
 
 
-def hand_over_kernel(*refs):
-    count = len(refs) // 2 - 1
-    for source, target in zip(refs[: count - 1], refs[count : 2 * count - 1]):
-        target[...] = source[...]
-    small = refs[count - 1]
-    table, gain_attn, gain_ffn = refs[2 * count - 1 :]
+def hand_over_kernel(rows, sums, down, small, *outs):
+    outs[0][...] = rows[0]
+    outs[1][...] = rows[1]
+    for out, (_, first, width) in zip(outs[2:8], SUMS):
+        out[...] = sums[:, first : first + width]
+    outs[8][...] = down[...]
+    table, gain_attn, gain_ffn = outs[9:]
     table[...] = small[12:24, :NB]
     gain_attn[...] = jnp.concatenate([small[at : at + 1, :] for at in range(6)], axis=1).reshape(D)
     gain_ffn[...] = jnp.concatenate([small[at : at + 1, :] for at in range(6, 12)], axis=1).reshape(D)
@@ -1267,9 +1302,8 @@
         "w_out": w_out, "w_gate": w_gate, "w_up": w_up, "w_down": w_down,
     }
     outs = {
-        "output": ((TOK, D), LOW), "grad_input": ((TOK, D), LOW), "g_query": ((OWN, D), F32), "g_key": ((OWN, D), F32),
-        "g_value": ((OWN, D), F32), "g_out": ((OWN, D), F32), "g_gate": ((OWN, FF), F32), "g_up": ((OWN, FF), F32),
-        "g_down": ((OWN_DOWN, D), F32), "small_sum": ((SMALL_ROWS, TOK), F32),
+        "rows_out": ((2, TOK, D), LOW), "sums_out": ((OWN, 4 * D + 2 * FF), F32), "g_down": ((OWN_DOWN, D), F32),
+        "small_sum": ((SMALL_ROWS, TOK), F32),
     }
     scratch = layer_scratch()
     names = tuple(ins) + tuple(outs) + tuple(scratch)
@@ -1284,8 +1318,10 @@
         compiler_params=pltpu.CompilerParams(collective_id=0, has_side_effects=True, vmem_limit_bytes=60 * 2**20),
         name="encoder_layer",
     )(*ins.values())
-    ends = [jax.ShapeDtypeStruct(shape, F32) for shape in ((H, NB), (D,), (D,))]
-    found = pl.pallas_call(hand_over_kernel, out_shape=shapes[:-1] + ends, name="hand_over")(*found)
+    ends = [jax.ShapeDtypeStruct((TOK, D), LOW)] * 2
+    ends += [jax.ShapeDtypeStruct((OWN, width), F32) for _, _, width in SUMS] + [shapes[2]]
+    ends += [jax.ShapeDtypeStruct(shape, F32) for shape in ((H, NB), (D,), (D,))]
+    found = pl.pallas_call(hand_over_kernel, out_shape=ends, name="hand_over")(*found)
     return (found[0][None], found[1][None], *found[2:9], found[9].T, *found[10:])
 
 

time: 102 us -> 101 us (level)
  no operation moved by 1% of the time
where the time goes in v6:
time: 101 us
  Pallas kernels  101 us (100%)
    pallas_call x1, Pallas kernels, fast_device(): pl.pallas_call(functools.partial(layer_kernel, names), out_shape=shapes,...  98.2 us
    pallas_call x1, Pallas kernels, fast_device(): pl.pallas_call(hand_over_kernel, out_shape=ends, name='hand_over')(*found)  2.31 us

profile of v6, /device:TPU:0, one launch (start us, length us, event | category | flops | bytes accessed | tf_op | source)
XLA Modules:
  0.0 101.3 jit_solution(11145915829870125859)
XLA Ops:
  0.6 98.2 %encoder_layer.1 = (bf16[2,128,768]{2,1,0:T(8,128)(2,1)}, f32[24,7168]{1,0:T(8,128)}, f32[64,768]{1,0:T(8,128)}, f32[24,128]{1,0:T(8,128)}) custom-call(bf16[128,768]{1,0:T(8,128)(2,1)} %bitcast.6, s32[1,128]{1,0:T(1,128)} %refs_1_.1, bf16[128,768]{1,0:T(8,128)(2,1)} %bitcast.7, bf16[12,32]{1,0:T(8,128)(2,1)} %bitcast.8, bf16[768]{0:T(1024)(128)(2,1)} %refs_4_.1, ...), custom_call_target="tpu_custom_call" | custom-call | tf_op jit(solution)/shard_map/encoder_layer/pallas_call | solution.py:1312
  98.9 2.3 %hand_over.1 = (bf16[128,768]{1,0:T(8,128)(2,1)}, bf16[128,768]{1,0:T(8,128)(2,1)}, f32[24,768]{1,0:T(8,128)}, f32[24,768]{1,0:T(8,128)}, f32[24,768]{1,0:T(8,12...) custom-call(bf16[2,128,768]{2,1,0:T(8,128)(2,1)} %get-tuple-element., ...), custom_call_target="tpu_custom_call" | custom-call | tf_op jit(solution)/shard_map/hand_over/pallas_call | solution.py:1324
